TPU v7x, 32 devices: a whole 2x2x4 slice. The times are simulated.
32 devices in a mesh: dp: 8 (over y, x, core), tp: 4 (over z).
Axes of the slice: x: 2, y: 2, z: 4, core: 2. Of those that a mesh axis runs over, the one named last changes fastest.
Arguments:
- tokens: bfloat16 [8192, 1536], P('dp'), may hold values from -6 to 6
- lengths: int32 [8], P('dp'), may hold values from 1 to 1024, as said below
- positions: int32 [8192], P('dp'), may hold values from 0 to 2046, as said below
- cotangent: bfloat16 [8192, 1536], P('dp'), may hold values from -6 to 6
- norm_gain: float32 [1536], replicated, may hold values from 0.5 to 1.5
- w_query: bfloat16 [1536, 1536], P(None, 'tp'), may hold values from -0.15625 to 0.15625
- w_key: bfloat16 [1536, 768], P(None, 'tp'), may hold values from -0.15625 to 0.15625
- w_value: bfloat16 [1536, 768], P(None, 'tp'), may hold values from -0.15625 to 0.15625
- w_out: bfloat16 [1536, 1536], P('tp'), may hold values from -0.625 to 0.625
- mlp_gain: float32 [1536], replicated, may hold values from 0.5 to 1.5
- w_gate: bfloat16 [1536, 4096], P(None, 'tp'), may hold values from -0.15625 to 0.15625
- w_up: bfloat16 [1536, 4096], P(None, 'tp'), may hold values from -0.15625 to 0.15625
- w_down: bfloat16 [4096, 1536], P('tp'), may hold values from -0.09375 to 0.09375
Outputs:
- layer_out: bfloat16 [8192, 1536], P(('dp', 'tp'))
- input_grad: bfloat16 [8192, 1536], P('dp')
- norm_gain_grad: float32 [1536], P('dp')
- w_query_grad: float32 [1536, 1536], P('dp', 'tp')
- w_key_grad: float32 [1536, 768], P('dp', 'tp')
- w_value_grad: float32 [1536, 768], P('dp', 'tp')
- w_out_grad: float32 [1536, 1536], P('tp', 'dp')
- mlp_gain_grad: float32 [1536], P('dp')
- w_gate_grad: float32 [1536, 4096], P('dp', 'tp')
- w_up_grad: float32 [1536, 4096], P('dp', 'tp')
- w_down_grad: float32 [4096, 1536], P('tp', 'dp')
Inputs may be any that keep to these rules, and one draw needn't show every extreme that they name: `lengths`: each sequence's length; at least one sequence has exactly 1024. Within each sequence positions start at 0 and rise by 1 or 2 from one token to the next; in one sequence every step is 2.
All inputs are finite; a program needn't handle non-finite values.
Results may differ from a plain program's by a relative error of at most 0.015.
Values sent between devices are 32-bit elements; how exact they have to be, the bound alone decides.
No kernel may reach another device: no remote copies, remote signals or barrier semaphores. Data moves between devices by JAX's collectives and lax.ppermute only.
A program may use at most 192 MiB of HBM per device.

v0:
```python
import functools

import jax
import jax.numpy as jnp
from jax import lax
from jax.experimental import pallas as pl
from jax.experimental.pallas import tpu as pltpu
from jax.sharding import Mesh
from jax.sharding import PartitionSpec as P

HD = 96
LANES = 128
GROUP = 2
KV_WIDE = (GROUP + 2) * LANES
rope_base = 100000.0
norm_eps = 1e-05
masked_score = -1e30
far_away = 1e30
score_scale = HD ** (-0.5)
score_scale_log2 = score_scale * 1.4426950408889634
CHUNKS = 4
EXTRA = 8
VMEM_BYTES = 56 * 1024 * 1024
NT = (((1,), (1,)), ((), ()))


def params():
    return pltpu.CompilerParams(vmem_limit_bytes=VMEM_BYTES)


def cost(flops, moved, exps=0):
    return pl.CostEstimate(
        flops=flops // 1024, bytes_accessed=moved // 1024, transcendentals=exps // 1024
    )


def dot32(a, b):
    return jnp.dot(a, b, preferred_element_type=jnp.float32)


def dot32_nt(a, b):
    return lax.dot_general(a, b, NT, preferred_element_type=jnp.float32)


def dot_split(a, places):
    high = a.astype(jnp.bfloat16)
    rest = (a - high.astype(jnp.float32)).astype(jnp.bfloat16)
    return dot32(high, places) + dot32(rest, places)


def fence(*trees):
    return lax.optimization_barrier(trees)


def whole(array, buffers=None):
    zeros = (0,) * len(array.shape)
    return pl.BlockSpec(array.shape, lambda *_: zeros)


SCALAR = pl.BlockSpec(memory_space=pltpu.SMEM)
ANYWHERE = pl.BlockSpec(memory_space=pl.ANY)


def halves(entry):
    half_dim = HD // 2
    return (entry // half_dim) * (LANES // 2) + entry % half_dim


def placement(lanes, width):
    return (lanes[:, None] == jnp.arange(width)[None, :]).astype(jnp.bfloat16)


def place_query(heads):
    source = jnp.arange(heads * HD)
    return placement((source // HD) * LANES + halves(source % HD), heads * LANES)


def place_key_value(kv_heads):
    source = jnp.arange(kv_heads * HD)
    head = source // HD
    keys = head * 2 * LANES + halves(source % HD)
    values = head * 2 * LANES + LANES + source % HD
    return placement(jnp.concatenate([keys, values]), kv_heads * 2 * LANES)


def place_all(heads, kv_heads):
    source = jnp.arange(heads * HD)
    head = source // HD
    query = (head // GROUP) * KV_WIDE + (head % GROUP) * LANES + halves(source % HD)
    source = jnp.arange(kv_heads * HD)
    base = (source // HD) * KV_WIDE + GROUP * LANES
    keys = base + halves(source % HD)
    values = base + LANES + source % HD
    return placement(jnp.concatenate([query, keys, values]), kv_heads * KV_WIDE)


def place_plain(heads):
    source = jnp.arange(heads * HD)
    return placement((source // HD) * LANES + source % HD, heads * LANES)


PAIRS = [(0, 1), (1, 0), (2, 3), (3, 2)]
INWARD = [(0, 1), (3, 2)]
MIDDLE = [(1, 2), (2, 1)]
OUTWARD = [(1, 0), (2, 3)]


def along(part, pairs):
    return lax.ppermute(part, "tp", pairs)


def store_qkv(out_ref, here, base, query, key_value):
    wide = GROUP * LANES
    for kv in range(key_value.shape[1] // (2 * LANES)):
        at = base + kv * KV_WIDE
        there = slice(kv * 2 * LANES, (kv + 1) * 2 * LANES)
        out_ref[here, at : at + wide] = query[:, kv * wide : (kv + 1) * wide]
        out_ref[here, at + wide : at + KV_WIDE] = key_value[:, there]


def store_turned(out_ref, at, lin, cos_ref, sin_ref):
    for h in range(GROUP + 2):
        one = lin[:, h * LANES : (h + 1) * LANES]
        if h < GROUP + 1:
            one = one * cos_ref[...] + pltpu.roll(one, LANES // 2, 1) * sin_ref[...]
        out_ref[:, at + h * LANES : at + (h + 1) * LANES] = one.astype(jnp.bfloat16)


def spread_out_kernel(meta_ref, own_ref, p_ref, mine_ref, theirs_ref, pad_ref, plain_ref):
    rows, width = mine_ref.shape[2:]
    wide = p_ref.shape[1]
    for side, ref in enumerate((mine_ref, theirs_ref)):
        here = pl.ds(pl.multiple_of((meta_ref[1] ^ side) * rows, rows), rows)
        for s in range(4):
            block = own_ref[here, :] if s == 0 else ref[0, s - 1].astype(jnp.bfloat16)
            plain_ref[here, s * width : (s + 1) * width] = block
            pad_ref[here, s * wide : (s + 1) * wide] = dot32(block, p_ref[...]).astype(
                jnp.bfloat16
            )


def spread_qkv_kernel(pq_ref, pkv_ref, far_ref, _, out_ref):
    parts, _, rows, width = far_ref.shape
    split = pq_ref.shape[0]
    block = far_ref[:, 0].reshape(parts * rows, width).astype(jnp.bfloat16)
    query = dot32(block[:, :split], pq_ref[...]).astype(jnp.bfloat16)
    key_value = dot32(block[:, split:], pkv_ref[...]).astype(jnp.bfloat16)
    store_qkv(out_ref, slice(None), 0, query, key_value)


def spread_qkv(padded, pq, pkv, far):
    total = padded.shape[0]
    dp, others, rows, width = far.shape
    wide = padded.shape[1] // (others + 1)
    parts = max(1, dp // 2)
    block = parts * rows
    return pl.pallas_call(
        spread_qkv_kernel,
        out_shape=jax.ShapeDtypeStruct(padded.shape, jnp.bfloat16),
        grid=(total // block, others),
        in_specs=[
            whole(pq),
            whole(pkv),
            pl.BlockSpec((parts, 1, rows, width), lambda i, s: (i, s, 0, 0)),
            pl.BlockSpec(memory_space=pl.ANY),
        ],
        out_specs=pl.BlockSpec((block, wide), lambda i, s: (i, s + 1)),
        input_output_aliases={3: 0},
        compiler_params=params(),
        cost_estimate=cost(8 * total * width * 512, 20 * total * wide),
    )(pq, pkv, far, padded)


def spread(kernel, meta, own, places, mine, theirs, widths):
    chips, others, rows, width = mine.shape
    total = own.shape[0]
    row_block = lambda m, meta: (meta[0] ^ m, 0)
    piece = pl.BlockSpec((1, others, rows, width), lambda m, meta: (m, 0, 0, 0))
    return pl.pallas_call(
        kernel,
        out_shape=[jax.ShapeDtypeStruct((total, wide), jnp.bfloat16) for wide in widths],
        grid_spec=pltpu.PrefetchScalarGridSpec(
            num_scalar_prefetch=1,
            grid=(chips,),
            in_specs=[pl.BlockSpec((2 * rows, own.shape[1]), row_block)]
            + [whole(place) for place in places]
            + [piece, piece],
            out_specs=[pl.BlockSpec((2 * rows, wide), row_block) for wide in widths],
        ),
        compiler_params=params(),
        cost_estimate=cost(
            8 * total * width * 512, total * (12 * width + 2 * sum(widths))
        ),
    )(meta, own, *places, mine, theirs)


def start_kernel(x_ref, gain_ref, q_ref, k_ref, v_ref, pq_ref, pkv_ref, cos_ref, sin_ref, *outs):
    qkv_ref, normed_ref, pad_ref = outs

    @pl.when(pl.program_id(0) == 0)
    def _():
        split = k_ref.shape[0]
        query = dot32(q_ref[...], pq_ref[...]).astype(jnp.bfloat16)
        key_value = dot32(k_ref[...].T, pkv_ref[:split, :])
        key_value = key_value + dot32(v_ref[...].T, pkv_ref[split:, :])
        store_qkv(pad_ref, slice(None), 0, query, key_value.astype(jnp.bfloat16))

    inputs = x_ref[...].astype(jnp.float32)
    rms = lax.rsqrt(jnp.mean(inputs * inputs, -1, keepdims=True) + norm_eps)
    normed = (inputs * rms * gain_ref[...]).astype(jnp.bfloat16)
    normed_ref[...] = normed
    for kv in range(pad_ref.shape[1] // KV_WIDE):
        at = kv * KV_WIDE
        store_turned(qkv_ref, at, dot32(normed, pad_ref[:, at : at + KV_WIDE]), cos_ref, sin_ref)


def start(tokens, gain, w_query, w_key_t, w_value_t, pq, pkv, cosines, sines):
    total, depth = tokens.shape
    rows = total // CHUNKS
    wide = pq.shape[1] + pkv.shape[1]
    gain = gain[None, :]
    by_rows = lambda width: pl.BlockSpec((rows, width), lambda i: (i, 0))
    arrays = [w_query, w_key_t, w_value_t, pq, pkv]
    shapes = [
        jax.ShapeDtypeStruct((total, 4 * wide), jnp.bfloat16),
        jax.ShapeDtypeStruct((total, depth), jnp.bfloat16),
        jax.ShapeDtypeStruct((depth, 4 * wide), jnp.bfloat16),
    ]
    return pl.pallas_call(
        start_kernel,
        out_shape=shapes,
        grid=(CHUNKS,),
        in_specs=[by_rows(depth), whole(gain)]
        + [whole(array) for array in arrays]
        + [by_rows(LANES), by_rows(LANES)],
        out_specs=[
            by_rows(wide),
            by_rows(depth),
            pl.BlockSpec((depth, wide), lambda i: (0, 0)),
        ],
        compiler_params=params(),
        cost_estimate=cost(2 * total * depth * wide, 12 * total * depth),
    )(tokens, gain, *arrays, cosines, sines)


def turn_kernel(length_ref, cot_ref, normed_ref, dout_ref, dout_t_ref, normed_t_ref):
    rows = cot_ref.shape[0]
    at = pl.program_id(0) * rows + lax.broadcasted_iota(jnp.int32, cot_ref.shape, 0)
    dout = jnp.where(at < length_ref[0], cot_ref[...].astype(jnp.float32), 0.0)
    dout = dout.astype(jnp.bfloat16)
    dout_ref[...] = dout
    dout_t_ref[...] = dout.T
    normed_t_ref[...] = normed_ref[...].T


def turn(length, cotangent, normed):
    total, depth = cotangent.shape
    rows = total // CHUNKS
    by_rows = pl.BlockSpec((rows, depth), lambda i: (i, 0))
    by_columns = pl.BlockSpec((depth, rows), lambda i: (0, i))
    turned = jax.ShapeDtypeStruct((depth, total), jnp.bfloat16)
    return pl.pallas_call(
        turn_kernel,
        out_shape=[jax.ShapeDtypeStruct((total, depth), jnp.bfloat16), turned, turned],
        grid=(CHUNKS,),
        in_specs=[SCALAR, by_rows, by_rows],
        out_specs=[by_rows, by_columns, by_columns],
        compiler_params=params(),
        cost_estimate=cost(total * depth, 10 * total * depth),
    )(length, cotangent, normed)


def project_kernel(x_ref, w_ref, cos_ref, sin_ref, _, out_ref):
    store_turned(out_ref, 0, dot32(x_ref[...], w_ref[...]), cos_ref, sin_ref)


def project(normed, weights, cosines, sines, qkv):
    rows, depth = normed.shape
    width = weights.shape[1]
    steps = width // KV_WIDE
    first = steps // 4
    return pl.pallas_call(
        project_kernel,
        out_shape=jax.ShapeDtypeStruct((rows, width), jnp.bfloat16),
        grid=(steps - first,),
        in_specs=[
            whole(normed),
            pl.BlockSpec((depth, KV_WIDE), lambda i: (0, i + first)),
            whole(cosines),
            whole(sines),
            pl.BlockSpec(memory_space=pl.ANY),
        ],
        out_specs=pl.BlockSpec((rows, KV_WIDE), lambda i: (0, i + first)),
        input_output_aliases={4: 0},
        compiler_params=params(),
        cost_estimate=cost(
            2 * rows * depth * width, 2 * (rows * depth + depth * width + rows * width)
        ),
    )(normed, weights, cosines, sines, qkv)


def attend_kernel(start, length_ref, q_ref, kv_ref, strip_ref, out_ref):
    rows = q_ref.shape[0]
    keys = kv_ref.shape[0]
    length = length_ref[0]
    row_ids = start + lax.broadcasted_iota(jnp.int32, (1, rows), 1)
    limit = jnp.minimum(row_ids, length - 1)
    allowed = lax.broadcasted_iota(jnp.int32, (keys, rows), 0) <= limit
    mixed = []
    sums = []
    for kv in range(kv_ref.shape[1] // KV_WIDE):
        base = kv * KV_WIDE
        at = base + GROUP * LANES
        key = kv_ref[:, at : at + LANES]
        value_t = kv_ref[:, at + LANES : at + 2 * LANES].T
        for g in range(GROUP):
            query = q_ref[:, base + g * LANES : base + (g + 1) * LANES]
            raw = jnp.where(allowed, dot32_nt(key, query), masked_score)
            peak = jnp.max(raw, axis=0, keepdims=True)
            expo = jnp.exp2((raw - peak) * score_scale_log2)
            total = jnp.sum(expo, axis=0, keepdims=True)
            probs = (expo * (1.0 / total)).astype(jnp.bfloat16)
            mixed.append(dot32(value_t, probs).T)
            log_sum = peak * score_scale_log2 + jnp.log2(total)
            sums.append(jnp.where(row_ids < length, log_sum, far_away))
    out_ref[:rows, :] = dot_split(jnp.concatenate(mixed, 1), strip_ref[...])
    out_ref[rows:, :] = jnp.zeros((EXTRA, out_ref.shape[1]), jnp.float32)
    out_ref[rows : rows + len(sums), :rows] = jnp.concatenate(sums, 0)


def attend(length, qkv, strip, index, rows):
    keys = (index + 1) * rows
    width = qkv.shape[1] // 4
    heads = width // KV_WIDE * GROUP
    shape = (rows + EXTRA, strip.shape[1])
    return pl.pallas_call(
        functools.partial(attend_kernel, index * rows),
        out_shape=jax.ShapeDtypeStruct(shape, jnp.float32),
        grid=(1,),
        in_specs=[
            SCALAR,
            pl.BlockSpec((rows, width), lambda i: (index, 0)),
            pl.BlockSpec((keys, width), lambda i: (0, 0)),
            whole(strip),
        ],
        out_specs=pl.BlockSpec(shape, lambda i: (0, 0)),
        compiler_params=params(),
        cost_estimate=cost(
            4 * heads * rows * keys * LANES, 2 * (rows + keys) * width, heads * rows * keys
        ),
    )(length, qkv, qkv, strip)


def forward_kernel(level_ref, part_ref, other_ref, across_ref, outer_ref, *refs):
    x_ref, dout_ref, wo_ref, gain_ref, gate_any, up_any, down_any = refs[:7]
    hidden_ref, normed_t_ref, activ_ref, dgate_ref, dup_ref, mlp_ref, dn_ref = refs[7:14]
    normed_ref, gate_ref, up_ref, down_ref, sems = refs[14:]
    rows = x_ref.shape[0]
    steps, block = down_ref.shape[:2]
    step = pl.program_id(0)

    def fetched(at):
        here = pl.ds(pl.multiple_of(at * block, block), block)
        return [
            pltpu.make_async_copy(gate_any.at[:, here], gate_ref.at[at], sems.at[0, at]),
            pltpu.make_async_copy(up_any.at[:, here], up_ref.at[at], sems.at[1, at]),
            pltpu.make_async_copy(down_any.at[here, :], down_ref.at[at], sems.at[2, at]),
        ]

    @pl.when(step == 0)
    def _():
        for at in range(steps):
            for copy in fetched(at):
                copy.start()
        level = level_ref[0]
        inner = (level == 1) | (level == 2)
        width = part_ref.shape[1]
        second = jnp.where(inner, across_ref[:rows, width:], outer_ref[:rows, :width])
        third = jnp.where(inner, across_ref[:rows, :width], outer_ref[:rows, width:])
        mixed = jnp.concatenate([part_ref[:rows, :], other_ref[:rows, :], second, third], 1)
        hidden = x_ref[...].astype(jnp.float32) + dot32_nt(mixed.astype(jnp.bfloat16), wo_ref[...])
        hidden_ref[...] = hidden
        rms = lax.rsqrt(jnp.mean(hidden * hidden, -1, keepdims=True) + norm_eps)
        normed = (hidden * rms * gain_ref[...]).astype(jnp.bfloat16)
        normed_ref[...] = normed
        normed_t_ref[...] = normed.T
        mlp_ref[...] = jnp.zeros_like(mlp_ref)
        dn_ref[...] = jnp.zeros_like(dn_ref)

    for copy in fetched(step):
        copy.wait()
    wg_ref, wu_ref, wd_ref = gate_ref.at[step], up_ref.at[step], down_ref.at[step]
    normed = normed_ref[...]
    gate = dot32(normed, wg_ref[...])
    up = dot32(normed, wu_ref[...])
    dact = dot32_nt(dout_ref[...], wd_ref[...])
    sigmoid = jax.nn.sigmoid(gate)
    silu = gate * sigmoid
    activ = (silu * up).astype(jnp.bfloat16)
    dgate = (dact * up * sigmoid * (1.0 + gate * (1.0 - sigmoid))).astype(jnp.bfloat16)
    dup = (dact * silu).astype(jnp.bfloat16)
    activ_ref[...] = activ
    dgate_ref[...] = dgate
    dup_ref[...] = dup
    mlp_ref[...] += dot32(activ, wd_ref[...])
    dn_ref[:rows, :] += dot32_nt(dgate, wg_ref[...]) + dot32_nt(dup, wu_ref[...])


def forward_chunk(level, gathered, tokens, dout, w_out, gain, w_gate, w_up, w_down, index, rows):
    depth = tokens.shape[1]
    units = w_gate.shape[1]
    block = 512
    own_rows = pl.BlockSpec((rows, depth), lambda i: (index, 0))
    steps = units // block
    gain = gain[None, :]
    f32, bf16 = jnp.float32, jnp.bfloat16
    outs = [
        jax.ShapeDtypeStruct((rows, depth), f32),
        jax.ShapeDtypeStruct((depth, rows), bf16),
        jax.ShapeDtypeStruct((rows, units), bf16),
        jax.ShapeDtypeStruct((rows, units), bf16),
        jax.ShapeDtypeStruct((rows, units), bf16),
        jax.ShapeDtypeStruct((rows, depth), f32),
        jax.ShapeDtypeStruct((rows + EXTRA, depth), f32),
    ]
    unit_out = pl.BlockSpec((rows, block), lambda i: (0, i))
    return pl.pallas_call(
        forward_kernel,
        out_shape=outs,
        grid=(steps,),
        in_specs=[SCALAR]
        + [whole(array) for array in gathered]
        + [own_rows, own_rows, whole(w_out), whole(gain)]
        + [ANYWHERE] * 3,
        out_specs=[
            whole(outs[0]),
            whole(outs[1]),
            unit_out,
            unit_out,
            unit_out,
            whole(outs[5]),
            whole(outs[6]),
        ],
        scratch_shapes=[
            pltpu.VMEM((rows, depth), bf16),
            pltpu.VMEM((steps, depth, block), bf16),
            pltpu.VMEM((steps, depth, block), bf16),
            pltpu.VMEM((steps, block, depth), bf16),
            pltpu.SemaphoreType.DMA((3, steps)),
        ],
        compiler_params=params(),
        cost_estimate=cost(
            2 * rows * depth * (6 * units + w_out.shape[1]),
            2 * depth * (3 * units + w_out.shape[1]) + 22 * rows * depth,
            rows * units,
        ),
    )(level, *gathered, tokens, dout, w_out, gain, w_gate, w_up, w_down)


def hidden_grad(inner, total_ref, final_ref, hidden_ref, dout_ref, gain_ref):
    dnormed = jnp.where(inner, total_ref[...], final_ref[...])
    hidden = hidden_ref[...]
    rms = lax.rsqrt(jnp.mean(hidden * hidden, -1, keepdims=True) + norm_eps)
    scaled = dnormed * gain_ref[...]
    shift = jnp.mean(scaled * hidden, -1, keepdims=True)
    dhid = dout_ref[...].astype(jnp.float32) + (rms * scaled - hidden * (rms**3 * shift))
    return dhid, dnormed * (hidden * rms)


def backward_kernel(
    start, full, adding, steps, level_ref, total_ref, final_ref, hidden_ref, dout_ref, *refs
):
    gain_two_ref, wo_ref, q_ref = refs[:3]
    kv_here = q_ref.shape[1] // KV_WIDE
    refs = refs[3:]
    kv_refs, refs = refs[: 2 * kv_here], refs[2 * kv_here :]
    part_ref, place_ref, strip_ref, cos_ref, sin_ref = refs[:5]
    extra = (2 if full else 0) + (1 if adding else 0) + 1
    outs, scratch = refs[5 : -3 - extra], refs[-3 - extra :]
    dhid_ref, low_ref, dn_ref, sems = scratch[:4]
    if full:
        x_any, gain_one_ref, other_ref, across_ref, outer_ref, w_any = outs[:6]
        outs = outs[6:]
        x_ref, w_buffers = scratch[4:6]
        tokens_here = pltpu.make_async_copy(
            x_any.at[pl.ds(start, x_ref.shape[0]), :], x_ref, sems.at[4]
        )
    count = (5 if start > 0 else 4) if full else 2
    if adding:
        acc_any, acc_buffers = outs[0], scratch[-1]
    outs = outs[-count:]
    dhid_t_ref, dqkv_ref = outs[:2]
    if full:
        input_grad_ref, gains_ref = outs[2:4]
    rows = q_ref.shape[0]
    keys = kv_refs[0].shape[0]
    shard = pl.program_id(0)
    level = level_ref[0]
    inner = (level == 1) | (level == 2)

    def fetched(at, sums):
        source, buffers = (acc_any, acc_buffers) if sums else (w_any, w_buffers)
        lanes = buffers.shape[2]
        here = pl.ds(pl.multiple_of(at * lanes, lanes), lanes)
        slot = at % 2
        sem = sems.at[slot + 2] if sums else sems.at[slot]
        return pltpu.make_async_copy(source.at[:, here], buffers.at[slot], sem)

    def fetch(at):
        if adding:
            fetched(at, True).start()
        if full:
            fetched(at, False).start()

    @pl.when(shard == 0)
    def _():
        for at in range(min(2, steps)):
            fetch(at)
        if full:
            tokens_here.start()
        dhid, dgain = hidden_grad(
            inner, total_ref, final_ref, hidden_ref, dout_ref, gain_two_ref
        )
        dhid_ref[...] = dhid
        low = dhid.astype(jnp.bfloat16)
        low_ref[...] = low
        dhid_t_ref[...] = low.T
        if full:
            gains_ref[...] = jnp.zeros_like(gains_ref)
            gains_ref[1:2, :] = jnp.sum(dgain, 0, keepdims=True)
            dn_ref[...] = jnp.zeros_like(dn_ref)

    def rotate_back(grads):
        turned = grads * cos_ref[...] - pltpu.roll(grads, LANES // 2, 1) * sin_ref[...]
        return turned.astype(jnp.bfloat16)

    dmixed_all = dot32(low_ref[...], wo_ref[...]).astype(jnp.bfloat16)
    mixed = part_ref[...]
    if full:
        far = jnp.where(inner, across_ref[...], outer_ref[...])
        far = jnp.where(shard == 1, other_ref[...], far)
        mixed = jnp.where(shard == 0, mixed, far)
    products = dmixed_all.astype(jnp.float32) * dot_split(mixed[:rows], place_ref[...])
    causal = lax.broadcasted_iota(jnp.int32, (rows, rows), 0) <= lax.broadcasted_iota(
        jnp.int32, (rows, rows), 1
    )
    acc_ref = None
    if adding:
        fetched(shard, True).wait()
        acc_ref = acc_buffers.at[shard % 2]
    grads = []
    for kv in range(kv_here):
        key_ref, value_ref = kv_refs[2 * kv : 2 * kv + 2]
        heads = range(kv * GROUP, (kv + 1) * GROUP)
        lanes = {h: slice(h * LANES, (h + 1) * LANES) for h in heads}
        row_dots = {h: jnp.sum(products[:, lanes[h]].T, axis=0, keepdims=True) for h in heads}
        log_sums = {h: mixed[rows + h : rows + h + 1, :rows] for h in heads}
        dqueries = dict.fromkeys(heads)
        here = slice(2 * kv * LANES, (2 * kv + 1) * LANES)
        there = slice((2 * kv + 1) * LANES, (2 * kv + 2) * LANES)
        for tile in range(keys // rows):
            span = slice(tile * rows, (tile + 1) * rows)
            key = key_ref[span, :]
            value = value_ref[span, :]
            key_t = key.T
            dkey = None if acc_ref is None else acc_ref[span, here]
            dvalue = None if acc_ref is None else acc_ref[span, there]
            last = tile * rows == start
            for h in heads:
                at = kv * KV_WIDE + (h % GROUP) * LANES
                query = q_ref[:, at : at + LANES]
                dmixed = dmixed_all[:, lanes[h]]
                raw = dot32_nt(key, query)
                probs = jnp.exp2(raw * score_scale_log2 - log_sums[h])
                if last:
                    probs = jnp.where(causal, probs, 0.0)
                dprobs = dot32_nt(value, dmixed)
                dscores = (probs * (dprobs - row_dots[h])).astype(jnp.bfloat16)
                dquery = dot32(key_t, dscores)
                dqueries[h] = dquery if dqueries[h] is None else dqueries[h] + dquery
                dkey_one = dot32(dscores, query)
                dvalue_one = dot32(probs.astype(jnp.bfloat16), dmixed)
                dkey = dkey_one if dkey is None else dkey + dkey_one
                dvalue = dvalue_one if dvalue is None else dvalue + dvalue_one
            if full and not last:
                outs[4][span, here] = dkey
                outs[4][span, there] = dvalue
        grads += [rotate_back(dqueries[h].T * score_scale) for h in heads]
        grads.append(rotate_back(dkey * score_scale))
        grads.append(dvalue.astype(jnp.bfloat16))
    grads = jnp.concatenate(grads, 1)
    if full:
        fetched(shard, False).wait()
        dn_ref[...] += dot32_nt(grads, w_buffers[shard % 2])

        @pl.when(shard + 2 < steps)
        def _():
            fetch(shard + 2)

    @pl.when(shard == 0)
    def _():
        wide = strip_ref.shape[1]
        for kv in range(kv_here):
            dqkv_ref[:, kv * wide : (kv + 1) * wide] = dot32(
                grads[:, kv * KV_WIDE : (kv + 1) * KV_WIDE], strip_ref[...]
            ).astype(jnp.bfloat16)

    if not full:
        return

    @pl.when(shard == pl.num_programs(0) - 1)
    def _():
        tokens_here.wait()
        dnormed = dn_ref[...]
        inputs = x_ref[...].astype(jnp.float32)
        rms = lax.rsqrt(jnp.mean(inputs * inputs, -1, keepdims=True) + norm_eps)
        scaled = dnormed * gain_one_ref[...]
        shift = jnp.mean(scaled * inputs, -1, keepdims=True)
        grad = dhid_ref[...] + (rms * scaled - inputs * (rms**3 * shift))
        input_grad_ref[...] = grad.astype(jnp.bfloat16)
        gains_ref[0:1, :] = jnp.sum(dnormed * (inputs * rms), 0, keepdims=True)


def backward_chunk(
    level, sums_two, hidden, dout, tokens, gains, weights, qkv, gathered, places, tables, acc,
    index, rows, full=True, grad_into=None
):
    start = index * rows
    keys = start + rows
    depth = tokens.shape[1]
    out_pad, qkv_pad = weights
    place_out, strip = places
    far_rows, width = gathered[0].shape
    out_wide = place_out.shape[1]
    kv_here = out_wide // (GROUP * LANES)
    wide = kv_here * KV_WIDE
    levels = qkv.shape[1] // wide
    own_rows = pl.BlockSpec((rows, depth), lambda t: (index, 0))
    table = pl.BlockSpec((rows, LANES), lambda t: (index, 0))
    gains = [gain[None, :] for gain in gains]
    key_value = lambda at: pl.BlockSpec(
        (keys, LANES), lambda t: (0, (wide // LANES) * t + at)
    )
    across = pl.BlockSpec((far_rows, width), lambda t: (0, jnp.where(t == 2, 1, 0)))
    outer = pl.BlockSpec((far_rows, width), lambda t: (0, jnp.where(t == 3, 1, 0)))
    in_specs = [
        SCALAR,
        whole(hidden),
        whole(hidden),
        whole(hidden),
        own_rows,
        whole(gains[1]),
        pl.BlockSpec((depth, out_wide), lambda t: (0, t)),
        pl.BlockSpec((rows, wide), lambda t: (index, t)),
    ]
    for kv in range(kv_here):
        at = kv * (KV_WIDE // LANES) + GROUP
        in_specs += [key_value(at), key_value(at + 1)]
    in_specs += [
        whole(gathered[0]),
        whole(place_out),
        whole(strip),
        table,
        table,
    ]
    args = [level, *sums_two, hidden, dout, gains[1], out_pad]
    args += [qkv] * (1 + 2 * kv_here)
    args += [gathered[0], place_out, strip, *tables]
    sums_wide = 2 * kv_here * LANES
    if full:
        in_specs += [ANYWHERE, whole(gains[0]), whole(gathered[1]), across, outer]
        in_specs.append(ANYWHERE)
        args += [tokens, gains[0], *gathered[1:], qkv_pad]
    if acc is not None:
        in_specs.append(ANYWHERE)
        args.append(acc)
    f32, bf16 = jnp.float32, jnp.bfloat16
    outs = [
        jax.ShapeDtypeStruct((depth, rows), bf16),
        jax.ShapeDtypeStruct((rows, kv_here * strip.shape[1]), bf16),
        jax.ShapeDtypeStruct(tokens.shape, bf16),
        jax.ShapeDtypeStruct((8, depth), f32),
    ]
    outs = outs if full else outs[:2]
    out_specs = [whole(out) for out in outs]
    aliases = {}
    if full:
        out_specs[2] = own_rows
        if grad_into is not None:
            aliases = {len(args): 2}
            in_specs.append(ANYWHERE)
            args.append(grad_into)
    if full and start > 0:
        outs.append(jax.ShapeDtypeStruct((start, levels * sums_wide), f32))
        out_specs.append(pl.BlockSpec((start, sums_wide), lambda t: (0, t)))
    steps = levels if full else 1
    scratch = [
        pltpu.VMEM((rows, depth), f32),
        pltpu.VMEM((rows, depth), bf16),
        pltpu.VMEM((rows, depth), f32),
        pltpu.SemaphoreType.DMA((5,)),
    ]
    if full:
        scratch += [pltpu.VMEM((rows, depth), bf16), pltpu.VMEM((2, depth, wide), bf16)]
    if acc is not None:
        scratch.append(pltpu.VMEM((min(2, steps), keys, sums_wide), f32))
    results = pl.pallas_call(
        functools.partial(backward_kernel, start, full, acc is not None, steps),
        out_shape=outs,
        grid=(steps,),
        input_output_aliases=aliases,
        in_specs=in_specs,
        out_specs=out_specs,
        scratch_shapes=scratch,
        compiler_params=params(),
        cost_estimate=cost(
            levels * rows * (20 * kv_here * keys * LANES + 2 * depth * (out_wide + wide)),
            2 * depth * levels * (out_wide + wide) + 16 * rows * depth,
            levels * kv_here * GROUP * rows * keys,
        ),
    )(*args)
    return results[:4], (results[4] if full and start > 0 else None)


def rows_kernel(lefts, groups, adding, picked, together, side_ref, *refs):
    refs = list(refs)
    held_ref = refs.pop()
    out_refs = refs[-len(picked) :]
    refs = refs[: -len(picked)]
    recv_ref = refs.pop() if adding else None
    step = pl.program_id(0)
    left_refs = []
    for count in lefts:
        left_refs.append(refs[:count])
        refs = refs[count:]
    rights = []
    for _ in groups:
        rights.append(refs[:CHUNKS])
        refs = refs[CHUNKS:]
    rows = left_refs[0][0].shape[0]
    blocks = held_ref.shape[1] // rows

    @pl.when(step == 0)
    def _():
        for which, pieces in enumerate(left_refs):
            for n, ref in enumerate(pieces):
                m, j = n % blocks, n // blocks
                wide = ref.shape[1]
                held_ref[which, m * rows : (m + 1) * rows, j * wide : (j + 1) * wide] = ref[...]

    chunk = held_ref.shape[2] // CHUNKS
    whole_columns = slice(0, out_refs[0].shape[1])

    def give(group, left, columns):
        right = jnp.concatenate([ref[:chunk, :].astype(jnp.bfloat16) for ref in group], 0)
        total = dot32(held_ref[left], right)
        if recv_ref is not None:
            total = total + recv_ref[:, columns]
        for out_ref, parts in zip(out_refs, picked):
            at = 0
            for start, size in parts:
                out_ref[at : at + size, columns] = total[start : start + size]
                at += size

    begin = 0
    for group, (left, first, steps) in zip(rights, groups):
        if together:
            width = group[0].shape[1]
            give(group, left, slice(begin, begin + width))
            begin += width
        else:

            @pl.when((step >= first) & (step < first + steps))
            def _(group=group, left=left):
                give(group, left, whole_columns)


def rows_of(lefts, groups, side, rows, blocks, step, recv=None, picked=None):
    if picked is None:
        picked = [[(0, rows * blocks)]]
    at = lambda m: lambda i, side: ((m ^ side[2]) * side[1] + side[0], 0)
    specs = []
    args = []
    counts = []
    for left in lefts:
        pieces = left if isinstance(left, list) else [left]
        counts.append(len(pieces) * blocks)
        for piece in pieces:
            for m in range(blocks):
                specs.append(pl.BlockSpec((rows, piece.shape[1]), at(m)))
                args.append(piece)
    tokens = sum(piece.shape[1] for piece in pieces)
    first = 0
    plan = []
    together = step is None
    for which, rights in groups:
        if together:
            plan.append((which, 0, 1))
            specs += [whole(right) for right in rights]
            args += rights
            first += rights[0].shape[1]
            continue
        steps = rights[0].shape[1] // step
        plan.append((which, first, steps))
        for right in rights:
            pick = lambda i, side, first=first, steps=steps: (0, jnp.clip(i - first, 0, steps - 1))
            specs.append(pl.BlockSpec((right.shape[0], step), pick))
            args.append(right)
        first += steps
    if together:
        first, step = 1, first
    total = first * step
    block = lambda height: pl.BlockSpec((height, step), lambda i, side: (0, i))
    if recv is not None:
        specs.append(block(rows * blocks))
        args.append(recv)
    heights = [sum(size for _, size in parts) for parts in picked]
    results = pl.pallas_call(
        functools.partial(rows_kernel, counts, plan, recv is not None, picked, together),
        out_shape=[jax.ShapeDtypeStruct((height, total), jnp.float32) for height in heights],
        grid_spec=pltpu.PrefetchScalarGridSpec(
            num_scalar_prefetch=1,
            grid=(first,),
            in_specs=specs,
            out_specs=[block(height) for height in heights],
            scratch_shapes=[pltpu.VMEM((len(lefts), rows * blocks, tokens), jnp.bfloat16)],
        ),
        compiler_params=params(),
        cost_estimate=cost(
            2 * rows * blocks * tokens * total,
            4 * rows * blocks * total + 2 * tokens * (total + rows * blocks),
        ),
    )(side, *args)
    return results[0] if len(picked) == 1 else results


def shards(
    tokens,
    lengths,
    positions,
    cotangent,
    norm_gain,
    w_query,
    w_key,
    w_value,
    w_out,
    mlp_gain,
    w_gate,
    w_up,
    w_down,
):
    seq_rows, depth = tokens.shape
    chips = lax.axis_size("chip")
    dp = chips * 2
    tp = lax.axis_size("tp")
    chip = lax.axis_index("chip")
    core = lax.axis_index("core")
    level = lax.axis_index("tp")
    low = level < 2
    inner = (level == 1) | (level == 2)
    heads_here = w_query.shape[1] // HD
    kv_here = w_key.shape[1] // HD
    rows = seq_rows // CHUNKS
    slice_rows = depth // dp
    level_ref = level.astype(jnp.int32).reshape(1)
    by_hand = dp == 8
    swap = lambda array: lax.ppermute(array, "core", [(0, 1), (1, 0)])
    to_level = lambda array, s: along(array, [(t, t ^ s) for t in range(tp)])

    at_row = (chip * 2 + core) * slice_rows
    cols = lambda w: lax.dynamic_slice_in_dim(w, at_row, slice_rows, 1).astype(jnp.float32).T
    (out_slice,) = fence(cols(w_out))
    qkv_slice = jnp.concatenate(
        [
            lax.dynamic_slice_in_dim(w_query, at_row, slice_rows, 0).astype(jnp.float32),
            cols(w_key.T),
            cols(w_value.T),
        ],
        1,
    )
    out_slice, qkv_slice = fence(out_slice, qkv_slice)
    out_near = along(out_slice, PAIRS)
    qkv_near = along(qkv_slice, PAIRS)
    meta = jnp.stack([chip, core]).astype(jnp.int32)

    pq = place_query(heads_here)
    pkv = place_key_value(kv_here)
    p_all = place_all(heads_here, kv_here)
    strip_one = place_all(GROUP, 1).T
    p_out = place_plain(heads_here)
    strip_out = p_out.T

    half_dim = HD // 2
    freqs = rope_base ** (-(jnp.arange(half_dim).astype(jnp.float32) * 2.0 / HD))
    freqs = jnp.pad(freqs, (0, LANES // 2 - half_dim))
    angles = positions.astype(jnp.float32)[:, None] * jnp.concatenate([freqs, freqs])[None, :]
    cosines = jnp.cos(angles)
    sines = jnp.sin(angles) * jnp.where(jnp.arange(LANES) < LANES // 2, -1.0, 1.0)

    cosines, sines, out_near = fence(cosines, sines, out_near)
    out_across = along(jnp.stack([out_slice, out_near]), MIDDLE)
    qkv_own, normed_one, own_pad = start(
        tokens, norm_gain, w_query, w_key.T, w_value.T, pq, pkv, cosines, sines
    )

    def far_slices(near, across, outer):
        return jnp.stack(
            [
                near,
                jnp.where(inner, across[1], outer[0]),
                jnp.where(inner, across[0], outer[1]),
            ]
        )

    order = list(reversed(range(CHUNKS)))
    c0, c1, c2, c3 = order
    own, other, across, outer = {}, {}, {}, {}
    part, total, final = {}, {}, {}

    def hop_1(j):
        other[j] = along(own[j], PAIRS)

    def hop_2(j):
        across[j] = along(jnp.concatenate([own[j], other[j]], 1), MIDDLE)

    def hop_3(j):
        outer[j] = along(across[j], OUTWARD)

    coming = {}

    def add_1(j):
        coming[j] = along(part[j], INWARD)

    def add_2(j):
        total[j] = part[j][:rows] + coming[j][:rows]
        coming[j] = along(total[j], MIDDLE)

    def add_3(j, inward, extra=0):
        both = jnp.where(inner, total[j] + coming[j], inward)
        total[j] = jnp.pad(both, ((0, extra), (0, 0)))
        final[j] = along(total[j], PAIRS)
        return final[j]

    def to_chip(array, m):
        return lax.ppermute(array, "chip", [(i, i ^ m) for i in range(chips)])

    def over_chips_1(piece):
        cut = piece.shape[1] // 2
        one, two = piece[:, :cut], piece[:, cut:]
        return jnp.stack([one, to_chip(one, 1)]), jnp.stack([two, to_chip(two, 2)])

    def over_chips_2(one, two):
        return one, to_chip(one, 2), two, to_chip(two, 1)

    def over_chips_3(one, one_far, two, two_far):
        upper = jnp.stack([one[0], one[1], one_far[0], one_far[1]])
        lower = jnp.stack([two[0], two_far[0], two[1], two_far[1]])
        return jnp.concatenate([upper, lower], 2)

    qkv_own, out_across, qkv_near = fence(qkv_own, out_across, qkv_near)
    out_outer = along(out_across, OUTWARD)
    qkv_across = along(jnp.stack([qkv_slice, qkv_near]), MIDDLE)
    own[c0] = attend(lengths, qkv_own, strip_out, c0, rows)
    own[c1] = attend(lengths, qkv_own, strip_out, c1, rows)
    own, qkv_own, out_outer = fence(own, qkv_own, out_outer)
    others = along(jnp.concatenate([own[c0], own[c1]], 0), PAIRS)
    out_far = far_slices(out_near, out_across, out_outer)
    out_mine = over_chips_1(out_far) if by_hand else out_far
    own[c2] = attend(lengths, qkv_own, strip_out, c2, rows)
    own[c3] = attend(lengths, qkv_own, strip_out, c3, rows)
    own[c3], qkv_across = fence(own[c3], qkv_across)
    qkv_outer = along(qkv_across, OUTWARD)
    own, others, normed_one, w_out, out_mine = fence(own, others, normed_one, w_out, out_mine)
    other[c0], other[c1] = others[: rows + EXTRA], others[rows + EXTRA :]
    if by_hand:
        out_mine = over_chips_2(*out_mine)
    else:
        out_mine = lax.all_gather(out_mine, ("chip", "core"))
    hop_2(c0)
    dout, dout_t, normed_one_t = turn(lengths, cotangent, normed_one)
    w_out_t = w_out.T
    own, other, across, dout, dout_t, normed_one_t, w_out_t, out_mine, qkv_outer = fence(
        own, other, across, dout, dout_t, normed_one_t, w_out_t, out_mine, qkv_outer
    )
    hop_1(c2)
    hop_3(c0)
    hop_2(c1)
    qkv_far = lax.all_gather(far_slices(qkv_near, qkv_across, qkv_outer), ("chip", "core"))
    if by_hand:
        out_mine = over_chips_3(*out_mine)
        out_theirs = swap(out_mine)
        out_pad, out_plain = spread(
            spread_out_kernel,
            meta,
            w_out_t,
            [p_out],
            out_mine,
            out_theirs,
            [4 * p_out.shape[1], 4 * p_out.shape[0]],
        )
    else:
        plain = [w_out_t] + [
            out_mine[:, s].reshape(depth, -1).astype(jnp.bfloat16) for s in range(tp - 1)
        ]
        out_plain = jnp.concatenate(plain, 1)
        out_pad = jnp.concatenate([dot32(w, p_out).astype(jnp.bfloat16) for w in plain], 1)
    hidden, normed_t, activ, dgate, dup, mlp_part = {}, {}, {}, {}, {}, {}

    def feed(j):
        gathered = (own[j], other[j], across[j], outer[j])
        (hidden[j], normed_t[j], activ[j], dgate[j], dup[j], mlp_part[j], part[j]) = forward_chunk(
            level_ref, gathered, tokens, dout, out_plain, mlp_gain, w_gate, w_up, w_down, j, rows
        )

    own, other, across, outer, out_pad, out_plain = fence(
        own, other, across, outer, out_pad, out_plain
    )
    hop_1(c3)
    hop_3(c1)
    hop_2(c2)
    feed(c0)
    part, other = fence(part, other)
    add_1(c0)
    own, other, across, outer, part, hidden = fence(own, other, across, outer, part, hidden)
    hop_3(c2)
    hop_2(c3)
    feed(c1)
    qkv_far, hidden[c1] = fence(qkv_far, hidden[c1])
    qkv_pad = spread_qkv(own_pad, pq, pkv, qkv_far)
    own, other, across, outer, part, total, coming, hidden, qkv_pad = fence(
        own, other, across, outer, part, total, coming, hidden, qkv_pad
    )
    add_1(c1)
    hop_3(c3)
    add_2(c0)
    feed(c2)
    qkv_pad, hidden[c2] = fence(qkv_pad, hidden[c2])
    qkv = project(normed_one, qkv_pad, cosines, sines, qkv_own)
    own, other, across, outer, part, total, coming, hidden, qkv = fence(
        own, other, across, outer, part, total, coming, hidden, qkv
    )
    coming[c2] = add_3(c0, part[c2][:rows])
    add_2(c1)
    feed(c3)

    listed = lambda pieces: [pieces[j] for j in range(CHUNKS)]
    keep_side = jnp.stack([core, 2, 0]).astype(jnp.int32)
    keep_turned = jnp.stack([core, 2, chip]).astype(jnp.int32)
    send_side = jnp.stack([1 - core, 2, 0]).astype(jnp.int32)
    send_turned = jnp.stack([1 - core, 2, chip]).astype(jnp.int32)
    all_rows = jnp.array([0, 1, 0], jnp.int32)

    def send_rows(lefts, groups, step, side=send_side):
        if not by_hand:
            return rows_of(lefts, groups, all_rows, depth // 4, 4, step)
        return rows_of(lefts, groups, side, slice_rows, chips, step)

    def keep_rows(lefts, groups, received, step, side=keep_side, picked=None):
        if not by_hand:
            return received
        return rows_of(lefts, groups, side, slice_rows, chips, step, received, picked)

    def swap_rows(array):
        return swap(array) if by_hand else array

    def scatter(array, axes):
        return lax.psum_scatter(array, axes, scatter_dimension=0, tiled=True)

    units = w_gate.shape[1]
    mlp_args = (
        [listed(normed_t), dout_t],
        [(0, listed(dgate)), (0, listed(dup)), (1, listed(activ))],
    )
    acc = None
    input_grad = None
    dhid_t, dqkv_own, gains = {}, {}, {}

    def back(j):
        nonlocal acc, input_grad
        (dhid_t[j], dqkv_own[j], input_grad, gains[j]), acc = back_some(j, True)

    def back_own(j):
        return back_some(j, False)[0]

    def back_some(j, full):
        return backward_chunk(
            level_ref,
            (total[j], final[j]),
            hidden[j],
            dout,
            tokens,
            (norm_gain, mlp_gain),
            (out_pad, qkv_pad),
            qkv,
            (own[j], other[j], across[j], outer[j]),
            (p_out, strip_one),
            (cosines, sines),
            acc,
            j,
            rows,
            full,
            input_grad,
        )

    grad_mlp = rows_of(*mlp_args, all_rows, depth // 4, 4, units // 2)
    own, other, across, outer, part, total, coming, final, hidden, grad_mlp = fence(
        own, other, across, outer, part, total, coming, final, hidden, grad_mlp
    )
    grad_mlp = scatter(grad_mlp, ("chip", "core"))
    coming[c3] = add_3(c1, part[c3][:rows])
    add_2(c2)
    back(c0)

    near = lambda: jnp.where(low, mlp_part[1], mlp_part[2])
    edge = lambda: jnp.where(low, mlp_part[0], mlp_part[3])
    leave_far = lambda: jnp.where(low, mlp_part[3], mlp_part[0])
    leave_near = lambda: jnp.where(low, mlp_part[2], mlp_part[1])
    total, coming, final, hidden, mlp_part, acc, dhid_t = fence(
        total, coming, final, hidden, mlp_part, acc, dhid_t
    )
    far_sum = add_3(c2, leave_far())
    add_2(c3)
    back(c1)
    total, coming, final, hidden, mlp_part, far_sum, acc, dhid_t = fence(
        total, coming, final, hidden, mlp_part, far_sum, acc, dhid_t
    )
    add_3(c3, leave_near(), EXTRA)
    far_in = along(leave_far() + far_sum, MIDDLE)
    back(c2)
    total, final, hidden, acc, dhid_t = fence(total, final, hidden, acc, dhid_t)
    dhid_t[c3], dqkv_own[c3] = back_own(c3)
    dhid_t, dqkv_own, far_in, mlp_part, final = fence(
        dhid_t, dqkv_own, far_in, mlp_part, final
    )
    last = along(jnp.where(inner, edge() + far_in, near()), PAIRS)
    near_in = along(leave_near() + final[c3][:rows], MIDDLE)
    q_cols = heads_here * HD
    attn_args = (
        [listed(dhid_t), normed_one_t],
        [(0, listed(own)), (1, listed(dqkv_own))],
    )
    sent = swap_rows(send_rows(*attn_args, None, send_turned))
    total, final, hidden, acc, sent = fence(total, final, hidden, acc, sent)
    if by_hand:
        half = slice_rows // 2
        upper = lambda m: (m * slice_rows, half)
        lower = lambda m: (m * slice_rows + half, half)
        picked = [
            [upper(1), upper(3)],
            [upper(0), upper(2)],
            [lower(2), lower(3)],
            [lower(0), lower(1)],
        ]
        pieces = keep_rows(*attn_args, sent, None, keep_turned, picked)
        pieces, hidden = fence(pieces, hidden)
        one_away, one, two_away, two = pieces
        pieces = (one, to_chip(one_away, 1), two, to_chip(two_away, 2))
    else:
        pieces = scatter(sent, ("chip", "core"))
    back(c3)
    pieces, gains, input_grad = fence(pieces, gains, input_grad)
    gain_sums = gains[0] + gains[1] + gains[2] + gains[3]
    gain_sums = gain_sums + swap(gain_sums)
    gain_sums, last, near_in = fence(gain_sums, last, near_in)
    if by_hand:
        others = [to_chip(gain_sums, m) for m in range(1, chips)]
        gain_sums = sum(others, gain_sums)
        one = pieces[0] + pieces[1]
        two = pieces[2] + pieces[3]
        one = one[:half] + to_chip(one[half:], 2)
        two = two[:half] + to_chip(two[half:], 1)
        attn = jnp.concatenate([one, two], 0)
    else:
        gain_sums = lax.psum(gain_sums, "chip")
        attn = pieces
    gain_rows = lax.dynamic_slice_in_dim(gain_sums, at_row, slice_rows, 1)
    grad_out, grad_qkv = attn[:, :q_cols], attn[:, q_cols:]
    mlp_rows = jnp.where(inner, near() + near_in, edge()) + last
    hidden_rows = jnp.where(
        low,
        jnp.where(level == 0, hidden[0], hidden[1]),
        jnp.where(level == 2, hidden[2], hidden[3]),
    )
    layer_out = (hidden_rows + mlp_rows).astype(jnp.bfloat16)
    one = strip_one.shape[1]
    picked = lambda at, width: jnp.concatenate(
        [grad_qkv[:, kv * one + at : kv * one + at + width] for kv in range(kv_here)], 1
    )
    return (
        layer_out,
        input_grad,
        gain_rows[0],
        picked(0, GROUP * HD),
        picked(GROUP * HD, HD),
        picked((GROUP + 1) * HD, HD),
        grad_out.T,
        gain_rows[1],
        grad_mlp[:, :units],
        grad_mlp[:, units : 2 * units],
        grad_mlp[:, 2 * units :].T,
    )


def solution(mesh):
    devices = mesh.devices
    dp, tp = devices.shape
    split = Mesh(devices.reshape(dp // 2, 2, tp), ("chip", "core", "tp"))
    data = ("chip", "core")
    return jax.shard_map(
        shards,
        mesh=split,
        in_specs=(
            P(data, None),
            P(data),
            P(data),
            P(data, None),
            P(),
            P(None, "tp"),
            P(None, "tp"),
            P(None, "tp"),
            P("tp", None),
            P(),
            P(None, "tp"),
            P(None, "tp"),
            P("tp", None),
        ),
        out_specs=(
            P(("chip", "core", "tp"), None),
            P(data, None),
            P(data),
            P(data, "tp"),
            P(data, "tp"),
            P(data, "tp"),
            P("tp", data),
            P(data),
            P(data, "tp"),
            P(data, "tp"),
            P("tp", data),
        ),
        check_vma=False,
    )
```

profile of v0, /device:TPU:0, one launch (start us, length us, event | category | flops | bytes accessed | tf_op | source)
XLA Modules:
  0.0 499.0 jit_solution(2424781664140223339)
XLA Ops:
  17.3 4.5 collective-permute-done
  25.1 10.4 %shard_map.221 = (bf16[1024,4096]{1,0:T(8,128)(2,1)}, bf16[1024,1536]{1,0:T(8,128)(2,1)}, bf16[1536,4096]{1,0:T(8,128)(2,1)}) custom-call(bf16[1024,1536]{1,0:T(8,128)(2,1)} %refs_12_.7, f32[1,1536]{1,0:T(1,128)} %broadcast_in_dim.10.gain_ref.refs_13_, bf16[1536,384]{1,0:T(8,128)(2,1)} %q_ref.1, bf16[192,1536]{1,0:T(8,128)(2,1)} %bitcast.34, ...), custom_call_target="tpu_custom_call" | custom-call | flops 3145728 | bytes 18432 | tf_op jit(solution)/shard_map/pallas_call | solution.py:229
  40.3 5.7 %shard_map.222.part_ref.refs_7_.refs_22_ = f32[264,384]{1,0:T(8,128)} custom-call(s32[1]{0:T(128)S(6)} %copy.46.length_ref, bf16[1024,4096]{1,0:T(8,128)(2,1)} %get-tuple-element.310.q_ref.kv_ref._, bf16[1024,4096]{1,0:T(8,128)(2,1)} %get-tuple-element.310.q_ref.kv_ref._, bf16[512,384]{1,0:T(8,128)(2,1)} %fusion.2.strip_ref), custom_call_target="tpu_custom_call" | custom-call | flops 393216 | bytes 2048 | tf_op jit(solution)/shard_map/pallas_call | solution.py:336
  46.0 6.5 %shard_map.223.part_ref.refs_7_.refs_23_ = f32[264,384]{1,0:T(8,128)} custom-call(s32[1]{0:T(128)S(6)} %copy.46.length_ref, bf16[1024,4096]{1,0:T(8,128)(2,1)} %get-tuple-element.310.q_ref.kv_ref._, bf16[1024,4096]{1,0:T(8,128)(2,1)} %get-tuple-element.310.q_ref.kv_ref._, bf16[512,384]{1,0:T(8,128)(2,1)} %fusion.2.strip_ref), custom_call_target="tpu_custom_call" | custom-call | flops 524288 | bytes 2560 | tf_op jit(solution)/shard_map/pallas_call | solution.py:336
  53.7 6.0 %collective-permute-start.5 = (f32[528,384]{1,0:T(8,128)S(1)}, f32[528,384]{1,0:T(8,128)S(1)}, u32[]{:S(2)}, u32[]{:S(2)}) collective-permute-start(f32[528,384]{1,0:T(8,128)S(1)} %pad_maximum_fusion.5), channel_id=1, source_target_pairs={{0,1},{1,0},{2,3},{3,2},{4,5},{5,4},{6,7},{7,6},{8,9},{9,8},{10,11... | collective-permute-start | bytes 2433032 | tf_op jit(solution)/shard_map/ppermute | solution.py:109
  63.1 3.9 shard_map.224.part_ref.refs_7_.refs_20_
  67.1 4.8 shard_map.225.part_ref.refs_7_.refs_21_
  73.5 3.8 collective-permute-done.5
  84.5 7.0 %shard_map.226 = (bf16[1024,1536]{1,0:T(8,128)(2,1)}, bf16[1536,1024]{1,0:T(8,128)(2,1)}, bf16[1536,1024]{1,0:T(8,128)(2,1)}) custom-call(s32[1]{0:T(128)S(6)} %copy.46.length_ref, bf16[1024,1536]{1,0:T(8,128)(2,1)} %cot_ref.1, bf16[1024,1536]{1,0:T(8,128)(2,1)} %get-tuple-element.322.normed_ref.x_ref), custom_call_target="tpu_custom_call" | custom-call | flops 1536 | bytes 15360 | tf_op jit(solution)/shard_map/pallas_call | solution.py:262
  94.7 5.9 %collective-permute-done.11 = f32[2,192,768]{2,1,0:T(8,128)} collective-permute-done((f32[2,192,768]{2,1,0:T(8,128)}, f32[2,192,768]{2,1,0:T(8,128)}, u32[]{:S(2)}, u32[]{:S(2)}) %collective-permute-start.11) | collective-permute-done | bytes 1179680 | tf_op jit(solution)/shard_map/ppermute | solution.py:109
  113.5 10.1 %shard_map.227 = (bf16[1536,2048]{1,0:T(8,128)(2,1)}, bf16[1536,1536]{1,0:T(8,128)(2,1)}) custom-call(s32[2]{0:T(128)} %pad_add_fusion.4.meta_ref, bf16[1536,384]{1,0:T(8,128)(2,1)} %bitcast.27, bf16[384,512]{1,0:T(8,128)(2,1)} %fusion.3.p_ref.refs_8_, f32[4,3,192,384]{3,2,1,0:T(8,128)} %copy-done.6, f32[4,3,192,384]{3,2,1,0:T(8,128)} %collective-permute-done.15.theirs_ref), custom_call_target="tpu_custom_call" | custom-call | flops 2359296 | bytes 17664 | tf_op jit(solution)/shard_map/pallas_call | solution.py:179
  123.6 15.5 %collective-permute-done.12.other_ref.refs_14_ = f32[264,384]{1,0:T(8,128)S(1)} collective-permute-done((f32[264,384]{1,0:T(8,128)S(1)}, f32[264,384]{1,0:T(8,128)S(1)}, u32[]{:S(2)}, u32[]{:S(2)}) %collective-permute-start.12) | collective-permute-done | bytes 405536 | tf_op jit(solution)/shard_map/ppermute | solution.py:109
  141.8 14.0 %shard_map.228 = (f32[256,1536]{1,0:T(8,128)}, bf16[1536,256]{1,0:T(8,128)(2,1)}, bf16[256,1024]{1,0:T(8,128)(2,1)}, bf16[256,1024]{1,0:T(8,128)(2,1)}, bf16[256...) custom-call(s32[1]{0:T(128)} %bitcast.2.level_ref, f32[264,384]{1,0:T(8,128)} %shard_map.223.part_ref.refs_7_.refs_23_, ...), custom_call_target="tpu_custom_call" | custom-call | flops 5898240 | bytes 22272 | tf_op jit(solution)/shard_map/pallas_call | solution.py:427
  155.9 7.4 %collective-permute-start.21 = (f32[264,1536]{1,0:T(8,128)}, f32[264,1536]{1,0:T(8,128)}, u32[]{:S(2)}, u32[]{:S(2)}) collective-permute-start(f32[264,1536]{1,0:T(8,128)} %get-tuple-element.401), channel_id=1, source_target_pairs={{0,1},{3,2},{4,5},{7,6},{8,9},{11,10},{12,13},{15,14},{16,17},{19,... | collective-permute-start | bytes 4866056 | tf_op jit(solution)/shard_map/ppermute | solution.py:109
  163.3 4.1 collective-permute-done.18.outer_ref.refs_16_
  170.4 14.1 %shard_map.229 = (f32[256,1536]{1,0:T(8,128)}, bf16[1536,256]{1,0:T(8,128)(2,1)}, bf16[256,1024]{1,0:T(8,128)(2,1)}, bf16[256,1024]{1,0:T(8,128)(2,1)}, bf16[256...) custom-call(s32[1]{0:T(128)} %bitcast.2.level_ref, f32[264,384]{1,0:T(8,128)} %shard_map.222.part_ref.refs_7_.refs_22_, ...), custom_call_target="tpu_custom_call" | custom-call | flops 5898240 | bytes 22272 | tf_op jit(solution)/shard_map/pallas_call | solution.py:427
  184.6 12.8 %shard_map.230.w_ref.refs_17_ = bf16[1536,4096]{1,0:T(8,128)(2,1)} custom-call(bf16[384,512]{1,0:T(8,128)(2,1)} %fusion.pq_ref, bf16[384,512]{1,0:T(8,128)(2,1)} %fusion.1.pkv_ref, f32[8,3,192,768]{3,2,1,0:T(8,128)} %bitcast.26, bf16[1536,4096]{1,0:T(8,128)(2,1)} %get-tuple-element.383._), custom_call_target="tpu_custom_call", output_to_operand_aliasing={{}: (3, {})} | custom-call | flops 4718592 | bytes 30720 | tf_op jit(solution)/shard_map/pallas_call | solution.py:157
  197.4 5.6 %collective-permute-start.23 = (f32[264,1536]{1,0:T(8,128)}, f32[264,1536]{1,0:T(8,128)}, u32[]{:S(2)}, u32[]{:S(2)}) collective-permute-start(f32[264,1536]{1,0:T(8,128)} %get-tuple-element.427), channel_id=1, source_target_pairs={{0,1},{3,2},{4,5},{7,6},{8,9},{11,10},{12,13},{15,14},{16,17},{19,... | collective-permute-start | bytes 4866056 | tf_op jit(solution)/shard_map/ppermute | solution.py:109
  208.0 13.9 %shard_map.231 = (f32[256,1536]{1,0:T(8,128)}, bf16[1536,256]{1,0:T(8,128)(2,1)}, bf16[256,1024]{1,0:T(8,128)(2,1)}, bf16[256,1024]{1,0:T(8,128)(2,1)}, bf16[256...) custom-call(s32[1]{0:T(128)} %bitcast.2.level_ref, f32[264,384]{1,0:T(8,128)} %shard_map.225.part_ref.refs_7_.refs_21_, ...), custom_call_target="tpu_custom_call" | custom-call | flops 5898240 | bytes 22272 | tf_op jit(solution)/shard_map/pallas_call | solution.py:427
  221.9 15.9 %shard_map.232.refs_2_.refs_3_.refs_4_.refs_5_.refs_6_ = bf16[1024,4096]{1,0:T(8,128)(2,1)} custom-call(bf16[1024,1536]{1,0:T(8,128)(2,1)} %get-tuple-element.322.normed_ref.x_ref, bf16[1536,4096]{1,0:T(8,128)(2,1)} %shard_map.230.w_ref.refs_17_, f32[1024,128]{1,0:T(8,128)} %get-tuple-element.303.cos_ref.refs_10_, ...), custom_call_target="tpu_custom_call", output_to_operand_aliasing={{}: (4, {})} | custom-call | flops 12582912 | bytes 23552 | tf_op jit(solution)/shard_map/pallas_call | solution.py:282
  246.6 13.9 %shard_map.233 = (f32[256,1536]{1,0:T(8,128)}, bf16[1536,256]{1,0:T(8,128)(2,1)}, bf16[256,1024]{1,0:T(8,128)(2,1)}, bf16[256,1024]{1,0:T(8,128)(2,1)}, bf16[256...) custom-call(s32[1]{0:T(128)} %bitcast.2.level_ref, f32[264,384]{1,0:T(8,128)} %shard_map.224.part_ref.refs_7_.refs_20_, ...), custom_call_target="tpu_custom_call" | custom-call | flops 5898240 | bytes 22272 | tf_op jit(solution)/shard_map/pallas_call | solution.py:427
  260.5 19.3 %shard_map.234 = f32[1536,3072]{1,0:T(8,128)} custom-call(s32[3]{0:T(128)} %constant.159.clone.side_ref, bf16[1536,256]{1,0:T(8,128)(2,1)} %get-tuple-element.435.refs_0_.refs_1_.refs_2_.refs_3_, bf16[1536,256]{1,0:T(8,128)(2,1)} %get-tuple-element.435.refs_0_.refs_1_.refs_2_.refs_3_, bf16[1536,256]{1,0:T(8,128)(2,1)} %get-tuple-element.435.refs_0_.refs_1_.refs_2_.refs_3_, ...), custom_call_target="tpu_custom_call" | custom-call | flops 9437184 | bytes 27648 | tf_op jit(solution)/shard_map/pallas_call | solution.py:818
  292.0 37.2 %shard_map.235 = (bf16[1536,256]{1,0:T(8,128)(2,1)}, bf16[256,768]{1,0:T(8,128)(2,1)}, bf16[1024,1536]{1,0:T(8,128)(2,1)}, f32[8,1536]{1,0:T(8,128)}, f32[768,2048]{1,0:T(8,128)}) custom-call(s32[1]{0:T(128)} %bitcast.2.level_ref, f32[256,1536]{1,0:T(8,128)} %copy-done.17, f32[256,1536]{1,0:T(8,128)} %collective-permute-done.25.final_ref, ...), custom_call_target="tpu_custom_call" | custom-call | flops 9961472 | bytes 24576 | tf_op jit(solution)/shard_map/pallas_call | solution.py:707
  329.3 4.0 select_select_fusion.1.total_ref
  338.9 31.7 %shard_map.236 = (bf16[1536,256]{1,0:T(8,128)(2,1)}, bf16[256,768]{1,0:T(8,128)(2,1)}, bf16[1024,1536]{1,0:T(8,128)(2,1)}, f32[8,1536]{1,0:T(8,128)}, f32[512,2048]{1,0:T(8,128)}) custom-call(s32[1]{0:T(128)} %bitcast.2.level_ref, f32[256,1536]{1,0:T(8,128)} %add_select_fusion.1.total_ref, ...), custom_call_target="tpu_custom_call", output_to_operand_aliasing={{2}: (24, {})} | custom-call | flops 8650752 | bytes 24576 | tf_op jit(solution)/shard_map/pallas_call | solution.py:707
  381.6 26.1 %shard_map.237 = (bf16[1536,256]{1,0:T(8,128)(2,1)}, bf16[256,768]{1,0:T(8,128)(2,1)}, bf16[1024,1536]{1,0:T(8,128)(2,1)}, f32[8,1536]{1,0:T(8,128)}, f32[256,2048]{1,0:T(8,128)}) custom-call(s32[1]{0:T(128)} %bitcast.2.level_ref, f32[256,1536]{1,0:T(8,128)} %select_select_fusion.1.total_ref, ...), custom_call_target="tpu_custom_call", output_to_operand_aliasing={{2}: (24, {})} | custom-call | flops 7340032 | bytes 24576 | tf_op jit(solution)/shard_map/pallas_call | solution.py:707
  408.3 7.5 %shard_map.238 = (bf16[1536,256]{1,0:T(8,128)(2,1)}, bf16[256,768]{1,0:T(8,128)(2,1)}) custom-call(s32[1]{0:T(128)} %bitcast.2.level_ref, f32[264,1536]{1,0:T(8,128)} %pad.9.total_ref, f32[264,1536]{1,0:T(8,128)} %collective-permute-done.31.final_ref, f32[256,1536]{1,0:T(8,128)} %get-tuple-element.555.hidden_ref, ...), custom_call_target="tpu_custom_call" | custom-call | flops 6029312 | bytes 24576 | tf_op jit(solution)/shard_map/pallas_call | solution.py:707
  415.8 7.8 %shard_map.239 = f32[768,1152]{1,0:T(8,128)} custom-call(s32[3]{0:T(128)} %get-tuple-element.623.side_ref, bf16[1536,256]{1,0:T(8,128)(2,1)} %get-tuple-element.533.refs_0_.refs_1_.refs_2_.refs_3_, bf16[1536,256]{1,0:T(8,128)(2,1)} %get-tuple-element.533.refs_0_.refs_1_.refs_2_.refs_3_, bf16[1536,256]{1,0:T(8,128)(2,1)} %get-tuple-element.533.refs_0_.refs_1_.refs_2_.refs_3_, ...), custom_call_target="tpu_custom_call" | custom-call | flops 1769472 | bytes 7296 | tf_op jit(solution)/shard_map/pallas_call | solution.py:818
  423.6 4.6 slice_add_fusion
  431.9 8.6 %shard_map.240 = (f32[192,1152]{1,0:T(8,128)}, f32[192,1152]{1,0:T(8,128)}, f32[192,1152]{1,0:T(8,128)}, f32[192,1152]{1,0:T(8,128)}) custom-call(s32[3]{0:T(128)} %get-tuple-element.622.side_ref, bf16[1536,256]{1,0:T(8,128)(2,1)} %get-tuple-element.533.refs_0_.refs_1_.refs_2_.refs_3_, bf16[1536,256]{1,0:T(8,128)(2,1)} %get-tuple-element.533.refs_0_.refs_1_.refs_2_.refs_3_, ...), custom_call_target="tpu_custom_call" | custom-call | flops 1769472 | bytes 7296 | tf_op jit(solution)/shard_map/pallas_call | solution.py:818
  443.4 21.6 %shard_map.241 = (bf16[1536,256]{1,0:T(8,128)(2,1)}, bf16[256,768]{1,0:T(8,128)(2,1)}, bf16[1024,1536]{1,0:T(8,128)(2,1)}, f32[8,1536]{1,0:T(8,128)}) custom-call(s32[1]{0:T(128)} %bitcast.2.level_ref, f32[264,1536]{1,0:T(8,128)} %pad.9.total_ref, f32[264,1536]{1,0:T(8,128)} %collective-permute-done.31.final_ref, ...), custom_call_target="tpu_custom_call", output_to_operand_aliasing={{2}: (24, {})} | custom-call | flops 6029312 | bytes 24576 | tf_op jit(solution)/shard_map/pallas_call | solution.py:707
  474.5 4.4 add_convert_fusion
  (240 shorter events, 124.4 us)
Async XLA Ops:
  7.2 177.4 %all-gather.3.cloned.1.call-start = ((), (), s32[]{:S(2)}) async-start(), calls=%async_computation.2 | async-start | bytes 15925248 | tf_op jit(solution)/shard_map/all_gather | solution.py:988
  14.0 21.5 %collective-permute-start.2 = (f32[192,768]{1,0:T(8,128)S(1)}, f32[192,768]{1,0:T(8,128)S(1)}, u32[]{:S(2)}, u32[]{:S(2)}) collective-permute-start(f32[192,768]{1,0:T(8,128)S(1)} %maximum_convert_fusion), channel_id=1, source_target_pairs={{0,1},{1,0},{2,3},{3,2},{4,5},{5,4},{6,7},{7,6},{8,9},{9,8},{10,11... | collective-permute-start | bytes 1769480 | tf_op jit(solution)/shard_map/ppermute | solution.py:109
  35.5 17.1 %collective-permute-start.3 = (f32[2,192,384]{2,1,0:T(8,128)S(1)}, f32[2,192,384]{2,1,0:T(8,128)S(1)}, u32[]{:S(2)}, u32[]{:S(2)}) collective-permute-start(f32[2,192,384]{2,1,0:T(8,128)S(1)} %collective-permute-done.1), channel_id=1, source_target_pairs={{1,0},{2,3},{5,4},{6,7},{9,8},{10,11},{13,12},{14,15},{17,16},{18,... | collective-permute-start | bytes 1769480 | tf_op jit(solution)/shard_map/ppermute | solution.py:109
  38.4 33.6 %collective-permute-start.4 = (f32[2,192,768]{2,1,0:T(8,128)S(1)}, f32[2,192,768]{2,1,0:T(8,128)}, u32[]{:S(2)}, u32[]{:S(2)}) collective-permute-start(f32[2,192,768]{2,1,0:T(8,128)S(1)} %pad_maximum_fusion.1), channel_id=1, source_target_pairs={{1,2},{2,1},{5,6},{6,5},{9,10},{10,9},{13,14},{14,13},{17,18},{18,... | collective-permute-start | bytes 3538952 | tf_op jit(solution)/shard_map/ppermute | solution.py:109
  53.7 23.6 %collective-permute-start.5 = (f32[528,384]{1,0:T(8,128)S(1)}, f32[528,384]{1,0:T(8,128)S(1)}, u32[]{:S(2)}, u32[]{:S(2)}) collective-permute-start(f32[528,384]{1,0:T(8,128)S(1)} %pad_maximum_fusion.5), channel_id=1, source_target_pairs={{0,1},{1,0},{2,3},{3,2},{4,5},{5,4},{6,7},{7,6},{8,9},{9,8},{10,11... | collective-permute-start | bytes 2433032 | tf_op jit(solution)/shard_map/ppermute | solution.py:109
  72.0 28.6 %collective-permute-start.11 = (f32[2,192,768]{2,1,0:T(8,128)}, f32[2,192,768]{2,1,0:T(8,128)}, u32[]{:S(2)}, u32[]{:S(2)}) collective-permute-start(f32[2,192,768]{2,1,0:T(8,128)} %collective-permute-done.4), channel_id=1, source_target_pairs={{1,0},{2,3},{5,4},{6,7},{9,8},{10,11},{13,12},{14,15},{17,16},{18,... | collective-permute-start | bytes 3538952 | tf_op jit(solution)/shard_map/ppermute | solution.py:109
  103.8 385.1 %reduce-scatter.2.cloned.1.call-start = ((), (), s32[]{:S(2)}) async-start(), calls=%async_computation.1 | async-start | bytes 21233664 | tf_op jit(solution)/shard_map/reduce_scatter | solution.py:1067
  107.1 32.0 %collective-permute-start.13 = (f32[264,768]{1,0:T(8,128)S(1)}, f32[264,768]{1,0:T(8,128)S(1)}, u32[]{:S(2)}, u32[]{:S(2)}) collective-permute-start(f32[264,768]{1,0:T(8,128)S(1)} %pad_maximum_fusion.7), channel_id=1, source_target_pairs={{1,2},{2,1},{5,6},{6,5},{9,10},{10,9},{13,14},{14,13},{17,18},{18,... | collective-permute-start | bytes 2433032 | tf_op jit(solution)/shard_map/ppermute | solution.py:109
  107.9 31.1 %collective-permute-start.14 = (f32[264,768]{1,0:T(8,128)}, f32[264,768]{1,0:T(8,128)S(1)}, u32[]{:S(2)}, u32[]{:S(2)}) collective-permute-start(f32[264,768]{1,0:T(8,128)} %collective-permute-done.8.across_ref.refs_15_), channel_id=1, source_target_pairs={{1,0},{2,3},{5,4},{6,7},{9,8},{10,11},{13,12},{14,15},{17,16},{18,... | collective-permute-start | bytes 2433032 | tf_op jit(solution)/shard_map/ppermute | solution.py:109
  109.2 29.8 %collective-permute-start.12 = (f32[264,384]{1,0:T(8,128)S(1)}, f32[264,384]{1,0:T(8,128)S(1)}, u32[]{:S(2)}, u32[]{:S(2)}) collective-permute-start(f32[264,384]{1,0:T(8,128)S(1)} %copy-done.5), channel_id=1, source_target_pairs={{0,1},{1,0},{2,3},{3,2},{4,5},{5,4},{6,7},{7,6},{8,9},{9,8},{10,11... | collective-permute-start | bytes 1216520 | tf_op jit(solution)/shard_map/ppermute | solution.py:109
  139.1 16.8 %collective-permute-start.16 = (f32[264,384]{1,0:T(8,128)S(1)}, f32[264,384]{1,0:T(8,128)S(1)}, u32[]{:S(2)}, u32[]{:S(2)}) collective-permute-start(f32[264,384]{1,0:T(8,128)S(1)} %copy-done.2), channel_id=1, source_target_pairs={{0,1},{1,0},{2,3},{3,2},{4,5},{5,4},{6,7},{7,6},{8,9},{9,8},{10,11... | collective-permute-start | bytes 1216520 | tf_op jit(solution)/shard_map/ppermute | solution.py:109
  139.2 24.1 %collective-permute-start.17 = (f32[264,768]{1,0:T(8,128)S(1)}, f32[264,768]{1,0:T(8,128)S(1)}, u32[]{:S(2)}, u32[]{:S(2)}) collective-permute-start(f32[264,768]{1,0:T(8,128)S(1)} %pad_maximum_fusion.8), channel_id=1, source_target_pairs={{1,2},{2,1},{5,6},{6,5},{9,10},{10,9},{13,14},{14,13},{17,18},{18,... | collective-permute-start | bytes 2433032 | tf_op jit(solution)/shard_map/ppermute | solution.py:109
  139.9 27.4 %collective-permute-start.18 = (f32[264,768]{1,0:T(8,128)S(1)}, f32[264,768]{1,0:T(8,128)S(1)}, u32[]{:S(2)}, u32[]{:S(2)}) collective-permute-start(f32[264,768]{1,0:T(8,128)S(1)} %collective-permute-done.13.across_ref.refs_15_), channel_id=1, source_target_pairs={{1,0},{2,3},{5,4},{6,7},{9,8},{10,11},{13,12},{14,15},{17,16},{18,... | collective-permute-start | bytes 2433032 | tf_op jit(solution)/shard_map/ppermute | solution.py:109
  155.9 41.6 %collective-permute-start.21 = (f32[264,1536]{1,0:T(8,128)}, f32[264,1536]{1,0:T(8,128)}, u32[]{:S(2)}, u32[]{:S(2)}) collective-permute-start(f32[264,1536]{1,0:T(8,128)} %get-tuple-element.401), channel_id=1, source_target_pairs={{0,1},{3,2},{4,5},{7,6},{8,9},{11,10},{12,13},{15,14},{16,17},{19,... | collective-permute-start | bytes 4866056 | tf_op jit(solution)/shard_map/ppermute | solution.py:109
  168.4 29.0 %collective-permute-start.19 = (f32[264,768]{1,0:T(8,128)}, f32[264,768]{1,0:T(8,128)S(1)}, u32[]{:S(2)}, u32[]{:S(2)}) collective-permute-start(f32[264,768]{1,0:T(8,128)} %pad_maximum_fusion.9), channel_id=1, source_target_pairs={{1,2},{2,1},{5,6},{6,5},{9,10},{10,9},{13,14},{14,13},{17,18},{18,... | collective-permute-start | bytes 2433032 | tf_op jit(solution)/shard_map/ppermute | solution.py:109
  169.1 28.3 %collective-permute-start.20 = (f32[264,768]{1,0:T(8,128)S(1)}, f32[264,768]{1,0:T(8,128)S(1)}, u32[]{:S(2)}, u32[]{:S(2)}) collective-permute-start(f32[264,768]{1,0:T(8,128)S(1)} %collective-permute-done.17.across_ref.refs_15_), channel_id=1, source_target_pairs={{1,0},{2,3},{5,4},{6,7},{9,8},{10,11},{13,12},{14,15},{17,16},{18,... | collective-permute-start | bytes 2433032 | tf_op jit(solution)/shard_map/ppermute | solution.py:109
  197.4 40.3 %collective-permute-start.23 = (f32[264,1536]{1,0:T(8,128)}, f32[264,1536]{1,0:T(8,128)}, u32[]{:S(2)}, u32[]{:S(2)}) collective-permute-start(f32[264,1536]{1,0:T(8,128)} %get-tuple-element.427), channel_id=1, source_target_pairs={{0,1},{3,2},{4,5},{7,6},{8,9},{11,10},{12,13},{15,14},{16,17},{19,... | collective-permute-start | bytes 4866056 | tf_op jit(solution)/shard_map/ppermute | solution.py:109
  204.6 33.1 %collective-permute-start.24 = (f32[256,1536]{1,0:T(8,128)S(1)}, f32[256,1536]{1,0:T(8,128)}, u32[]{:S(2)}, u32[]{:S(2)}) collective-permute-start(f32[256,1536]{1,0:T(8,128)S(1)} %slice_add_fusion.3), channel_id=1, source_target_pairs={{1,2},{2,1},{5,6},{6,5},{9,10},{10,9},{13,14},{14,13},{17,18},{18,... | collective-permute-start | bytes 4718600 | tf_op jit(solution)/shard_map/ppermute | solution.py:109
  206.5 31.2 %collective-permute-start.22 = (f32[264,768]{1,0:T(8,128)S(1)}, f32[264,768]{1,0:T(8,128)S(1)}, u32[]{:S(2)}, u32[]{:S(2)}) collective-permute-start(f32[264,768]{1,0:T(8,128)S(1)} %collective-permute-done.19.across_ref.refs_15_), channel_id=1, source_target_pairs={{1,0},{2,3},{5,4},{6,7},{9,8},{10,11},{13,12},{14,15},{17,16},{18,... | collective-permute-start | bytes 2433032 | tf_op jit(solution)/shard_map/ppermute | solution.py:109
  239.9 39.9 %collective-permute-start.25 = (f32[256,1536]{1,0:T(8,128)S(1)}, f32[256,1536]{1,0:T(8,128)}, u32[]{:S(2)}, u32[]{:S(2)}) collective-permute-start(f32[256,1536]{1,0:T(8,128)S(1)} %slice_select_fusion.total_ref), channel_id=1, source_target_pairs={{0,1},{1,0},{2,3},{3,2},{4,5},{5,4},{6,7},{7,6},{8,9},{9,8},{10,11... | collective-permute-start | bytes 4718600 | tf_op jit(solution)/shard_map/ppermute | solution.py:109
  244.7 35.1 %collective-permute-start.26 = (f32[256,1536]{1,0:T(8,128)S(1)}, f32[256,1536]{1,0:T(8,128)}, u32[]{:S(2)}, u32[]{:S(2)}) collective-permute-start(f32[256,1536]{1,0:T(8,128)S(1)} %slice_add_fusion.2), channel_id=1, source_target_pairs={{1,2},{2,1},{5,6},{6,5},{9,10},{10,9},{13,14},{14,13},{17,18},{18,... | collective-permute-start | bytes 4718600 | tf_op jit(solution)/shard_map/ppermute | solution.py:109
  284.4 44.8 %collective-permute-start.27 = (f32[256,1536]{1,0:T(8,128)}, f32[256,1536]{1,0:T(8,128)}, u32[]{:S(2)}, u32[]{:S(2)}) collective-permute-start(f32[256,1536]{1,0:T(8,128)} %add_select_fusion.1.total_ref), channel_id=1, source_target_pairs={{0,1},{1,0},{2,3},{3,2},{4,5},{5,4},{6,7},{7,6},{8,9},{9,8},{10,11... | collective-permute-start | bytes 4718600 | tf_op jit(solution)/shard_map/ppermute | solution.py:109
  289.0 40.2 %collective-permute-start.28 = (f32[256,1536]{1,0:T(8,128)}, f32[256,1536]{1,0:T(8,128)}, u32[]{:S(2)}, u32[]{:S(2)}) collective-permute-start(f32[256,1536]{1,0:T(8,128)} %slice_add_fusion.1), channel_id=1, source_target_pairs={{1,2},{2,1},{5,6},{6,5},{9,10},{10,9},{13,14},{14,13},{17,18},{18,... | collective-permute-start | bytes 4718600 | tf_op jit(solution)/shard_map/ppermute | solution.py:109
  333.3 37.3 %collective-permute-start.30 = (f32[256,1536]{1,0:T(8,128)}, f32[256,1536]{1,0:T(8,128)}, u32[]{:S(2)}, u32[]{:S(2)}) collective-permute-start(f32[256,1536]{1,0:T(8,128)} %select_select_fusion.1.total_ref), channel_id=1, source_target_pairs={{0,1},{1,0},{2,3},{3,2},{4,5},{5,4},{6,7},{7,6},{8,9},{9,8},{10,11... | collective-permute-start | bytes 4718600 | tf_op jit(solution)/shard_map/ppermute | solution.py:109
  336.7 34.0 %collective-permute-start.29 = (f32[256,1536]{1,0:T(8,128)S(1)}, f32[256,1536]{1,0:T(8,128)}, u32[]{:S(2)}, u32[]{:S(2)}) collective-permute-start(f32[256,1536]{1,0:T(8,128)S(1)} %slice_add_fusion.4), channel_id=1, source_target_pairs={{1,2},{2,1},{5,6},{6,5},{9,10},{10,9},{13,14},{14,13},{17,18},{18,... | collective-permute-start | bytes 4718600 | tf_op jit(solution)/shard_map/ppermute | solution.py:109
  374.1 34.1 %collective-permute-start.31 = (f32[264,1536]{1,0:T(8,128)}, f32[264,1536]{1,0:T(8,128)}, u32[]{:S(2)}, u32[]{:S(2)}) collective-permute-start(f32[264,1536]{1,0:T(8,128)} %pad.9.total_ref), channel_id=1, source_target_pairs={{0,1},{1,0},{2,3},{3,2},{4,5},{5,4},{6,7},{7,6},{8,9},{9,8},{10,11... | collective-permute-start | bytes 4866056 | tf_op jit(solution)/shard_map/ppermute | solution.py:109
  379.0 36.7 %collective-permute-start.32 = (f32[256,1536]{1,0:T(8,128)}, f32[256,1536]{1,0:T(8,128)}, u32[]{:S(2)}, u32[]{:S(2)}) collective-permute-start(f32[256,1536]{1,0:T(8,128)} %select_add_fusion), channel_id=1, source_target_pairs={{1,2},{2,1},{5,6},{6,5},{9,10},{10,9},{13,14},{14,13},{17,18},{18,... | collective-permute-start | bytes 4718600 | tf_op jit(solution)/shard_map/ppermute | solution.py:109
  428.2 42.7 %collective-permute-start.37 = (f32[256,1536]{1,0:T(8,128)}, f32[256,1536]{1,0:T(8,128)}, u32[]{:S(2)}, u32[]{:S(2)}) collective-permute-start(f32[256,1536]{1,0:T(8,128)} %get-tuple-element.594), channel_id=1, source_target_pairs={{0,1},{1,0},{2,3},{3,2},{4,5},{5,4},{6,7},{7,6},{8,9},{9,8},{10,11... | collective-permute-start | bytes 4718600 | tf_op jit(solution)/shard_map/ppermute | solution.py:109
  429.9 41.1 %collective-permute-start.38 = (f32[256,1536]{1,0:T(8,128)}, f32[256,1536]{1,0:T(8,128)}, u32[]{:S(2)}, u32[]{:S(2)}) collective-permute-start(f32[256,1536]{1,0:T(8,128)} %get-tuple-element.593), channel_id=1, source_target_pairs={{1,2},{2,1},{5,6},{6,5},{9,10},{10,9},{13,14},{14,13},{17,18},{18,... | collective-permute-start | bytes 4718600 | tf_op jit(solution)/shard_map/ppermute | solution.py:109
  440.5 24.4 %collective-permute-start.34 = (f32[192,1152]{1,0:T(8,128)}, f32[192,1152]{1,0:T(8,128)}, u32[]{:S(2)}, u32[]{:S(2)}) collective-permute-start(f32[192,1152]{1,0:T(8,128)} %get-tuple-element.562), channel_id=1, source_target_pairs={{0,8},{8,0},{16,24},{24,16},{1,9},{9,1},{17,25},{25,17},{2,10},{10... | collective-permute-start | bytes 2654216 | tf_op jit(solution)/shard_map/ppermute | solution.py:945
  442.2 22.8 %collective-permute-start.35 = (f32[192,1152]{1,0:T(8,128)}, f32[192,1152]{1,0:T(8,128)}, u32[]{:S(2)}, u32[]{:S(2)}) collective-permute-start(f32[192,1152]{1,0:T(8,128)} %get-tuple-element.564), channel_id=1, source_target_pairs={{0,16},{8,24},{16,0},{24,8},{1,17},{9,25},{17,1},{25,9},{2,18},{10... | collective-permute-start | bytes 2654216 | tf_op jit(solution)/shard_map/ppermute | solution.py:945
  467.7 17.7 %collective-permute-start.43 = (f32[96,1152]{1,0:T(8,128)S(1)}, f32[96,1152]{1,0:T(8,128)S(1)}, u32[]{:S(2)}, u32[]{:S(2)}) collective-permute-start(f32[96,1152]{1,0:T(8,128)S(1)} %slice.180), channel_id=1, source_target_pairs={{0,8},{8,0},{16,24},{24,16},{1,9},{9,1},{17,25},{25,17},{2,10},{10... | collective-permute-start | bytes 1327112 | tf_op jit(solution)/shard_map/ppermute | solution.py:945
  (54 other events, 696.6 us)
Sparse Core Ops, SparseCore 0:
  103.9 78.1 all-gather.2
  280.0 125.8 reduce-scatter.1
where the time goes:
time: 504 us; the launch traced here: 499 us
  Pallas kernels  293 us (58%)
  starting transfers between devices  77.2 us (15%)
  other arithmetic  56.7 us (11%)
  waiting for transfers between devices  41.2 us (8%)
  between operations  16 us (3%)
  local copies, waits for them, and re-layouts  15.2 us (3%)
    pallas_call x5, Pallas kernels, backward_chunk(): pl.pallas_call(functools.partial(backward_kernel, start, full, acc is not...  124 us
    ppermute x30, starting transfers between devices, along(): return lax.ppermute(part, 'tp', pairs)  61 us
    pallas_call x4, Pallas kernels, forward_chunk(): pl.pallas_call(forward_kernel, out_shape=outs, grid=(steps,), in_specs=[S...  55.9 us
    pallas_call x3, Pallas kernels, rows_of(): pl.pallas_call(functools.partial(rows_kernel, counts, plan, recv is not N...  35.7 us
    ppermute x30, waiting for transfers between devices, along(): return lax.ppermute(part, 'tp', pairs)  34.5 us
    pallas_call x4, Pallas kernels, attend(): pl.pallas_call(functools.partial(attend_kernel, index * rows), out_shape=...  21 us
    pallas_call x1, Pallas kernels, project(): pl.pallas_call(project_kernel, out_shape=jax.ShapeDtypeStruct((rows, widt...  15.9 us
    ppermute x11, starting transfers between devices, to_chip(): return lax.ppermute(array, 'chip', [(i, i ^ m) for i in range(chips)])  15.5 us
  transfers between devices with their start and end apart: 46, of which 10 were waited for; matrix products, arithmetic and copies ran while one was open for 12% of the time, Pallas kernels for 59%

commit v1 on v0

--- a/solution.py
+++ b/solution.py
@@ -834,6 +834,45 @@
     return results[0] if len(picked) == 1 else results
 
 
+def finish_kernel(*refs):
+    query_ref, key_ref, value_ref, out_ref = refs[4:]
+    kv_here = key_ref.shape[1] // HD
+    q_cols = out_ref.shape[1]
+    for at in range(2):
+        kept_ref, far_ref = refs[2 * at : 2 * at + 2]
+        half = far_ref.shape[0]
+        sums = kept_ref[...] + far_ref[...]
+        here = slice(at * half, (at + 1) * half)
+        out_ref[here, :] = sums[:, :q_cols]
+        start = q_cols
+        cut = [[], [], []]
+        for kv in range(kv_here):
+            for i, width in enumerate((GROUP * HD, HD, HD)):
+                cut[i].append(sums[:, start : start + width])
+                start += width
+        for ref, pieces in zip((query_ref, key_ref, value_ref), cut):
+            ref[here, :] = jnp.concatenate(pieces, 1)
+
+
+def finish(one, far_one, two, far_two, kv_here):
+    half, columns = far_one.shape
+    first = pl.BlockSpec((half, columns), lambda i: (0, 0))
+    q_cols = kv_here * GROUP * HD
+    outs = [
+        jax.ShapeDtypeStruct((2 * half, width), jnp.float32)
+        for width in (q_cols, kv_here * HD, kv_here * HD, q_cols)
+    ]
+    return pl.pallas_call(
+        finish_kernel,
+        out_shape=outs,
+        grid=(1,),
+        in_specs=[first] * 4,
+        out_specs=[whole(out) for out in outs],
+        compiler_params=params(),
+        cost_estimate=cost(4 * half * columns, 32 * half * columns),
+    )(one, far_one, two, far_two)
+
+
 def shards(
     tokens,
     lengths,
@@ -1162,19 +1201,6 @@
     gain_sums = gains[0] + gains[1] + gains[2] + gains[3]
     gain_sums = gain_sums + swap(gain_sums)
     gain_sums, last, near_in = fence(gain_sums, last, near_in)
-    if by_hand:
-        others = [to_chip(gain_sums, m) for m in range(1, chips)]
-        gain_sums = sum(others, gain_sums)
-        one = pieces[0] + pieces[1]
-        two = pieces[2] + pieces[3]
-        one = one[:half] + to_chip(one[half:], 2)
-        two = two[:half] + to_chip(two[half:], 1)
-        attn = jnp.concatenate([one, two], 0)
-    else:
-        gain_sums = lax.psum(gain_sums, "chip")
-        attn = pieces
-    gain_rows = lax.dynamic_slice_in_dim(gain_sums, at_row, slice_rows, 1)
-    grad_out, grad_qkv = attn[:, :q_cols], attn[:, q_cols:]
     mlp_rows = jnp.where(inner, near() + near_in, edge()) + last
     hidden_rows = jnp.where(
         low,
@@ -1182,22 +1208,44 @@
         jnp.where(level == 2, hidden[2], hidden[3]),
     )
     layer_out = (hidden_rows + mlp_rows).astype(jnp.bfloat16)
-    one = strip_one.shape[1]
-    picked = lambda at, width: jnp.concatenate(
-        [grad_qkv[:, kv * one + at : kv * one + at + width] for kv in range(kv_here)], 1
-    )
+    mlp_grads = [grad_mlp[:, at * units : (at + 1) * units] for at in range(3)]
+    if by_hand:
+        one = pieces[0] + pieces[1]
+        two = pieces[2] + pieces[3]
+        far_one = to_chip(one[half:], 2)
+        far_two = to_chip(two[half:], 1)
+        others = [to_chip(gain_sums, m) for m in range(1, chips)]
+        far_one, far_two, mlp_grads, layer_out = fence(far_one, far_two, mlp_grads, layer_out)
+        attn_grads = finish(one, far_one, two, far_two, kv_here)
+        others, attn_grads = fence(others, attn_grads)
+        gain_sums = sum(others, gain_sums)
+    else:
+        gain_sums = lax.psum(gain_sums, "chip")
+        grad_qkv = pieces[:, q_cols:]
+        one = strip_one.shape[1]
+        picked = lambda at, width: jnp.concatenate(
+            [grad_qkv[:, kv * one + at : kv * one + at + width] for kv in range(kv_here)], 1
+        )
+        attn_grads = (
+            picked(0, GROUP * HD),
+            picked(GROUP * HD, HD),
+            picked((GROUP + 1) * HD, HD),
+            pieces[:, :q_cols],
+        )
+    gain_rows = lax.dynamic_slice_in_dim(gain_sums, at_row, slice_rows, 1)
+    grad_query, grad_key, grad_value, grad_out_t = attn_grads
     return (
         layer_out,
         input_grad,
         gain_rows[0],
-        picked(0, GROUP * HD),
-        picked(GROUP * HD, HD),
-        picked((GROUP + 1) * HD, HD),
-        grad_out.T,
+        grad_query,
+        grad_key,
+        grad_value,
+        grad_out_t.T,
         gain_rows[1],
-        grad_mlp[:, :units],
-        grad_mlp[:, units : 2 * units],
-        grad_mlp[:, 2 * units :].T,
+        mlp_grads[0],
+        mlp_grads[1],
+        mlp_grads[2].T,
     )
 
 

time: 504 us -> 502 us (level)
  transfers between devices with their start and end apart: 46 -> 46, of which waited for: 10 -> 9; matrix products, arithmetic and copies ran while one was open for 12% -> 12% of each run, Pallas kernels for 59% -> 59%
where the time goes in v1:
time: 502 us; the launch traced here: 497 us
  Pallas kernels  296 us (59%)
  starting transfers between devices  76.8 us (15%)
  other arithmetic  53.5 us (11%)
  waiting for transfers between devices  38 us (8%)
  local copies, waits for them, and re-layouts  17 us (3%)
  between operations  16 us (3%)
    pallas_call x5, Pallas kernels, backward_chunk(): pl.pallas_call(functools.partial(backward_kernel, start, full, acc is not...  124 us
    ppermute x30, starting transfers between devices, along(): return lax.ppermute(part, 'tp', pairs)  60.9 us
    pallas_call x4, Pallas kernels, forward_chunk(): pl.pallas_call(forward_kernel, out_shape=outs, grid=(steps,), in_specs=[S...  56 us
    pallas_call x3, Pallas kernels, rows_of(): pl.pallas_call(functools.partial(rows_kernel, counts, plan, recv is not N...  35.8 us
    ppermute x30, waiting for transfers between devices, along(): return lax.ppermute(part, 'tp', pairs)  34.7 us
    pallas_call x4, Pallas kernels, attend(): pl.pallas_call(functools.partial(attend_kernel, index * rows), out_shape=...  20.9 us
    pallas_call x1, Pallas kernels, project(): pl.pallas_call(project_kernel, out_shape=jax.ShapeDtypeStruct((rows, widt...  15.9 us
    ppermute x11, starting transfers between devices, to_chip(): return lax.ppermute(array, 'chip', [(i, i ^ m) for i in range(chips)])  15.2 us
  transfers between devices with their start and end apart: 46, of which 9 were waited for; matrix products, arithmetic and copies ran while one was open for 12% of the time, Pallas kernels for 59%

profile of v1, /device:TPU:0, one launch (start us, length us, event | category | flops | bytes accessed | tf_op | source)
XLA Modules:
  0.0 496.8 jit_solution(16204967883676381045)
XLA Ops:
  17.3 4.5 collective-permute-done
  25.1 10.4 %shard_map.221 = (bf16[1024,4096]{1,0:T(8,128)(2,1)}, bf16[1024,1536]{1,0:T(8,128)(2,1)}, bf16[1536,4096]{1,0:T(8,128)(2,1)}) custom-call(bf16[1024,1536]{1,0:T(8,128)(2,1)} %refs_12_.7, f32[1,1536]{1,0:T(1,128)} %broadcast_in_dim.10.gain_ref.refs_13_, bf16[1536,384]{1,0:T(8,128)(2,1)} %q_ref.1, bf16[192,1536]{1,0:T(8,128)(2,1)} %bitcast.32, ...), custom_call_target="tpu_custom_call" | custom-call | flops 3145728 | bytes 18432 | tf_op jit(solution)/shard_map/pallas_call | solution.py:229
  40.3 5.6 %shard_map.222.part_ref.refs_7_.refs_22_ = f32[264,384]{1,0:T(8,128)} custom-call(s32[1]{0:T(128)S(6)} %copy.46.length_ref, bf16[1024,4096]{1,0:T(8,128)(2,1)} %get-tuple-element.327.q_ref.kv_ref._, bf16[1024,4096]{1,0:T(8,128)(2,1)} %get-tuple-element.327.q_ref.kv_ref._, bf16[512,384]{1,0:T(8,128)(2,1)} %fusion.2.strip_ref), custom_call_target="tpu_custom_call" | custom-call | flops 393216 | bytes 2048 | tf_op jit(solution)/shard_map/pallas_call | solution.py:336
  45.9 6.6 %shard_map.223.part_ref.refs_7_.refs_23_ = f32[264,384]{1,0:T(8,128)} custom-call(s32[1]{0:T(128)S(6)} %copy.46.length_ref, bf16[1024,4096]{1,0:T(8,128)(2,1)} %get-tuple-element.327.q_ref.kv_ref._, bf16[1024,4096]{1,0:T(8,128)(2,1)} %get-tuple-element.327.q_ref.kv_ref._, bf16[512,384]{1,0:T(8,128)(2,1)} %fusion.2.strip_ref), custom_call_target="tpu_custom_call" | custom-call | flops 524288 | bytes 2560 | tf_op jit(solution)/shard_map/pallas_call | solution.py:336
  53.7 6.0 %collective-permute-start.5 = (f32[528,384]{1,0:T(8,128)S(1)}, f32[528,384]{1,0:T(8,128)S(1)}, u32[]{:S(2)}, u32[]{:S(2)}) collective-permute-start(f32[528,384]{1,0:T(8,128)S(1)} %pad_maximum_fusion.5), channel_id=1, source_target_pairs={{0,1},{1,0},{2,3},{3,2},{4,5},{5,4},{6,7},{7,6},{8,9},{9,8},{10,11... | collective-permute-start | bytes 2433032 | tf_op jit(solution)/shard_map/ppermute | solution.py:109
  63.1 4.0 shard_map.224.part_ref.refs_7_.refs_20_
  67.0 4.8 shard_map.225.part_ref.refs_7_.refs_21_
  73.4 3.9 collective-permute-done.5
  84.4 7.0 %shard_map.226 = (bf16[1024,1536]{1,0:T(8,128)(2,1)}, bf16[1536,1024]{1,0:T(8,128)(2,1)}, bf16[1536,1024]{1,0:T(8,128)(2,1)}) custom-call(s32[1]{0:T(128)S(6)} %copy.46.length_ref, bf16[1024,1536]{1,0:T(8,128)(2,1)} %cot_ref.1, bf16[1024,1536]{1,0:T(8,128)(2,1)} %get-tuple-element.339.normed_ref.x_ref), custom_call_target="tpu_custom_call" | custom-call | flops 1536 | bytes 15360 | tf_op jit(solution)/shard_map/pallas_call | solution.py:262
  94.7 5.9 %collective-permute-done.11 = f32[2,192,768]{2,1,0:T(8,128)} collective-permute-done((f32[2,192,768]{2,1,0:T(8,128)}, f32[2,192,768]{2,1,0:T(8,128)}, u32[]{:S(2)}, u32[]{:S(2)}) %collective-permute-start.11) | collective-permute-done | bytes 1179680 | tf_op jit(solution)/shard_map/ppermute | solution.py:109
  113.5 10.1 %shard_map.227 = (bf16[1536,2048]{1,0:T(8,128)(2,1)}, bf16[1536,1536]{1,0:T(8,128)(2,1)}) custom-call(s32[2]{0:T(128)} %pad_add_fusion.4.meta_ref, bf16[1536,384]{1,0:T(8,128)(2,1)} %bitcast.25, bf16[384,512]{1,0:T(8,128)(2,1)} %fusion.3.p_ref.refs_8_, f32[4,3,192,384]{3,2,1,0:T(8,128)} %copy-done.6, f32[4,3,192,384]{3,2,1,0:T(8,128)} %collective-permute-done.15.theirs_ref), custom_call_target="tpu_custom_call" | custom-call | flops 2359296 | bytes 17664 | tf_op jit(solution)/shard_map/pallas_call | solution.py:179
  123.5 15.5 %collective-permute-done.12.other_ref.refs_14_ = f32[264,384]{1,0:T(8,128)S(1)} collective-permute-done((f32[264,384]{1,0:T(8,128)S(1)}, f32[264,384]{1,0:T(8,128)S(1)}, u32[]{:S(2)}, u32[]{:S(2)}) %collective-permute-start.12) | collective-permute-done | bytes 405536 | tf_op jit(solution)/shard_map/ppermute | solution.py:109
  141.8 14.0 %shard_map.228 = (f32[256,1536]{1,0:T(8,128)}, bf16[1536,256]{1,0:T(8,128)(2,1)}, bf16[256,1024]{1,0:T(8,128)(2,1)}, bf16[256,1024]{1,0:T(8,128)(2,1)}, bf16[256...) custom-call(s32[1]{0:T(128)} %bitcast.2.level_ref, f32[264,384]{1,0:T(8,128)} %shard_map.223.part_ref.refs_7_.refs_23_, ...), custom_call_target="tpu_custom_call" | custom-call | flops 5898240 | bytes 22272 | tf_op jit(solution)/shard_map/pallas_call | solution.py:427
  155.9 7.4 %collective-permute-start.21 = (f32[264,1536]{1,0:T(8,128)}, f32[264,1536]{1,0:T(8,128)}, u32[]{:S(2)}, u32[]{:S(2)}) collective-permute-start(f32[264,1536]{1,0:T(8,128)} %get-tuple-element.418), channel_id=1, source_target_pairs={{0,1},{3,2},{4,5},{7,6},{8,9},{11,10},{12,13},{15,14},{16,17},{19,... | collective-permute-start | bytes 4866056 | tf_op jit(solution)/shard_map/ppermute | solution.py:109
  163.3 4.1 collective-permute-done.18.outer_ref.refs_16_
  170.4 14.1 %shard_map.229 = (f32[256,1536]{1,0:T(8,128)}, bf16[1536,256]{1,0:T(8,128)(2,1)}, bf16[256,1024]{1,0:T(8,128)(2,1)}, bf16[256,1024]{1,0:T(8,128)(2,1)}, bf16[256...) custom-call(s32[1]{0:T(128)} %bitcast.2.level_ref, f32[264,384]{1,0:T(8,128)} %shard_map.222.part_ref.refs_7_.refs_22_, ...), custom_call_target="tpu_custom_call" | custom-call | flops 5898240 | bytes 22272 | tf_op jit(solution)/shard_map/pallas_call | solution.py:427
  184.6 12.7 %shard_map.230.w_ref.refs_17_ = bf16[1536,4096]{1,0:T(8,128)(2,1)} custom-call(bf16[384,512]{1,0:T(8,128)(2,1)} %fusion.pq_ref, bf16[384,512]{1,0:T(8,128)(2,1)} %fusion.1.pkv_ref, f32[8,3,192,768]{3,2,1,0:T(8,128)} %bitcast.24, bf16[1536,4096]{1,0:T(8,128)(2,1)} %get-tuple-element.400._), custom_call_target="tpu_custom_call", output_to_operand_aliasing={{}: (3, {})} | custom-call | flops 4718592 | bytes 30720 | tf_op jit(solution)/shard_map/pallas_call | solution.py:157
  197.3 5.6 %collective-permute-start.23 = (f32[264,1536]{1,0:T(8,128)}, f32[264,1536]{1,0:T(8,128)}, u32[]{:S(2)}, u32[]{:S(2)}) collective-permute-start(f32[264,1536]{1,0:T(8,128)} %get-tuple-element.444), channel_id=1, source_target_pairs={{0,1},{3,2},{4,5},{7,6},{8,9},{11,10},{12,13},{15,14},{16,17},{19,... | collective-permute-start | bytes 4866056 | tf_op jit(solution)/shard_map/ppermute | solution.py:109
  207.8 14.0 %shard_map.231 = (f32[256,1536]{1,0:T(8,128)}, bf16[1536,256]{1,0:T(8,128)(2,1)}, bf16[256,1024]{1,0:T(8,128)(2,1)}, bf16[256,1024]{1,0:T(8,128)(2,1)}, bf16[256...) custom-call(s32[1]{0:T(128)} %bitcast.2.level_ref, f32[264,384]{1,0:T(8,128)} %shard_map.225.part_ref.refs_7_.refs_21_, ...), custom_call_target="tpu_custom_call" | custom-call | flops 5898240 | bytes 22272 | tf_op jit(solution)/shard_map/pallas_call | solution.py:427
  221.8 15.9 %shard_map.232.refs_2_.refs_3_.refs_4_.refs_5_.refs_6_ = bf16[1024,4096]{1,0:T(8,128)(2,1)} custom-call(bf16[1024,1536]{1,0:T(8,128)(2,1)} %get-tuple-element.339.normed_ref.x_ref, bf16[1536,4096]{1,0:T(8,128)(2,1)} %shard_map.230.w_ref.refs_17_, f32[1024,128]{1,0:T(8,128)} %get-tuple-element.320.cos_ref.refs_10_, ...), custom_call_target="tpu_custom_call", output_to_operand_aliasing={{}: (4, {})} | custom-call | flops 12582912 | bytes 23552 | tf_op jit(solution)/shard_map/pallas_call | solution.py:282
  246.5 13.9 %shard_map.233 = (f32[256,1536]{1,0:T(8,128)}, bf16[1536,256]{1,0:T(8,128)(2,1)}, bf16[256,1024]{1,0:T(8,128)(2,1)}, bf16[256,1024]{1,0:T(8,128)(2,1)}, bf16[256...) custom-call(s32[1]{0:T(128)} %bitcast.2.level_ref, f32[264,384]{1,0:T(8,128)} %shard_map.224.part_ref.refs_7_.refs_20_, ...), custom_call_target="tpu_custom_call" | custom-call | flops 5898240 | bytes 22272 | tf_op jit(solution)/shard_map/pallas_call | solution.py:427
  260.5 19.3 %shard_map.234 = f32[1536,3072]{1,0:T(8,128)} custom-call(s32[3]{0:T(128)} %constant.159.clone.side_ref, bf16[1536,256]{1,0:T(8,128)(2,1)} %get-tuple-element.452.refs_0_.refs_1_.refs_2_.refs_3_, bf16[1536,256]{1,0:T(8,128)(2,1)} %get-tuple-element.452.refs_0_.refs_1_.refs_2_.refs_3_, bf16[1536,256]{1,0:T(8,128)(2,1)} %get-tuple-element.452.refs_0_.refs_1_.refs_2_.refs_3_, ...), custom_call_target="tpu_custom_call" | custom-call | flops 9437184 | bytes 27648 | tf_op jit(solution)/shard_map/pallas_call | solution.py:818
  292.0 37.2 %shard_map.235 = (bf16[1536,256]{1,0:T(8,128)(2,1)}, bf16[256,768]{1,0:T(8,128)(2,1)}, bf16[1024,1536]{1,0:T(8,128)(2,1)}, f32[8,1536]{1,0:T(8,128)}, f32[768,2048]{1,0:T(8,128)}) custom-call(s32[1]{0:T(128)} %bitcast.2.level_ref, f32[256,1536]{1,0:T(8,128)} %copy-done.17, f32[256,1536]{1,0:T(8,128)} %collective-permute-done.25.final_ref, ...), custom_call_target="tpu_custom_call" | custom-call | flops 9961472 | bytes 24576 | tf_op jit(solution)/shard_map/pallas_call | solution.py:707
  329.3 4.1 select_select_fusion.1.total_ref
  339.0 31.7 %shard_map.236 = (bf16[1536,256]{1,0:T(8,128)(2,1)}, bf16[256,768]{1,0:T(8,128)(2,1)}, bf16[1024,1536]{1,0:T(8,128)(2,1)}, f32[8,1536]{1,0:T(8,128)}, f32[512,2048]{1,0:T(8,128)}) custom-call(s32[1]{0:T(128)} %bitcast.2.level_ref, f32[256,1536]{1,0:T(8,128)} %add_select_fusion.1.total_ref, ...), custom_call_target="tpu_custom_call", output_to_operand_aliasing={{2}: (24, {})} | custom-call | flops 8650752 | bytes 24576 | tf_op jit(solution)/shard_map/pallas_call | solution.py:707
  381.8 26.0 %shard_map.237 = (bf16[1536,256]{1,0:T(8,128)(2,1)}, bf16[256,768]{1,0:T(8,128)(2,1)}, bf16[1024,1536]{1,0:T(8,128)(2,1)}, f32[8,1536]{1,0:T(8,128)}, f32[256,2048]{1,0:T(8,128)}) custom-call(s32[1]{0:T(128)} %bitcast.2.level_ref, f32[256,1536]{1,0:T(8,128)} %select_select_fusion.1.total_ref, ...), custom_call_target="tpu_custom_call", output_to_operand_aliasing={{2}: (24, {})} | custom-call | flops 7340032 | bytes 24576 | tf_op jit(solution)/shard_map/pallas_call | solution.py:707
  408.4 7.6 %shard_map.238 = (bf16[1536,256]{1,0:T(8,128)(2,1)}, bf16[256,768]{1,0:T(8,128)(2,1)}) custom-call(s32[1]{0:T(128)} %bitcast.2.level_ref, f32[264,1536]{1,0:T(8,128)} %pad.9.total_ref, f32[264,1536]{1,0:T(8,128)} %collective-permute-done.31.final_ref, f32[256,1536]{1,0:T(8,128)} %get-tuple-element.578.hidden_ref, ...), custom_call_target="tpu_custom_call" | custom-call | flops 6029312 | bytes 24576 | tf_op jit(solution)/shard_map/pallas_call | solution.py:707
  416.0 7.8 %shard_map.239 = f32[768,1152]{1,0:T(8,128)} custom-call(s32[3]{0:T(128)} %get-tuple-element.651.side_ref, bf16[1536,256]{1,0:T(8,128)(2,1)} %get-tuple-element.550.refs_0_.refs_1_.refs_2_.refs_3_, bf16[1536,256]{1,0:T(8,128)(2,1)} %get-tuple-element.550.refs_0_.refs_1_.refs_2_.refs_3_, bf16[1536,256]{1,0:T(8,128)(2,1)} %get-tuple-element.550.refs_0_.refs_1_.refs_2_.refs_3_, ...), custom_call_target="tpu_custom_call" | custom-call | flops 1769472 | bytes 7296 | tf_op jit(solution)/shard_map/pallas_call | solution.py:818
  423.9 4.6 slice_add_fusion
  432.1 8.6 %shard_map.240 = (f32[192,1152]{1,0:T(8,128)}, f32[192,1152]{1,0:T(8,128)}, f32[192,1152]{1,0:T(8,128)}, f32[192,1152]{1,0:T(8,128)}) custom-call(s32[3]{0:T(128)} %get-tuple-element.650.side_ref, bf16[1536,256]{1,0:T(8,128)(2,1)} %get-tuple-element.550.refs_0_.refs_1_.refs_2_.refs_3_, bf16[1536,256]{1,0:T(8,128)(2,1)} %get-tuple-element.550.refs_0_.refs_1_.refs_2_.refs_3_, ...), custom_call_target="tpu_custom_call" | custom-call | flops 1769472 | bytes 7296 | tf_op jit(solution)/shard_map/pallas_call | solution.py:818
  443.6 21.7 %shard_map.241 = (bf16[1536,256]{1,0:T(8,128)(2,1)}, bf16[256,768]{1,0:T(8,128)(2,1)}, bf16[1024,1536]{1,0:T(8,128)(2,1)}, f32[8,1536]{1,0:T(8,128)}) custom-call(s32[1]{0:T(128)} %bitcast.2.level_ref, f32[264,1536]{1,0:T(8,128)} %pad.9.total_ref, f32[264,1536]{1,0:T(8,128)} %collective-permute-done.31.final_ref, ...), custom_call_target="tpu_custom_call", output_to_operand_aliasing={{2}: (24, {})} | custom-call | flops 6029312 | bytes 24576 | tf_op jit(solution)/shard_map/pallas_call | solution.py:707
  476.6 4.4 add_convert_fusion
  (237 shorter events, 121.9 us)
Async XLA Ops:
  7.2 177.4 %all-gather.3.cloned.1.call-start = ((), (), s32[]{:S(2)}) async-start(), calls=%async_computation.2 | async-start | bytes 15925248 | tf_op jit(solution)/shard_map/all_gather | solution.py:1027
  14.0 21.5 %collective-permute-start.2 = (f32[192,768]{1,0:T(8,128)S(1)}, f32[192,768]{1,0:T(8,128)S(1)}, u32[]{:S(2)}, u32[]{:S(2)}) collective-permute-start(f32[192,768]{1,0:T(8,128)S(1)} %maximum_convert_fusion), channel_id=1, source_target_pairs={{0,1},{1,0},{2,3},{3,2},{4,5},{5,4},{6,7},{7,6},{8,9},{9,8},{10,11... | collective-permute-start | bytes 1769480 | tf_op jit(solution)/shard_map/ppermute | solution.py:109
  35.5 17.1 %collective-permute-start.3 = (f32[2,192,384]{2,1,0:T(8,128)S(1)}, f32[2,192,384]{2,1,0:T(8,128)S(1)}, u32[]{:S(2)}, u32[]{:S(2)}) collective-permute-start(f32[2,192,384]{2,1,0:T(8,128)S(1)} %collective-permute-done.1), channel_id=1, source_target_pairs={{1,0},{2,3},{5,4},{6,7},{9,8},{10,11},{13,12},{14,15},{17,16},{18,... | collective-permute-start | bytes 1769480 | tf_op jit(solution)/shard_map/ppermute | solution.py:109
  38.4 33.5 %collective-permute-start.4 = (f32[2,192,768]{2,1,0:T(8,128)S(1)}, f32[2,192,768]{2,1,0:T(8,128)}, u32[]{:S(2)}, u32[]{:S(2)}) collective-permute-start(f32[2,192,768]{2,1,0:T(8,128)S(1)} %pad_maximum_fusion.1), channel_id=1, source_target_pairs={{1,2},{2,1},{5,6},{6,5},{9,10},{10,9},{13,14},{14,13},{17,18},{18,... | collective-permute-start | bytes 3538952 | tf_op jit(solution)/shard_map/ppermute | solution.py:109
  53.7 23.5 %collective-permute-start.5 = (f32[528,384]{1,0:T(8,128)S(1)}, f32[528,384]{1,0:T(8,128)S(1)}, u32[]{:S(2)}, u32[]{:S(2)}) collective-permute-start(f32[528,384]{1,0:T(8,128)S(1)} %pad_maximum_fusion.5), channel_id=1, source_target_pairs={{0,1},{1,0},{2,3},{3,2},{4,5},{5,4},{6,7},{7,6},{8,9},{9,8},{10,11... | collective-permute-start | bytes 2433032 | tf_op jit(solution)/shard_map/ppermute | solution.py:109
  72.0 28.6 %collective-permute-start.11 = (f32[2,192,768]{2,1,0:T(8,128)}, f32[2,192,768]{2,1,0:T(8,128)}, u32[]{:S(2)}, u32[]{:S(2)}) collective-permute-start(f32[2,192,768]{2,1,0:T(8,128)} %collective-permute-done.4), channel_id=1, source_target_pairs={{1,0},{2,3},{5,4},{6,7},{9,8},{10,11},{13,12},{14,15},{17,16},{18,... | collective-permute-start | bytes 3538952 | tf_op jit(solution)/shard_map/ppermute | solution.py:109
  77.3 16.6 %collective-permute-start.10 = (f32[2,3,96,384]{3,2,1,0:T(8,128)S(1)}, f32[2,3,96,384]{3,2,1,0:T(8,128)}, u32[]{:S(2)}, u32[]{:S(2)}) collective-permute-start(f32[2,3,96,384]{3,2,1,0:T(8,128)S(1)} %pad_maximum_fusion.4), channel_id=1, source_target_pairs={{0,8},{8,0},{16,24},{24,16},{1,9},{9,1},{17,25},{25,17},{2,10},{10... | collective-permute-start | bytes 2654216 | tf_op jit(solution)/shard_map/ppermute | solution.py:984
  103.7 377.3 %reduce-scatter.2.cloned.1.call-start = ((), (), s32[]{:S(2)}) async-start(), calls=%async_computation.1 | async-start | bytes 21233664 | tf_op jit(solution)/shard_map/reduce_scatter | solution.py:1106
  107.1 32.0 %collective-permute-start.13 = (f32[264,768]{1,0:T(8,128)S(1)}, f32[264,768]{1,0:T(8,128)S(1)}, u32[]{:S(2)}, u32[]{:S(2)}) collective-permute-start(f32[264,768]{1,0:T(8,128)S(1)} %pad_maximum_fusion.7), channel_id=1, source_target_pairs={{1,2},{2,1},{5,6},{6,5},{9,10},{10,9},{13,14},{14,13},{17,18},{18,... | collective-permute-start | bytes 2433032 | tf_op jit(solution)/shard_map/ppermute | solution.py:109
  107.9 31.1 %collective-permute-start.14 = (f32[264,768]{1,0:T(8,128)}, f32[264,768]{1,0:T(8,128)S(1)}, u32[]{:S(2)}, u32[]{:S(2)}) collective-permute-start(f32[264,768]{1,0:T(8,128)} %collective-permute-done.8.across_ref.refs_15_), channel_id=1, source_target_pairs={{1,0},{2,3},{5,4},{6,7},{9,8},{10,11},{13,12},{14,15},{17,16},{18,... | collective-permute-start | bytes 2433032 | tf_op jit(solution)/shard_map/ppermute | solution.py:109
  109.2 29.8 %collective-permute-start.12 = (f32[264,384]{1,0:T(8,128)S(1)}, f32[264,384]{1,0:T(8,128)S(1)}, u32[]{:S(2)}, u32[]{:S(2)}) collective-permute-start(f32[264,384]{1,0:T(8,128)S(1)} %copy-done.5), channel_id=1, source_target_pairs={{0,1},{1,0},{2,3},{3,2},{4,5},{5,4},{6,7},{7,6},{8,9},{9,8},{10,11... | collective-permute-start | bytes 1216520 | tf_op jit(solution)/shard_map/ppermute | solution.py:109
  139.1 16.8 %collective-permute-start.16 = (f32[264,384]{1,0:T(8,128)S(1)}, f32[264,384]{1,0:T(8,128)S(1)}, u32[]{:S(2)}, u32[]{:S(2)}) collective-permute-start(f32[264,384]{1,0:T(8,128)S(1)} %copy-done.2), channel_id=1, source_target_pairs={{0,1},{1,0},{2,3},{3,2},{4,5},{5,4},{6,7},{7,6},{8,9},{9,8},{10,11... | collective-permute-start | bytes 1216520 | tf_op jit(solution)/shard_map/ppermute | solution.py:109
  139.2 24.1 %collective-permute-start.17 = (f32[264,768]{1,0:T(8,128)S(1)}, f32[264,768]{1,0:T(8,128)S(1)}, u32[]{:S(2)}, u32[]{:S(2)}) collective-permute-start(f32[264,768]{1,0:T(8,128)S(1)} %pad_maximum_fusion.8), channel_id=1, source_target_pairs={{1,2},{2,1},{5,6},{6,5},{9,10},{10,9},{13,14},{14,13},{17,18},{18,... | collective-permute-start | bytes 2433032 | tf_op jit(solution)/shard_map/ppermute | solution.py:109
  139.9 27.4 %collective-permute-start.18 = (f32[264,768]{1,0:T(8,128)S(1)}, f32[264,768]{1,0:T(8,128)S(1)}, u32[]{:S(2)}, u32[]{:S(2)}) collective-permute-start(f32[264,768]{1,0:T(8,128)S(1)} %collective-permute-done.13.across_ref.refs_15_), channel_id=1, source_target_pairs={{1,0},{2,3},{5,4},{6,7},{9,8},{10,11},{13,12},{14,15},{17,16},{18,... | collective-permute-start | bytes 2433032 | tf_op jit(solution)/shard_map/ppermute | solution.py:109
  155.9 41.4 %collective-permute-start.21 = (f32[264,1536]{1,0:T(8,128)}, f32[264,1536]{1,0:T(8,128)}, u32[]{:S(2)}, u32[]{:S(2)}) collective-permute-start(f32[264,1536]{1,0:T(8,128)} %get-tuple-element.418), channel_id=1, source_target_pairs={{0,1},{3,2},{4,5},{7,6},{8,9},{11,10},{12,13},{15,14},{16,17},{19,... | collective-permute-start | bytes 4866056 | tf_op jit(solution)/shard_map/ppermute | solution.py:109
  168.4 28.9 %collective-permute-start.19 = (f32[264,768]{1,0:T(8,128)}, f32[264,768]{1,0:T(8,128)S(1)}, u32[]{:S(2)}, u32[]{:S(2)}) collective-permute-start(f32[264,768]{1,0:T(8,128)} %pad_maximum_fusion.9), channel_id=1, source_target_pairs={{1,2},{2,1},{5,6},{6,5},{9,10},{10,9},{13,14},{14,13},{17,18},{18,... | collective-permute-start | bytes 2433032 | tf_op jit(solution)/shard_map/ppermute | solution.py:109
  169.1 28.2 %collective-permute-start.20 = (f32[264,768]{1,0:T(8,128)S(1)}, f32[264,768]{1,0:T(8,128)S(1)}, u32[]{:S(2)}, u32[]{:S(2)}) collective-permute-start(f32[264,768]{1,0:T(8,128)S(1)} %collective-permute-done.17.across_ref.refs_15_), channel_id=1, source_target_pairs={{1,0},{2,3},{5,4},{6,7},{9,8},{10,11},{13,12},{14,15},{17,16},{18,... | collective-permute-start | bytes 2433032 | tf_op jit(solution)/shard_map/ppermute | solution.py:109
  197.3 40.4 %collective-permute-start.23 = (f32[264,1536]{1,0:T(8,128)}, f32[264,1536]{1,0:T(8,128)}, u32[]{:S(2)}, u32[]{:S(2)}) collective-permute-start(f32[264,1536]{1,0:T(8,128)} %get-tuple-element.444), channel_id=1, source_target_pairs={{0,1},{3,2},{4,5},{7,6},{8,9},{11,10},{12,13},{15,14},{16,17},{19,... | collective-permute-start | bytes 4866056 | tf_op jit(solution)/shard_map/ppermute | solution.py:109
  204.6 33.2 %collective-permute-start.24 = (f32[256,1536]{1,0:T(8,128)S(1)}, f32[256,1536]{1,0:T(8,128)}, u32[]{:S(2)}, u32[]{:S(2)}) collective-permute-start(f32[256,1536]{1,0:T(8,128)S(1)} %slice_add_fusion.3), channel_id=1, source_target_pairs={{1,2},{2,1},{5,6},{6,5},{9,10},{10,9},{13,14},{14,13},{17,18},{18,... | collective-permute-start | bytes 4718600 | tf_op jit(solution)/shard_map/ppermute | solution.py:109
  206.4 31.4 %collective-permute-start.22 = (f32[264,768]{1,0:T(8,128)S(1)}, f32[264,768]{1,0:T(8,128)S(1)}, u32[]{:S(2)}, u32[]{:S(2)}) collective-permute-start(f32[264,768]{1,0:T(8,128)S(1)} %collective-permute-done.19.across_ref.refs_15_), channel_id=1, source_target_pairs={{1,0},{2,3},{5,4},{6,7},{9,8},{10,11},{13,12},{14,15},{17,16},{18,... | collective-permute-start | bytes 2433032 | tf_op jit(solution)/shard_map/ppermute | solution.py:109
  239.9 39.9 %collective-permute-start.25 = (f32[256,1536]{1,0:T(8,128)S(1)}, f32[256,1536]{1,0:T(8,128)}, u32[]{:S(2)}, u32[]{:S(2)}) collective-permute-start(f32[256,1536]{1,0:T(8,128)S(1)} %slice_select_fusion.total_ref), channel_id=1, source_target_pairs={{0,1},{1,0},{2,3},{3,2},{4,5},{5,4},{6,7},{7,6},{8,9},{9,8},{10,11... | collective-permute-start | bytes 4718600 | tf_op jit(solution)/shard_map/ppermute | solution.py:109
  244.7 35.1 %collective-permute-start.26 = (f32[256,1536]{1,0:T(8,128)S(1)}, f32[256,1536]{1,0:T(8,128)}, u32[]{:S(2)}, u32[]{:S(2)}) collective-permute-start(f32[256,1536]{1,0:T(8,128)S(1)} %slice_add_fusion.2), channel_id=1, source_target_pairs={{1,2},{2,1},{5,6},{6,5},{9,10},{10,9},{13,14},{14,13},{17,18},{18,... | collective-permute-start | bytes 4718600 | tf_op jit(solution)/shard_map/ppermute | solution.py:109
  284.4 44.8 %collective-permute-start.27 = (f32[256,1536]{1,0:T(8,128)}, f32[256,1536]{1,0:T(8,128)}, u32[]{:S(2)}, u32[]{:S(2)}) collective-permute-start(f32[256,1536]{1,0:T(8,128)} %add_select_fusion.1.total_ref), channel_id=1, source_target_pairs={{0,1},{1,0},{2,3},{3,2},{4,5},{5,4},{6,7},{7,6},{8,9},{9,8},{10,11... | collective-permute-start | bytes 4718600 | tf_op jit(solution)/shard_map/ppermute | solution.py:109
  289.1 40.2 %collective-permute-start.28 = (f32[256,1536]{1,0:T(8,128)}, f32[256,1536]{1,0:T(8,128)}, u32[]{:S(2)}, u32[]{:S(2)}) collective-permute-start(f32[256,1536]{1,0:T(8,128)} %slice_add_fusion.1), channel_id=1, source_target_pairs={{1,2},{2,1},{5,6},{6,5},{9,10},{10,9},{13,14},{14,13},{17,18},{18,... | collective-permute-start | bytes 4718600 | tf_op jit(solution)/shard_map/ppermute | solution.py:109
  333.4 37.3 %collective-permute-start.30 = (f32[256,1536]{1,0:T(8,128)}, f32[256,1536]{1,0:T(8,128)}, u32[]{:S(2)}, u32[]{:S(2)}) collective-permute-start(f32[256,1536]{1,0:T(8,128)} %select_select_fusion.1.total_ref), channel_id=1, source_target_pairs={{0,1},{1,0},{2,3},{3,2},{4,5},{5,4},{6,7},{7,6},{8,9},{9,8},{10,11... | collective-permute-start | bytes 4718600 | tf_op jit(solution)/shard_map/ppermute | solution.py:109
  336.7 34.0 %collective-permute-start.29 = (f32[256,1536]{1,0:T(8,128)S(1)}, f32[256,1536]{1,0:T(8,128)}, u32[]{:S(2)}, u32[]{:S(2)}) collective-permute-start(f32[256,1536]{1,0:T(8,128)S(1)} %slice_add_fusion.4), channel_id=1, source_target_pairs={{1,2},{2,1},{5,6},{6,5},{9,10},{10,9},{13,14},{14,13},{17,18},{18,... | collective-permute-start | bytes 4718600 | tf_op jit(solution)/shard_map/ppermute | solution.py:109
  374.2 34.2 %collective-permute-start.31 = (f32[264,1536]{1,0:T(8,128)}, f32[264,1536]{1,0:T(8,128)}, u32[]{:S(2)}, u32[]{:S(2)}) collective-permute-start(f32[264,1536]{1,0:T(8,128)} %pad.9.total_ref), channel_id=1, source_target_pairs={{0,1},{1,0},{2,3},{3,2},{4,5},{5,4},{6,7},{7,6},{8,9},{9,8},{10,11... | collective-permute-start | bytes 4866056 | tf_op jit(solution)/shard_map/ppermute | solution.py:109
  379.1 36.9 %collective-permute-start.32 = (f32[256,1536]{1,0:T(8,128)}, f32[256,1536]{1,0:T(8,128)}, u32[]{:S(2)}, u32[]{:S(2)}) collective-permute-start(f32[256,1536]{1,0:T(8,128)} %select_add_fusion), channel_id=1, source_target_pairs={{1,2},{2,1},{5,6},{6,5},{9,10},{10,9},{13,14},{14,13},{17,18},{18,... | collective-permute-start | bytes 4718600 | tf_op jit(solution)/shard_map/ppermute | solution.py:109
  428.5 44.5 %collective-permute-start.39 = (f32[256,1536]{1,0:T(8,128)}, f32[256,1536]{1,0:T(8,128)}, u32[]{:S(2)}, u32[]{:S(2)}) collective-permute-start(f32[256,1536]{1,0:T(8,128)} %get-tuple-element.628), channel_id=1, source_target_pairs={{0,1},{1,0},{2,3},{3,2},{4,5},{5,4},{6,7},{7,6},{8,9},{9,8},{10,11... | collective-permute-start | bytes 4718600 | tf_op jit(solution)/shard_map/ppermute | solution.py:109
  430.1 42.9 %collective-permute-start.40 = (f32[256,1536]{1,0:T(8,128)}, f32[256,1536]{1,0:T(8,128)}, u32[]{:S(2)}, u32[]{:S(2)}) collective-permute-start(f32[256,1536]{1,0:T(8,128)} %get-tuple-element.627), channel_id=1, source_target_pairs={{1,2},{2,1},{5,6},{6,5},{9,10},{10,9},{13,14},{14,13},{17,18},{18,... | collective-permute-start | bytes 4718600 | tf_op jit(solution)/shard_map/ppermute | solution.py:109
  440.8 24.5 %collective-permute-start.34 = (f32[192,1152]{1,0:T(8,128)}, f32[192,1152]{1,0:T(8,128)}, u32[]{:S(2)}, u32[]{:S(2)}) collective-permute-start(f32[192,1152]{1,0:T(8,128)} %get-tuple-element.573), channel_id=1, source_target_pairs={{0,8},{8,0},{16,24},{24,16},{1,9},{9,1},{17,25},{25,17},{2,10},{10... | collective-permute-start | bytes 2654216 | tf_op jit(solution)/shard_map/ppermute | solution.py:984
  442.4 22.9 %collective-permute-start.35 = (f32[192,1152]{1,0:T(8,128)}, f32[192,1152]{1,0:T(8,128)}, u32[]{:S(2)}, u32[]{:S(2)}) collective-permute-start(f32[192,1152]{1,0:T(8,128)} %get-tuple-element.575), channel_id=1, source_target_pairs={{0,16},{8,24},{16,0},{24,8},{1,17},{9,25},{17,1},{25,9},{2,18},{10... | collective-permute-start | bytes 2654216 | tf_op jit(solution)/shard_map/ppermute | solution.py:984
  (56 other events, 716.1 us)
Sparse Core Ops, SparseCore 0:
  103.9 78.1 all-gather.2
  280.0 125.8 reduce-scatter.1

commit v2 on v1

--- a/solution.py
+++ b/solution.py
@@ -21,11 +21,12 @@
 CHUNKS = 4
 EXTRA = 8
 VMEM_BYTES = 56 * 1024 * 1024
+LATE_VMEM_BYTES = 40 * 1024 * 1024
 NT = (((1,), (1,)), ((), ()))
 
 
-def params():
-    return pltpu.CompilerParams(vmem_limit_bytes=VMEM_BYTES)
+def params(vmem=VMEM_BYTES):
+    return pltpu.CompilerParams(vmem_limit_bytes=vmem)
 
 
 def cost(flops, moved, exps=0):
@@ -712,7 +713,7 @@
         in_specs=in_specs,
         out_specs=out_specs,
         scratch_shapes=scratch,
-        compiler_params=params(),
+        compiler_params=params(VMEM_BYTES if start else LATE_VMEM_BYTES),
         cost_estimate=cost(
             levels * rows * (20 * kv_here * keys * LANES + 2 * depth * (out_wide + wide)),
             2 * depth * levels * (out_wide + wide) + 16 * rows * depth,
@@ -775,7 +776,9 @@
                 give(group, left, whole_columns)
 
 
-def rows_of(lefts, groups, side, rows, blocks, step, recv=None, picked=None):
+def rows_of(
+    lefts, groups, side, rows, blocks, step, recv=None, picked=None, vmem=LATE_VMEM_BYTES
+):
     if picked is None:
         picked = [[(0, rows * blocks)]]
     at = lambda m: lambda i, side: ((m ^ side[2]) * side[1] + side[0], 0)
@@ -825,7 +828,7 @@
             out_specs=[block(height) for height in heights],
             scratch_shapes=[pltpu.VMEM((len(lefts), rows * blocks, tokens), jnp.bfloat16)],
         ),
-        compiler_params=params(),
+        compiler_params=params(vmem),
         cost_estimate=cost(
             2 * rows * blocks * tokens * total,
             4 * rows * blocks * total + 2 * tokens * (total + rows * blocks),
@@ -868,7 +871,7 @@
         grid=(1,),
         in_specs=[first] * 4,
         out_specs=[whole(out) for out in outs],
-        compiler_params=params(),
+        compiler_params=params(LATE_VMEM_BYTES),
         cost_estimate=cost(4 * half * columns, 32 * half * columns),
     )(one, far_one, two, far_two)
 
@@ -1141,7 +1144,9 @@
             input_grad,
         )
 
-    grad_mlp = rows_of(*mlp_args, all_rows, depth // 4, 4, units // 2)
+    grad_mlp = rows_of(
+        *mlp_args, all_rows, depth // 4, 4, units // 2, vmem=VMEM_BYTES
+    )
     own, other, across, outer, part, total, coming, final, hidden, grad_mlp = fence(
         own, other, across, outer, part, total, coming, final, hidden, grad_mlp
     )

time: 502 us -> 492 us (0.980)
  Pallas kernels: 296 us -> 283 us
  local copies, waits for them, and re-layouts: 17 us -> 23.8 us
    unnamed x87 -> x143, local copies, waits for them, and re-layouts: 2.1 us -> 11.8 us
    pallas_call x3, Pallas kernels: 35.8 us -> 27 us  [rows_of(): pl.pallas_call(functools.partial(rows_kernel, counts, plan, recv is not N...]
  transfers between devices with their start and end apart: 46 -> 46, of which waited for: 9 -> 9; matrix products, arithmetic and copies ran while one was open for 12% -> 12% of each run, Pallas kernels for 59% -> 58%
where the time goes in v2:
time: 492 us; the launch traced here: 486 us
  Pallas kernels  283 us (58%)
  starting transfers between devices  75.3 us (15%)
  other arithmetic  53.9 us (11%)
  waiting for transfers between devices  34 us (7%)
  local copies, waits for them, and re-layouts  23.8 us (5%)
  between operations  16.2 us (3%)
    pallas_call x5, Pallas kernels, backward_chunk(): pl.pallas_call(functools.partial(backward_kernel, start, full, acc is not...  121 us
    ppermute x30, starting transfers between devices, along(): return lax.ppermute(part, 'tp', pairs)  59.3 us
    pallas_call x4, Pallas kernels, forward_chunk(): pl.pallas_call(forward_kernel, out_shape=outs, grid=(steps,), in_specs=[S...  56.1 us
    ppermute x30, waiting for transfers between devices, along(): return lax.ppermute(part, 'tp', pairs)  32 us
    pallas_call x3, Pallas kernels, rows_of(): pl.pallas_call(functools.partial(rows_kernel, counts, plan, recv is not N...  27 us
    pallas_call x4, Pallas kernels, attend(): pl.pallas_call(functools.partial(attend_kernel, index * rows), out_shape=...  21.1 us
    pallas_call x1, Pallas kernels, project(): pl.pallas_call(project_kernel, out_shape=jax.ShapeDtypeStruct((rows, widt...  15.9 us
    ppermute x11, starting transfers between devices, to_chip(): return lax.ppermute(array, 'chip', [(i, i ^ m) for i in range(chips)])  15.3 us
  transfers between devices with their start and end apart: 46, of which 9 were waited for; matrix products, arithmetic and copies ran while one was open for 12% of the time, Pallas kernels for 58%

profile of v2, /device:TPU:0, one launch (start us, length us, event | category | flops | bytes accessed | tf_op | source)
XLA Modules:
  0.0 486.3 jit_solution(711557294886074441)
XLA Ops:
  10.9 3.1 collective-permute-start
  17.3 4.5 collective-permute-done
  25.1 10.4 %shard_map.221 = (bf16[1024,4096]{1,0:T(8,128)(2,1)}, bf16[1024,1536]{1,0:T(8,128)(2,1)}, bf16[1536,4096]{1,0:T(8,128)(2,1)}) custom-call(bf16[1024,1536]{1,0:T(8,128)(2,1)} %refs_12_.7, f32[1,1536]{1,0:T(1,128)} %broadcast_in_dim.10.gain_ref.refs_13_, bf16[1536,384]{1,0:T(8,128)(2,1)} %q_ref.1, bf16[192,1536]{1,0:T(8,128)(2,1)} %bitcast.32, ...), custom_call_target="tpu_custom_call" | custom-call | flops 3145728 | bytes 18432 | tf_op jit(solution)/shard_map/pallas_call | solution.py:230
  40.3 5.6 %shard_map.222.part_ref.refs_7_.refs_22_ = f32[264,384]{1,0:T(8,128)} custom-call(s32[1]{0:T(128)S(6)} %copy.46.length_ref, bf16[1024,4096]{1,0:T(8,128)(2,1)} %get-tuple-element.327.q_ref.kv_ref._, bf16[1024,4096]{1,0:T(8,128)(2,1)} %get-tuple-element.327.q_ref.kv_ref._, bf16[512,384]{1,0:T(8,128)(2,1)} %fusion.2.strip_ref), custom_call_target="tpu_custom_call" | custom-call | flops 393216 | bytes 2048 | tf_op jit(solution)/shard_map/pallas_call | solution.py:337
  45.9 6.6 %shard_map.223.part_ref.refs_7_.refs_23_ = f32[264,384]{1,0:T(8,128)} custom-call(s32[1]{0:T(128)S(6)} %copy.46.length_ref, bf16[1024,4096]{1,0:T(8,128)(2,1)} %get-tuple-element.327.q_ref.kv_ref._, bf16[1024,4096]{1,0:T(8,128)(2,1)} %get-tuple-element.327.q_ref.kv_ref._, bf16[512,384]{1,0:T(8,128)(2,1)} %fusion.2.strip_ref), custom_call_target="tpu_custom_call" | custom-call | flops 524288 | bytes 2560 | tf_op jit(solution)/shard_map/pallas_call | solution.py:337
  53.7 6.0 %collective-permute-start.5 = (f32[528,384]{1,0:T(8,128)S(1)}, f32[528,384]{1,0:T(8,128)S(1)}, u32[]{:S(2)}, u32[]{:S(2)}) collective-permute-start(f32[528,384]{1,0:T(8,128)S(1)} %pad_maximum_fusion.5), channel_id=1, source_target_pairs={{0,1},{1,0},{2,3},{3,2},{4,5},{5,4},{6,7},{7,6},{8,9},{9,8},{10,11... | collective-permute-start | bytes 2433032 | tf_op jit(solution)/shard_map/ppermute | solution.py:110
  63.0 4.1 shard_map.224.part_ref.refs_7_.refs_20_
  67.2 4.8 shard_map.225.part_ref.refs_7_.refs_21_
  83.5 7.0 %shard_map.226 = (bf16[1024,1536]{1,0:T(8,128)(2,1)}, bf16[1536,1024]{1,0:T(8,128)(2,1)}, bf16[1536,1024]{1,0:T(8,128)(2,1)}) custom-call(s32[1]{0:T(128)S(6)} %copy.46.length_ref, bf16[1024,1536]{1,0:T(8,128)(2,1)} %cot_ref.1, bf16[1024,1536]{1,0:T(8,128)(2,1)} %get-tuple-element.339.normed_ref.x_ref), custom_call_target="tpu_custom_call" | custom-call | flops 1536 | bytes 15360 | tf_op jit(solution)/shard_map/pallas_call | solution.py:263
  94.9 5.7 %collective-permute-done.11 = f32[2,192,768]{2,1,0:T(8,128)} collective-permute-done((f32[2,192,768]{2,1,0:T(8,128)}, f32[2,192,768]{2,1,0:T(8,128)}, u32[]{:S(2)}, u32[]{:S(2)}) %collective-permute-start.11) | collective-permute-done | bytes 1179680 | tf_op jit(solution)/shard_map/ppermute | solution.py:110
  113.7 10.2 %shard_map.227 = (bf16[1536,2048]{1,0:T(8,128)(2,1)}, bf16[1536,1536]{1,0:T(8,128)(2,1)}) custom-call(s32[2]{0:T(128)} %pad_add_fusion.4.meta_ref, bf16[1536,384]{1,0:T(8,128)(2,1)} %bitcast.25, bf16[384,512]{1,0:T(8,128)(2,1)} %fusion.3.p_ref.refs_8_, f32[4,3,192,384]{3,2,1,0:T(8,128)} %copy-done.42, f32[4,3,192,384]{3,2,1,0:T(8,128)} %collective-permute-done.15.theirs_ref), custom_call_target="tpu_custom_call" | custom-call | flops 2359296 | bytes 17664 | tf_op jit(solution)/shard_map/pallas_call | solution.py:180
  123.9 15.4 %collective-permute-done.12.other_ref.refs_14_ = f32[264,384]{1,0:T(8,128)S(1)} collective-permute-done((f32[264,384]{1,0:T(8,128)S(1)}, f32[264,384]{1,0:T(8,128)S(1)}, u32[]{:S(2)}, u32[]{:S(2)}) %collective-permute-start.12) | collective-permute-done | bytes 405536 | tf_op jit(solution)/shard_map/ppermute | solution.py:110
  143.0 13.9 %shard_map.228 = (f32[256,1536]{1,0:T(8,128)}, bf16[1536,256]{1,0:T(8,128)(2,1)}, bf16[256,1024]{1,0:T(8,128)(2,1)}, bf16[256,1024]{1,0:T(8,128)(2,1)}, bf16[256...) custom-call(s32[1]{0:T(128)} %bitcast.2.level_ref, f32[264,384]{1,0:T(8,128)} %shard_map.223.part_ref.refs_7_.refs_23_, ...), custom_call_target="tpu_custom_call" | custom-call | flops 5898240 | bytes 22272 | tf_op jit(solution)/shard_map/pallas_call | solution.py:428
  156.9 6.7 %collective-permute-start.21 = (f32[264,1536]{1,0:T(8,128)}, f32[264,1536]{1,0:T(8,128)}, u32[]{:S(2)}, u32[]{:S(2)}) collective-permute-start(f32[264,1536]{1,0:T(8,128)} %get-tuple-element.418), channel_id=1, source_target_pairs={{0,1},{3,2},{4,5},{7,6},{8,9},{11,10},{12,13},{15,14},{16,17},{19,... | collective-permute-start | bytes 4866056 | tf_op jit(solution)/shard_map/ppermute | solution.py:110
  163.6 4.0 collective-permute-done.18.outer_ref.refs_16_
  169.7 14.2 %shard_map.229 = (f32[256,1536]{1,0:T(8,128)}, bf16[1536,256]{1,0:T(8,128)(2,1)}, bf16[256,1024]{1,0:T(8,128)(2,1)}, bf16[256,1024]{1,0:T(8,128)(2,1)}, bf16[256...) custom-call(s32[1]{0:T(128)} %bitcast.2.level_ref, f32[264,384]{1,0:T(8,128)} %shard_map.222.part_ref.refs_7_.refs_22_, ...), custom_call_target="tpu_custom_call" | custom-call | flops 5898240 | bytes 22272 | tf_op jit(solution)/shard_map/pallas_call | solution.py:428
  184.0 12.7 %shard_map.230.w_ref.refs_17_ = bf16[1536,4096]{1,0:T(8,128)(2,1)} custom-call(bf16[384,512]{1,0:T(8,128)(2,1)} %fusion.pq_ref, bf16[384,512]{1,0:T(8,128)(2,1)} %fusion.1.pkv_ref, f32[8,3,192,768]{3,2,1,0:T(8,128)} %bitcast.24, bf16[1536,4096]{1,0:T(8,128)(2,1)} %get-tuple-element.400._), custom_call_target="tpu_custom_call", output_to_operand_aliasing={{}: (3, {})} | custom-call | flops 4718592 | bytes 30720 | tf_op jit(solution)/shard_map/pallas_call | solution.py:158
  196.7 5.7 %collective-permute-start.23 = (f32[264,1536]{1,0:T(8,128)}, f32[264,1536]{1,0:T(8,128)}, u32[]{:S(2)}, u32[]{:S(2)}) collective-permute-start(f32[264,1536]{1,0:T(8,128)} %get-tuple-element.444), channel_id=1, source_target_pairs={{0,1},{3,2},{4,5},{7,6},{8,9},{11,10},{12,13},{15,14},{16,17},{19,... | collective-permute-start | bytes 4866056 | tf_op jit(solution)/shard_map/ppermute | solution.py:110
  206.3 14.0 %shard_map.231 = (f32[256,1536]{1,0:T(8,128)}, bf16[1536,256]{1,0:T(8,128)(2,1)}, bf16[256,1024]{1,0:T(8,128)(2,1)}, bf16[256,1024]{1,0:T(8,128)(2,1)}, bf16[256...) custom-call(s32[1]{0:T(128)} %bitcast.2.level_ref, f32[264,384]{1,0:T(8,128)} %shard_map.225.part_ref.refs_7_.refs_21_, ...), custom_call_target="tpu_custom_call" | custom-call | flops 5898240 | bytes 22272 | tf_op jit(solution)/shard_map/pallas_call | solution.py:428
  220.3 15.9 %shard_map.232.refs_2_.refs_3_.refs_4_.refs_5_.refs_6_ = bf16[1024,4096]{1,0:T(8,128)(2,1)} custom-call(bf16[1024,1536]{1,0:T(8,128)(2,1)} %get-tuple-element.339.normed_ref.x_ref, bf16[1536,4096]{1,0:T(8,128)(2,1)} %shard_map.230.w_ref.refs_17_, f32[1024,128]{1,0:T(8,128)} %get-tuple-element.320.cos_ref.refs_10_, ...), custom_call_target="tpu_custom_call", output_to_operand_aliasing={{}: (4, {})} | custom-call | flops 12582912 | bytes 23552 | tf_op jit(solution)/shard_map/pallas_call | solution.py:283
  246.1 13.9 %shard_map.233 = (f32[256,1536]{1,0:T(8,128)}, bf16[1536,256]{1,0:T(8,128)(2,1)}, bf16[256,1024]{1,0:T(8,128)(2,1)}, bf16[256,1024]{1,0:T(8,128)(2,1)}, bf16[256...) custom-call(s32[1]{0:T(128)} %bitcast.2.level_ref, f32[264,384]{1,0:T(8,128)} %shard_map.224.part_ref.refs_7_.refs_20_, ...), custom_call_target="tpu_custom_call" | custom-call | flops 5898240 | bytes 22272 | tf_op jit(solution)/shard_map/pallas_call | solution.py:428
  260.0 19.4 %shard_map.234 = f32[1536,3072]{1,0:T(8,128)} custom-call(s32[3]{0:T(128)} %constant.159.clone.side_ref, bf16[1536,256]{1,0:T(8,128)(2,1)} %get-tuple-element.452.refs_0_.refs_1_.refs_2_.refs_3_, bf16[1536,256]{1,0:T(8,128)(2,1)} %get-tuple-element.452.refs_0_.refs_1_.refs_2_.refs_3_, bf16[1536,256]{1,0:T(8,128)(2,1)} %get-tuple-element.452.refs_0_.refs_1_.refs_2_.refs_3_, ...), custom_call_target="tpu_custom_call" | custom-call | flops 9437184 | bytes 27648 | tf_op jit(solution)/shard_map/pallas_call | solution.py:821
  288.6 37.3 %shard_map.235 = (bf16[1536,256]{1,0:T(8,128)(2,1)}, bf16[256,768]{1,0:T(8,128)(2,1)}, bf16[1024,1536]{1,0:T(8,128)(2,1)}, f32[8,1536]{1,0:T(8,128)}, f32[768,2048]{1,0:T(8,128)}) custom-call(s32[1]{0:T(128)} %bitcast.2.level_ref, f32[256,1536]{1,0:T(8,128)} %copy-done.49, f32[256,1536]{1,0:T(8,128)} %collective-permute-done.25.final_ref, ...), custom_call_target="tpu_custom_call" | custom-call | flops 9961472 | bytes 24576 | tf_op jit(solution)/shard_map/pallas_call | solution.py:708
  325.9 3.5 select_select_fusion.1.total_ref
  334.5 31.6 %shard_map.236 = (bf16[1536,256]{1,0:T(8,128)(2,1)}, bf16[256,768]{1,0:T(8,128)(2,1)}, bf16[1024,1536]{1,0:T(8,128)(2,1)}, f32[8,1536]{1,0:T(8,128)}, f32[512,2048]{1,0:T(8,128)}) custom-call(s32[1]{0:T(128)} %bitcast.2.level_ref, f32[256,1536]{1,0:T(8,128)} %copy-done.50, ...), custom_call_target="tpu_custom_call", output_to_operand_aliasing={{2}: (24, {})} | custom-call | flops 8650752 | bytes 24576 | tf_op jit(solution)/shard_map/pallas_call | solution.py:708
  370.2 3.1 select_add_fusion
  375.3 26.9 %shard_map.237 = (bf16[1536,256]{1,0:T(8,128)(2,1)}, bf16[256,768]{1,0:T(8,128)(2,1)}, bf16[1024,1536]{1,0:T(8,128)(2,1)}, f32[8,1536]{1,0:T(8,128)}, f32[256,2048]{1,0:T(8,128)}) custom-call(s32[1]{0:T(128)} %bitcast.2.level_ref, f32[256,1536]{1,0:T(8,128)} %select_select_fusion.1.total_ref, ...), custom_call_target="tpu_custom_call", output_to_operand_aliasing={{2}: (24, {})} | custom-call | flops 7340032 | bytes 24576 | tf_op jit(solution)/shard_map/pallas_call | solution.py:708
  405.7 5.5 %shard_map.238 = (bf16[1536,256]{1,0:T(8,128)(2,1)S(1)}, bf16[256,768]{1,0:T(8,128)(2,1)S(1)}) custom-call(s32[1]{0:T(128)} %bitcast.2.level_ref, f32[264,1536]{1,0:T(8,128)S(1)} %pad.9.total_ref, f32[264,1536]{1,0:T(8,128)} %collective-permute-done.31.final_ref, f32[256,1536]{1,0:T(8,128)S(1)} %copy-done.17, bf16[1024,1536]{1,0:T(8,128)(2,1)S(1)} %copy-done, ...), custom_call_target="tpu_custom_call" | custom-call | flops 6029312 | bytes 24576 | tf_op jit(solution)/shard_map/pallas_call | solution.py:708
  414.3 5.1 %slice_add_fusion = (f32[256,1536]{1,0:T(8,128)}, f32[256,1536]{1,0:T(8,128)}) fusion(f32[264,1536]{1,0:T(8,128)} %collective-permute-done.31.final_ref, f32[256,1536]{1,0:T(8,128)S(1)} %copy-done.44, f32[256,1536]{1,0:T(8,128)} %get-tuple-element.597, pred[]{:T(512)S(6)} %lt.101, f32[256,1536]{1,0:T(8,128)} %collective-permute-done.32, ...), kind=kLoop, calls=%fused_computation.3 | loop fusion | flops 2359296 | bytes 12582914 | tf_op jit(solution)/shard_map/add | solution.py:1180
  424.6 4.9 shard_map.240
  437.2 20.1 %shard_map.241 = (bf16[1536,256]{1,0:T(8,128)(2,1)}, bf16[256,768]{1,0:T(8,128)(2,1)}, bf16[1024,1536]{1,0:T(8,128)(2,1)}, f32[8,1536]{1,0:T(8,128)S(1)}) custom-call(s32[1]{0:T(128)} %bitcast.2.level_ref, f32[264,1536]{1,0:T(8,128)S(1)} %pad.9.total_ref, f32[264,1536]{1,0:T(8,128)} %collective-permute-done.31.final_ref, ...), custom_call_target="tpu_custom_call", output_to_operand_aliasing={{2}: (24, {})} | custom-call | flops 6029312 | bytes 24576 | tf_op jit(solution)/shard_map/pallas_call | solution.py:708
  468.2 5.4 %add_convert_fusion = bf16[256,1536]{1,0:T(8,128)(2,1)} fusion(f32[256,1536]{1,0:T(8,128)} %collective-permute-done.39, f32[256,1536]{1,0:T(8,128)} %collective-permute-done.40, f32[256,1536]{1,0:T(8,128)} %get-tuple-element.595.hidden_ref, f32[256,1536]{1,0:T(8,128)} %get-tuple-element.596.hidden_ref, f32[256,1536]{1,0:T(8,128)S(1)} %copy-done.19, ...), kind=kLoop, calls=%fused_computation.2 | loop fusion | flops 3932160 | bytes 16515076 | tf_op jit(solution)/shard_map/convert_element_type | solution.py:1215
  (293 shorter events, 122.8 us)
Async XLA Ops:
  7.2 176.8 %all-gather.3.cloned.1.call-start = ((), (), s32[]{:S(2)}) async-start(), calls=%async_computation.2 | async-start | bytes 15925248 | tf_op jit(solution)/shard_map/all_gather | solution.py:1030
  14.0 21.5 %collective-permute-start.2 = (f32[192,768]{1,0:T(8,128)S(1)}, f32[192,768]{1,0:T(8,128)S(1)}, u32[]{:S(2)}, u32[]{:S(2)}) collective-permute-start(f32[192,768]{1,0:T(8,128)S(1)} %maximum_convert_fusion), channel_id=1, source_target_pairs={{0,1},{1,0},{2,3},{3,2},{4,5},{5,4},{6,7},{7,6},{8,9},{9,8},{10,11... | collective-permute-start | bytes 1769480 | tf_op jit(solution)/shard_map/ppermute | solution.py:110
  35.5 17.2 %collective-permute-start.3 = (f32[2,192,384]{2,1,0:T(8,128)S(1)}, f32[2,192,384]{2,1,0:T(8,128)S(1)}, u32[]{:S(2)}, u32[]{:S(2)}) collective-permute-start(f32[2,192,384]{2,1,0:T(8,128)S(1)} %collective-permute-done.1), channel_id=1, source_target_pairs={{1,0},{2,3},{5,4},{6,7},{9,8},{10,11},{13,12},{14,15},{17,16},{18,... | collective-permute-start | bytes 1769480 | tf_op jit(solution)/shard_map/ppermute | solution.py:110
  38.4 34.7 %collective-permute-start.4 = (f32[2,192,768]{2,1,0:T(8,128)S(1)}, f32[2,192,768]{2,1,0:T(8,128)}, u32[]{:S(2)}, u32[]{:S(2)}) collective-permute-start(f32[2,192,768]{2,1,0:T(8,128)S(1)} %pad_maximum_fusion.1), channel_id=1, source_target_pairs={{1,2},{2,1},{5,6},{6,5},{9,10},{10,9},{13,14},{14,13},{17,18},{18,... | collective-permute-start | bytes 3538952 | tf_op jit(solution)/shard_map/ppermute | solution.py:110
  53.7 22.5 %collective-permute-start.5 = (f32[528,384]{1,0:T(8,128)S(1)}, f32[528,384]{1,0:T(8,128)S(1)}, u32[]{:S(2)}, u32[]{:S(2)}) collective-permute-start(f32[528,384]{1,0:T(8,128)S(1)} %pad_maximum_fusion.5), channel_id=1, source_target_pairs={{0,1},{1,0},{2,3},{3,2},{4,5},{5,4},{6,7},{7,6},{8,9},{9,8},{10,11... | collective-permute-start | bytes 2433032 | tf_op jit(solution)/shard_map/ppermute | solution.py:110
  73.1 27.5 %collective-permute-start.11 = (f32[2,192,768]{2,1,0:T(8,128)}, f32[2,192,768]{2,1,0:T(8,128)}, u32[]{:S(2)}, u32[]{:S(2)}) collective-permute-start(f32[2,192,768]{2,1,0:T(8,128)} %collective-permute-done.4), channel_id=1, source_target_pairs={{1,0},{2,3},{5,4},{6,7},{9,8},{10,11},{13,12},{14,15},{17,16},{18,... | collective-permute-start | bytes 3538952 | tf_op jit(solution)/shard_map/ppermute | solution.py:110
  76.3 17.2 %collective-permute-start.10 = (f32[2,3,96,384]{3,2,1,0:T(8,128)S(1)}, f32[2,3,96,384]{3,2,1,0:T(8,128)}, u32[]{:S(2)}, u32[]{:S(2)}) collective-permute-start(f32[2,3,96,384]{3,2,1,0:T(8,128)S(1)} %pad_maximum_fusion.4), channel_id=1, source_target_pairs={{0,8},{8,0},{16,24},{24,16},{1,9},{9,1},{17,25},{25,17},{2,10},{10... | collective-permute-start | bytes 2654216 | tf_op jit(solution)/shard_map/ppermute | solution.py:987
  103.7 369.8 %reduce-scatter.2.cloned.1.call-start = ((), (), s32[]{:S(2)}) async-start(), calls=%async_computation.1 | async-start | bytes 21233664 | tf_op jit(solution)/shard_map/reduce_scatter | solution.py:1109
  107.3 32.0 %collective-permute-start.13 = (f32[264,768]{1,0:T(8,128)S(1)}, f32[264,768]{1,0:T(8,128)S(1)}, u32[]{:S(2)}, u32[]{:S(2)}) collective-permute-start(f32[264,768]{1,0:T(8,128)S(1)} %pad_maximum_fusion.7), channel_id=1, source_target_pairs={{1,2},{2,1},{5,6},{6,5},{9,10},{10,9},{13,14},{14,13},{17,18},{18,... | collective-permute-start | bytes 2433032 | tf_op jit(solution)/shard_map/ppermute | solution.py:110
  108.2 31.1 %collective-permute-start.14 = (f32[264,768]{1,0:T(8,128)}, f32[264,768]{1,0:T(8,128)S(1)}, u32[]{:S(2)}, u32[]{:S(2)}) collective-permute-start(f32[264,768]{1,0:T(8,128)} %collective-permute-done.8.across_ref.refs_15_), channel_id=1, source_target_pairs={{1,0},{2,3},{5,4},{6,7},{9,8},{10,11},{13,12},{14,15},{17,16},{18,... | collective-permute-start | bytes 2433032 | tf_op jit(solution)/shard_map/ppermute | solution.py:110
  109.5 29.8 %collective-permute-start.12 = (f32[264,384]{1,0:T(8,128)S(1)}, f32[264,384]{1,0:T(8,128)S(1)}, u32[]{:S(2)}, u32[]{:S(2)}) collective-permute-start(f32[264,384]{1,0:T(8,128)S(1)} %copy-done.14), channel_id=1, source_target_pairs={{0,1},{1,0},{2,3},{3,2},{4,5},{5,4},{6,7},{7,6},{8,9},{9,8},{10,11... | collective-permute-start | bytes 1216520 | tf_op jit(solution)/shard_map/ppermute | solution.py:110
  139.3 17.6 %collective-permute-start.16 = (f32[264,384]{1,0:T(8,128)S(1)}, f32[264,384]{1,0:T(8,128)S(1)}, u32[]{:S(2)}, u32[]{:S(2)}) collective-permute-start(f32[264,384]{1,0:T(8,128)S(1)} %copy-done.7), channel_id=1, source_target_pairs={{0,1},{1,0},{2,3},{3,2},{4,5},{5,4},{6,7},{7,6},{8,9},{9,8},{10,11... | collective-permute-start | bytes 1216520 | tf_op jit(solution)/shard_map/ppermute | solution.py:110
  139.5 24.1 %collective-permute-start.17 = (f32[264,768]{1,0:T(8,128)S(1)}, f32[264,768]{1,0:T(8,128)}, u32[]{:S(2)}, u32[]{:S(2)}) collective-permute-start(f32[264,768]{1,0:T(8,128)S(1)} %pad_maximum_fusion.8), channel_id=1, source_target_pairs={{1,2},{2,1},{5,6},{6,5},{9,10},{10,9},{13,14},{14,13},{17,18},{18,... | collective-permute-start | bytes 2433032 | tf_op jit(solution)/shard_map/ppermute | solution.py:110
  141.1 26.6 %collective-permute-start.18 = (f32[264,768]{1,0:T(8,128)S(1)}, f32[264,768]{1,0:T(8,128)S(1)}, u32[]{:S(2)}, u32[]{:S(2)}) collective-permute-start(f32[264,768]{1,0:T(8,128)S(1)} %collective-permute-done.13.across_ref.refs_15_), channel_id=1, source_target_pairs={{1,0},{2,3},{5,4},{6,7},{9,8},{10,11},{13,12},{14,15},{17,16},{18,... | collective-permute-start | bytes 2433032 | tf_op jit(solution)/shard_map/ppermute | solution.py:110
  156.9 39.7 %collective-permute-start.21 = (f32[264,1536]{1,0:T(8,128)}, f32[264,1536]{1,0:T(8,128)}, u32[]{:S(2)}, u32[]{:S(2)}) collective-permute-start(f32[264,1536]{1,0:T(8,128)} %get-tuple-element.418), channel_id=1, source_target_pairs={{0,1},{3,2},{4,5},{7,6},{8,9},{11,10},{12,13},{15,14},{16,17},{19,... | collective-permute-start | bytes 4866056 | tf_op jit(solution)/shard_map/ppermute | solution.py:110
  167.7 29.0 %collective-permute-start.19 = (f32[264,768]{1,0:T(8,128)S(1)}, f32[264,768]{1,0:T(8,128)S(1)}, u32[]{:S(2)}, u32[]{:S(2)}) collective-permute-start(f32[264,768]{1,0:T(8,128)S(1)} %pad_maximum_fusion.9), channel_id=1, source_target_pairs={{1,2},{2,1},{5,6},{6,5},{9,10},{10,9},{13,14},{14,13},{17,18},{18,... | collective-permute-start | bytes 2433032 | tf_op jit(solution)/shard_map/ppermute | solution.py:110
  168.4 28.2 %collective-permute-start.20 = (f32[264,768]{1,0:T(8,128)}, f32[264,768]{1,0:T(8,128)S(1)}, u32[]{:S(2)}, u32[]{:S(2)}) collective-permute-start(f32[264,768]{1,0:T(8,128)} %collective-permute-done.17.across_ref.refs_15_), channel_id=1, source_target_pairs={{1,0},{2,3},{5,4},{6,7},{9,8},{10,11},{13,12},{14,15},{17,16},{18,... | collective-permute-start | bytes 2433032 | tf_op jit(solution)/shard_map/ppermute | solution.py:110
  196.7 39.6 %collective-permute-start.23 = (f32[264,1536]{1,0:T(8,128)}, f32[264,1536]{1,0:T(8,128)}, u32[]{:S(2)}, u32[]{:S(2)}) collective-permute-start(f32[264,1536]{1,0:T(8,128)} %get-tuple-element.444), channel_id=1, source_target_pairs={{0,1},{3,2},{4,5},{7,6},{8,9},{11,10},{12,13},{15,14},{16,17},{19,... | collective-permute-start | bytes 4866056 | tf_op jit(solution)/shard_map/ppermute | solution.py:110
  204.0 32.2 %collective-permute-start.24 = (f32[256,1536]{1,0:T(8,128)S(1)}, f32[256,1536]{1,0:T(8,128)S(1)}, u32[]{:S(2)}, u32[]{:S(2)}) collective-permute-start(f32[256,1536]{1,0:T(8,128)S(1)} %slice_add_fusion.3), channel_id=1, source_target_pairs={{1,2},{2,1},{5,6},{6,5},{9,10},{10,9},{13,14},{14,13},{17,18},{18,... | collective-permute-start | bytes 4718600 | tf_op jit(solution)/shard_map/ppermute | solution.py:110
  204.8 31.4 %collective-permute-start.22 = (f32[264,768]{1,0:T(8,128)S(1)}, f32[264,768]{1,0:T(8,128)S(1)}, u32[]{:S(2)}, u32[]{:S(2)}) collective-permute-start(f32[264,768]{1,0:T(8,128)S(1)} %collective-permute-done.19.across_ref.refs_15_), channel_id=1, source_target_pairs={{1,0},{2,3},{5,4},{6,7},{9,8},{10,11},{13,12},{14,15},{17,16},{18,... | collective-permute-start | bytes 2433032 | tf_op jit(solution)/shard_map/ppermute | solution.py:110
  239.2 40.1 %collective-permute-start.25 = (f32[256,1536]{1,0:T(8,128)S(1)}, f32[256,1536]{1,0:T(8,128)}, u32[]{:S(2)}, u32[]{:S(2)}) collective-permute-start(f32[256,1536]{1,0:T(8,128)S(1)} %slice_select_fusion.total_ref), channel_id=1, source_target_pairs={{0,1},{1,0},{2,3},{3,2},{4,5},{5,4},{6,7},{7,6},{8,9},{9,8},{10,11... | collective-permute-start | bytes 4718600 | tf_op jit(solution)/shard_map/ppermute | solution.py:110
  244.3 35.1 %collective-permute-start.26 = (f32[256,1536]{1,0:T(8,128)S(1)}, f32[256,1536]{1,0:T(8,128)}, u32[]{:S(2)}, u32[]{:S(2)}) collective-permute-start(f32[256,1536]{1,0:T(8,128)S(1)} %slice_add_fusion.2), channel_id=1, source_target_pairs={{1,2},{2,1},{5,6},{6,5},{9,10},{10,9},{13,14},{14,13},{17,18},{18,... | collective-permute-start | bytes 4718600 | tf_op jit(solution)/shard_map/ppermute | solution.py:110
  281.8 44.0 %collective-permute-start.27 = (f32[256,1536]{1,0:T(8,128)S(1)}, f32[256,1536]{1,0:T(8,128)}, u32[]{:S(2)}, u32[]{:S(2)}) collective-permute-start(f32[256,1536]{1,0:T(8,128)S(1)} %add_select_fusion.1.total_ref), channel_id=1, source_target_pairs={{0,1},{1,0},{2,3},{3,2},{4,5},{5,4},{6,7},{7,6},{8,9},{9,8},{10,11... | collective-permute-start | bytes 4718600 | tf_op jit(solution)/shard_map/ppermute | solution.py:110
  285.6 40.3 %collective-permute-start.28 = (f32[256,1536]{1,0:T(8,128)S(1)}, f32[256,1536]{1,0:T(8,128)}, u32[]{:S(2)}, u32[]{:S(2)}) collective-permute-start(f32[256,1536]{1,0:T(8,128)S(1)} %slice_add_fusion.1), channel_id=1, source_target_pairs={{1,2},{2,1},{5,6},{6,5},{9,10},{10,9},{13,14},{14,13},{17,18},{18,... | collective-permute-start | bytes 4718600 | tf_op jit(solution)/shard_map/ppermute | solution.py:110
  329.5 36.7 %collective-permute-start.30 = (f32[256,1536]{1,0:T(8,128)}, f32[256,1536]{1,0:T(8,128)}, u32[]{:S(2)}, u32[]{:S(2)}) collective-permute-start(f32[256,1536]{1,0:T(8,128)} %select_select_fusion.1.total_ref), channel_id=1, source_target_pairs={{0,1},{1,0},{2,3},{3,2},{4,5},{5,4},{6,7},{7,6},{8,9},{9,8},{10,11... | collective-permute-start | bytes 4718600 | tf_op jit(solution)/shard_map/ppermute | solution.py:110
  332.3 33.9 %collective-permute-start.29 = (f32[256,1536]{1,0:T(8,128)S(1)}, f32[256,1536]{1,0:T(8,128)}, u32[]{:S(2)}, u32[]{:S(2)}) collective-permute-start(f32[256,1536]{1,0:T(8,128)S(1)} %slice_add_fusion.4), channel_id=1, source_target_pairs={{1,2},{2,1},{5,6},{6,5},{9,10},{10,9},{13,14},{14,13},{17,18},{18,... | collective-permute-start | bytes 4718600 | tf_op jit(solution)/shard_map/ppermute | solution.py:110
  368.4 34.2 %collective-permute-start.31 = (f32[264,1536]{1,0:T(8,128)S(1)}, f32[264,1536]{1,0:T(8,128)}, u32[]{:S(2)}, u32[]{:S(2)}) collective-permute-start(f32[264,1536]{1,0:T(8,128)S(1)} %pad.9.total_ref), channel_id=1, source_target_pairs={{0,1},{1,0},{2,3},{3,2},{4,5},{5,4},{6,7},{7,6},{8,9},{9,8},{10,11... | collective-permute-start | bytes 4866056 | tf_op jit(solution)/shard_map/ppermute | solution.py:110
  373.2 38.0 %collective-permute-start.32 = (f32[256,1536]{1,0:T(8,128)}, f32[256,1536]{1,0:T(8,128)}, u32[]{:S(2)}, u32[]{:S(2)}) collective-permute-start(f32[256,1536]{1,0:T(8,128)} %select_add_fusion), channel_id=1, source_target_pairs={{1,2},{2,1},{5,6},{6,5},{9,10},{10,9},{13,14},{14,13},{17,18},{18,... | collective-permute-start | bytes 4718600 | tf_op jit(solution)/shard_map/ppermute | solution.py:110
  419.4 45.3 %collective-permute-start.39 = (f32[256,1536]{1,0:T(8,128)}, f32[256,1536]{1,0:T(8,128)}, u32[]{:S(2)}, u32[]{:S(2)}) collective-permute-start(f32[256,1536]{1,0:T(8,128)} %get-tuple-element.628), channel_id=1, source_target_pairs={{0,1},{1,0},{2,3},{3,2},{4,5},{5,4},{6,7},{7,6},{8,9},{9,8},{10,11... | collective-permute-start | bytes 4718600 | tf_op jit(solution)/shard_map/ppermute | solution.py:110
  420.8 43.9 %collective-permute-start.40 = (f32[256,1536]{1,0:T(8,128)}, f32[256,1536]{1,0:T(8,128)}, u32[]{:S(2)}, u32[]{:S(2)}) collective-permute-start(f32[256,1536]{1,0:T(8,128)} %get-tuple-element.627), channel_id=1, source_target_pairs={{1,2},{2,1},{5,6},{6,5},{9,10},{10,9},{13,14},{14,13},{17,18},{18,... | collective-permute-start | bytes 4718600 | tf_op jit(solution)/shard_map/ppermute | solution.py:110
  430.4 26.8 %collective-permute-start.34 = (f32[192,1152]{1,0:T(8,128)S(1)}, f32[192,1152]{1,0:T(8,128)S(1)}, u32[]{:S(2)}, u32[]{:S(2)}) collective-permute-start(f32[192,1152]{1,0:T(8,128)S(1)} %get-tuple-element.573), channel_id=1, source_target_pairs={{0,8},{8,0},{16,24},{24,16},{1,9},{9,1},{17,25},{25,17},{2,10},{10... | collective-permute-start | bytes 2654216 | tf_op jit(solution)/shard_map/ppermute | solution.py:987
  431.9 25.4 %collective-permute-start.35 = (f32[192,1152]{1,0:T(8,128)S(1)}, f32[192,1152]{1,0:T(8,128)S(1)}, u32[]{:S(2)}, u32[]{:S(2)}) collective-permute-start(f32[192,1152]{1,0:T(8,128)S(1)} %get-tuple-element.575), channel_id=1, source_target_pairs={{0,16},{8,24},{16,0},{24,8},{1,17},{9,25},{17,1},{25,9},{2,18},{10... | collective-permute-start | bytes 2654216 | tf_op jit(solution)/shard_map/ppermute | solution.py:987
  (84 other events, 957.1 us)
Sparse Core Ops, SparseCore 0:
  103.9 78.2 all-gather.2
  279.5 125.6 reduce-scatter.1

commit v3 on v2

--- a/solution.py
+++ b/solution.py
@@ -713,7 +713,7 @@
         in_specs=in_specs,
         out_specs=out_specs,
         scratch_shapes=scratch,
-        compiler_params=params(VMEM_BYTES if start else LATE_VMEM_BYTES),
+        compiler_params=params(),
         cost_estimate=cost(
             levels * rows * (20 * kv_here * keys * LANES + 2 * depth * (out_wide + wide)),
             2 * depth * levels * (out_wide + wide) + 16 * rows * depth,

time: 492 us -> 493 us (level)
  Pallas kernels: 283 us -> 288 us
    unnamed x143 -> x129, local copies, waits for them, and re-layouts: 11.8 us -> 9.78 us
  transfers between devices with their start and end apart: 46 -> 46, of which waited for: 9 -> 8; matrix products, arithmetic and copies ran while one was open for 12% -> 11% of each run, Pallas kernels for 58% -> 59%
where the time goes in v3:
time: 493 us; the launch traced here: 487 us
  Pallas kernels  288 us (58%)
  starting transfers between devices  74.2 us (15%)
  other arithmetic  51.7 us (10%)
  waiting for transfers between devices  35.5 us (7%)
  local copies, waits for them, and re-layouts  21.8 us (4%)
  between operations  16.2 us (3%)
    pallas_call x5, Pallas kernels, backward_chunk(): pl.pallas_call(functools.partial(backward_kernel, start, full, acc is not...  125 us
    ppermute x30, starting transfers between devices, along(): return lax.ppermute(part, 'tp', pairs)  58.3 us
    pallas_call x4, Pallas kernels, forward_chunk(): pl.pallas_call(forward_kernel, out_shape=outs, grid=(steps,), in_specs=[S...  56 us
    ppermute x30, waiting for transfers between devices, along(): return lax.ppermute(part, 'tp', pairs)  34.4 us
    pallas_call x3, Pallas kernels, rows_of(): pl.pallas_call(functools.partial(rows_kernel, counts, plan, recv is not N...  28.2 us
    pallas_call x4, Pallas kernels, attend(): pl.pallas_call(functools.partial(attend_kernel, index * rows), out_shape=...  21.1 us
    pallas_call x1, Pallas kernels, project(): pl.pallas_call(project_kernel, out_shape=jax.ShapeDtypeStruct((rows, widt...  15.9 us
    ppermute x11, starting transfers between devices, to_chip(): return lax.ppermute(array, 'chip', [(i, i ^ m) for i in range(chips)])  15.3 us
  transfers between devices with their start and end apart: 46, of which 8 were waited for; matrix products, arithmetic and copies ran while one was open for 11% of the time, Pallas kernels for 59%

profile of v3, /device:TPU:0, one launch (start us, length us, event | category | flops | bytes accessed | tf_op | source)
XLA Modules:
  0.0 487.3 jit_solution(11785120943808559881)
XLA Ops:
  14.2 3.1 fusion.5
  17.3 4.5 collective-permute-done
  25.1 10.5 %shard_map.221 = (bf16[1024,4096]{1,0:T(8,128)(2,1)}, bf16[1024,1536]{1,0:T(8,128)(2,1)}, bf16[1536,4096]{1,0:T(8,128)(2,1)}) custom-call(bf16[1024,1536]{1,0:T(8,128)(2,1)} %refs_12_.7, f32[1,1536]{1,0:T(1,128)} %broadcast_in_dim.10.gain_ref.refs_13_, bf16[1536,384]{1,0:T(8,128)(2,1)} %q_ref.1, bf16[192,1536]{1,0:T(8,128)(2,1)} %bitcast.32, ...), custom_call_target="tpu_custom_call" | custom-call | flops 3145728 | bytes 18432 | tf_op jit(solution)/shard_map/pallas_call | solution.py:230
  40.3 5.6 %shard_map.222.part_ref.refs_7_.refs_22_ = f32[264,384]{1,0:T(8,128)} custom-call(s32[1]{0:T(128)S(6)} %copy.46.length_ref, bf16[1024,4096]{1,0:T(8,128)(2,1)} %get-tuple-element.327.q_ref.kv_ref._, bf16[1024,4096]{1,0:T(8,128)(2,1)} %get-tuple-element.327.q_ref.kv_ref._, bf16[512,384]{1,0:T(8,128)(2,1)} %fusion.2.strip_ref), custom_call_target="tpu_custom_call" | custom-call | flops 393216 | bytes 2048 | tf_op jit(solution)/shard_map/pallas_call | solution.py:337
  45.9 6.6 %shard_map.223.part_ref.refs_7_.refs_23_ = f32[264,384]{1,0:T(8,128)} custom-call(s32[1]{0:T(128)S(6)} %copy.46.length_ref, bf16[1024,4096]{1,0:T(8,128)(2,1)} %get-tuple-element.327.q_ref.kv_ref._, bf16[1024,4096]{1,0:T(8,128)(2,1)} %get-tuple-element.327.q_ref.kv_ref._, bf16[512,384]{1,0:T(8,128)(2,1)} %fusion.2.strip_ref), custom_call_target="tpu_custom_call" | custom-call | flops 524288 | bytes 2560 | tf_op jit(solution)/shard_map/pallas_call | solution.py:337
  53.8 6.0 %collective-permute-start.5 = (f32[528,384]{1,0:T(8,128)S(1)}, f32[528,384]{1,0:T(8,128)S(1)}, u32[]{:S(2)}, u32[]{:S(2)}) collective-permute-start(f32[528,384]{1,0:T(8,128)S(1)} %pad_maximum_fusion.5), channel_id=1, source_target_pairs={{0,1},{1,0},{2,3},{3,2},{4,5},{5,4},{6,7},{7,6},{8,9},{9,8},{10,11... | collective-permute-start | bytes 2433032 | tf_op jit(solution)/shard_map/ppermute | solution.py:110
  63.2 4.0 shard_map.224.part_ref.refs_7_.refs_20_
  67.1 4.9 %shard_map.225.part_ref.refs_7_.refs_21_ = f32[264,384]{1,0:T(8,128)} custom-call(s32[1]{0:T(128)S(6)} %copy.46.length_ref, bf16[1024,4096]{1,0:T(8,128)(2,1)} %get-tuple-element.327.q_ref.kv_ref._, bf16[1024,4096]{1,0:T(8,128)(2,1)} %get-tuple-element.327.q_ref.kv_ref._, bf16[512,384]{1,0:T(8,128)(2,1)} %fusion.2.strip_ref), custom_call_target="tpu_custom_call" | custom-call | flops 262144 | bytes 1536 | tf_op jit(solution)/shard_map/pallas_call | solution.py:337
  73.7 3.5 collective-permute-done.5
  84.4 7.0 %shard_map.226 = (bf16[1024,1536]{1,0:T(8,128)(2,1)}, bf16[1536,1024]{1,0:T(8,128)(2,1)}, bf16[1536,1024]{1,0:T(8,128)(2,1)}) custom-call(s32[1]{0:T(128)S(6)} %copy.46.length_ref, bf16[1024,1536]{1,0:T(8,128)(2,1)} %cot_ref.1, bf16[1024,1536]{1,0:T(8,128)(2,1)} %get-tuple-element.339.normed_ref.x_ref), custom_call_target="tpu_custom_call" | custom-call | flops 1536 | bytes 15360 | tf_op jit(solution)/shard_map/pallas_call | solution.py:263
  94.8 5.9 %collective-permute-done.11 = f32[2,192,768]{2,1,0:T(8,128)} collective-permute-done((f32[2,192,768]{2,1,0:T(8,128)}, f32[2,192,768]{2,1,0:T(8,128)}, u32[]{:S(2)}, u32[]{:S(2)}) %collective-permute-start.11) | collective-permute-done | bytes 1179680 | tf_op jit(solution)/shard_map/ppermute | solution.py:110
  113.5 10.2 %shard_map.227 = (bf16[1536,2048]{1,0:T(8,128)(2,1)}, bf16[1536,1536]{1,0:T(8,128)(2,1)}) custom-call(s32[2]{0:T(128)} %pad_add_fusion.4.meta_ref, bf16[1536,384]{1,0:T(8,128)(2,1)} %bitcast.25, bf16[384,512]{1,0:T(8,128)(2,1)} %fusion.3.p_ref.refs_8_, f32[4,3,192,384]{3,2,1,0:T(8,128)} %copy-done.30, f32[4,3,192,384]{3,2,1,0:T(8,128)} %collective-permute-done.15.theirs_ref), custom_call_target="tpu_custom_call" | custom-call | flops 2359296 | bytes 17664 | tf_op jit(solution)/shard_map/pallas_call | solution.py:180
  123.8 15.3 %collective-permute-done.12.other_ref.refs_14_ = f32[264,384]{1,0:T(8,128)S(1)} collective-permute-done((f32[264,384]{1,0:T(8,128)S(1)}, f32[264,384]{1,0:T(8,128)S(1)}, u32[]{:S(2)}, u32[]{:S(2)}) %collective-permute-start.12) | collective-permute-done | bytes 405536 | tf_op jit(solution)/shard_map/ppermute | solution.py:110
  143.5 13.9 %shard_map.228 = (f32[256,1536]{1,0:T(8,128)}, bf16[1536,256]{1,0:T(8,128)(2,1)}, bf16[256,1024]{1,0:T(8,128)(2,1)}, bf16[256,1024]{1,0:T(8,128)(2,1)}, bf16[256...) custom-call(s32[1]{0:T(128)} %bitcast.2.level_ref, f32[264,384]{1,0:T(8,128)} %shard_map.223.part_ref.refs_7_.refs_23_, ...), custom_call_target="tpu_custom_call" | custom-call | flops 5898240 | bytes 22272 | tf_op jit(solution)/shard_map/pallas_call | solution.py:428
  157.5 5.8 %collective-permute-start.21 = (f32[264,1536]{1,0:T(8,128)}, f32[264,1536]{1,0:T(8,128)}, u32[]{:S(2)}, u32[]{:S(2)}) collective-permute-start(f32[264,1536]{1,0:T(8,128)} %get-tuple-element.418), channel_id=1, source_target_pairs={{0,1},{3,2},{4,5},{7,6},{8,9},{11,10},{12,13},{15,14},{16,17},{19,... | collective-permute-start | bytes 4866056 | tf_op jit(solution)/shard_map/ppermute | solution.py:110
  163.3 4.1 collective-permute-done.18.outer_ref.refs_16_
  170.5 14.1 %shard_map.229 = (f32[256,1536]{1,0:T(8,128)}, bf16[1536,256]{1,0:T(8,128)(2,1)}, bf16[256,1024]{1,0:T(8,128)(2,1)}, bf16[256,1024]{1,0:T(8,128)(2,1)}, bf16[256...) custom-call(s32[1]{0:T(128)} %bitcast.2.level_ref, f32[264,384]{1,0:T(8,128)} %shard_map.222.part_ref.refs_7_.refs_22_, ...), custom_call_target="tpu_custom_call" | custom-call | flops 5898240 | bytes 22272 | tf_op jit(solution)/shard_map/pallas_call | solution.py:428
  184.6 12.7 %shard_map.230.w_ref.refs_17_ = bf16[1536,4096]{1,0:T(8,128)(2,1)} custom-call(bf16[384,512]{1,0:T(8,128)(2,1)} %fusion.pq_ref, bf16[384,512]{1,0:T(8,128)(2,1)} %fusion.1.pkv_ref, f32[8,3,192,768]{3,2,1,0:T(8,128)} %bitcast.24, bf16[1536,4096]{1,0:T(8,128)(2,1)} %get-tuple-element.400._), custom_call_target="tpu_custom_call", output_to_operand_aliasing={{}: (3, {})} | custom-call | flops 4718592 | bytes 30720 | tf_op jit(solution)/shard_map/pallas_call | solution.py:158
  197.4 5.6 %collective-permute-start.23 = (f32[264,1536]{1,0:T(8,128)}, f32[264,1536]{1,0:T(8,128)}, u32[]{:S(2)}, u32[]{:S(2)}) collective-permute-start(f32[264,1536]{1,0:T(8,128)} %get-tuple-element.444), channel_id=1, source_target_pairs={{0,1},{3,2},{4,5},{7,6},{8,9},{11,10},{12,13},{15,14},{16,17},{19,... | collective-permute-start | bytes 4866056 | tf_op jit(solution)/shard_map/ppermute | solution.py:110
  206.8 14.0 %shard_map.231 = (f32[256,1536]{1,0:T(8,128)}, bf16[1536,256]{1,0:T(8,128)(2,1)}, bf16[256,1024]{1,0:T(8,128)(2,1)}, bf16[256,1024]{1,0:T(8,128)(2,1)}, bf16[256...) custom-call(s32[1]{0:T(128)} %bitcast.2.level_ref, f32[264,384]{1,0:T(8,128)} %shard_map.225.part_ref.refs_7_.refs_21_, ...), custom_call_target="tpu_custom_call" | custom-call | flops 5898240 | bytes 22272 | tf_op jit(solution)/shard_map/pallas_call | solution.py:428
  220.9 15.9 %shard_map.232.refs_2_.refs_3_.refs_4_.refs_5_.refs_6_ = bf16[1024,4096]{1,0:T(8,128)(2,1)} custom-call(bf16[1024,1536]{1,0:T(8,128)(2,1)} %get-tuple-element.339.normed_ref.x_ref, bf16[1536,4096]{1,0:T(8,128)(2,1)} %shard_map.230.w_ref.refs_17_, f32[1024,128]{1,0:T(8,128)} %get-tuple-element.320.cos_ref.refs_10_, ...), custom_call_target="tpu_custom_call", output_to_operand_aliasing={{}: (4, {})} | custom-call | flops 12582912 | bytes 23552 | tf_op jit(solution)/shard_map/pallas_call | solution.py:283
  246.6 13.9 %shard_map.233 = (f32[256,1536]{1,0:T(8,128)}, bf16[1536,256]{1,0:T(8,128)(2,1)}, bf16[256,1024]{1,0:T(8,128)(2,1)}, bf16[256,1024]{1,0:T(8,128)(2,1)}, bf16[256...) custom-call(s32[1]{0:T(128)} %bitcast.2.level_ref, f32[264,384]{1,0:T(8,128)} %shard_map.224.part_ref.refs_7_.refs_20_, ...), custom_call_target="tpu_custom_call" | custom-call | flops 5898240 | bytes 22272 | tf_op jit(solution)/shard_map/pallas_call | solution.py:428
  260.6 19.4 %shard_map.234 = f32[1536,3072]{1,0:T(8,128)} custom-call(s32[3]{0:T(128)} %constant.159.clone.side_ref, bf16[1536,256]{1,0:T(8,128)(2,1)} %get-tuple-element.452.refs_0_.refs_1_.refs_2_.refs_3_, bf16[1536,256]{1,0:T(8,128)(2,1)} %get-tuple-element.452.refs_0_.refs_1_.refs_2_.refs_3_, bf16[1536,256]{1,0:T(8,128)(2,1)} %get-tuple-element.452.refs_0_.refs_1_.refs_2_.refs_3_, ...), custom_call_target="tpu_custom_call" | custom-call | flops 9437184 | bytes 27648 | tf_op jit(solution)/shard_map/pallas_call | solution.py:821
  289.3 37.3 %shard_map.235 = (bf16[1536,256]{1,0:T(8,128)(2,1)}, bf16[256,768]{1,0:T(8,128)(2,1)}, bf16[1024,1536]{1,0:T(8,128)(2,1)}, f32[8,1536]{1,0:T(8,128)}, f32[768,2048]{1,0:T(8,128)}) custom-call(s32[1]{0:T(128)} %bitcast.2.level_ref, f32[256,1536]{1,0:T(8,128)} %copy-done.39, f32[256,1536]{1,0:T(8,128)} %collective-permute-done.25.final_ref, ...), custom_call_target="tpu_custom_call" | custom-call | flops 9961472 | bytes 24576 | tf_op jit(solution)/shard_map/pallas_call | solution.py:708
  326.6 3.5 select_select_fusion.1.total_ref
  335.1 31.7 %shard_map.236 = (bf16[1536,256]{1,0:T(8,128)(2,1)}, bf16[256,768]{1,0:T(8,128)(2,1)}, bf16[1024,1536]{1,0:T(8,128)(2,1)}, f32[8,1536]{1,0:T(8,128)}, f32[512,2048]{1,0:T(8,128)}) custom-call(s32[1]{0:T(128)} %bitcast.2.level_ref, f32[256,1536]{1,0:T(8,128)} %copy-done.40, ...), custom_call_target="tpu_custom_call", output_to_operand_aliasing={{2}: (24, {})} | custom-call | flops 8650752 | bytes 24576 | tf_op jit(solution)/shard_map/pallas_call | solution.py:708
  375.8 26.4 %shard_map.237 = (bf16[1536,256]{1,0:T(8,128)(2,1)}, bf16[256,768]{1,0:T(8,128)(2,1)}, bf16[1024,1536]{1,0:T(8,128)(2,1)}, f32[8,1536]{1,0:T(8,128)}, f32[256,2048]{1,0:T(8,128)}) custom-call(s32[1]{0:T(128)} %bitcast.2.level_ref, f32[256,1536]{1,0:T(8,128)} %select_select_fusion.1.total_ref, ...), custom_call_target="tpu_custom_call", output_to_operand_aliasing={{2}: (24, {})} | custom-call | flops 7340032 | bytes 24576 | tf_op jit(solution)/shard_map/pallas_call | solution.py:708
  404.3 8.3 %shard_map.238 = (bf16[1536,256]{1,0:T(8,128)(2,1)}, bf16[256,768]{1,0:T(8,128)(2,1)}) custom-call(s32[1]{0:T(128)} %bitcast.2.level_ref, f32[264,1536]{1,0:T(8,128)} %copy-done.27, f32[264,1536]{1,0:T(8,128)} %copy-done.28, f32[256,1536]{1,0:T(8,128)} %get-tuple-element.578.hidden_ref, bf16[1024,1536]{1,0:T(8,128)(2,1)} %get-tuple-element.368.refs_1_.dout_ref, ...), custom_call_target="tpu_custom_call" | custom-call | flops 6029312 | bytes 24576 | tf_op jit(solution)/shard_map/pallas_call | solution.py:708
  418.2 4.1 slice_add_fusion
  427.3 6.0 %shard_map.240 = (f32[192,1152]{1,0:T(8,128)}, f32[192,1152]{1,0:T(8,128)S(1)}, f32[192,1152]{1,0:T(8,128)}, f32[192,1152]{1,0:T(8,128)S(1)}) custom-call(s32[3]{0:T(128)S(1)} %get-tuple-element.650.side_ref, bf16[1536,256]{1,0:T(8,128)(2,1)S(1)} %copy-done.4, bf16[1536,256]{1,0:T(8,128)(2,1)S(1)} %copy-done.4, bf16[1536,256]{1,0:T(8,128)(2,1)S(1)} %copy-done.4, ...), custom_call_target="tpu_custom_call" | custom-call | flops 1769472 | bytes 7296 | tf_op jit(solution)/shard_map/pallas_call | solution.py:821
  437.8 21.7 %shard_map.241 = (bf16[1536,256]{1,0:T(8,128)(2,1)}, bf16[256,768]{1,0:T(8,128)(2,1)}, bf16[1024,1536]{1,0:T(8,128)(2,1)}, f32[8,1536]{1,0:T(8,128)}) custom-call(s32[1]{0:T(128)} %bitcast.2.level_ref, f32[264,1536]{1,0:T(8,128)} %copy-done.27, f32[264,1536]{1,0:T(8,128)} %copy-done.28, ...), custom_call_target="tpu_custom_call", output_to_operand_aliasing={{2}: (24, {})} | custom-call | flops 6029312 | bytes 24576 | tf_op jit(solution)/shard_map/pallas_call | solution.py:708
  469.2 5.4 %add_convert_fusion = bf16[256,1536]{1,0:T(8,128)(2,1)} fusion(f32[256,1536]{1,0:T(8,128)} %collective-permute-done.39, f32[256,1536]{1,0:T(8,128)} %collective-permute-done.40, f32[256,1536]{1,0:T(8,128)} %get-tuple-element.595.hidden_ref, f32[256,1536]{1,0:T(8,128)} %get-tuple-element.596.hidden_ref, f32[256,1536]{1,0:T(8,128)} %get-tuple-element.578.hidden_ref, ...), kind=kLoop, calls=%fused_computation.2 | loop fusion | flops 3932160 | bytes 16515076 | tf_op jit(solution)/shard_map/convert_element_type | solution.py:1215
  (279 shorter events, 120.2 us)
Async XLA Ops:
  7.2 177.4 %all-gather.3.cloned.1.call-start = ((), (), s32[]{:S(2)}) async-start(), calls=%async_computation.2 | async-start | bytes 15925248 | tf_op jit(solution)/shard_map/all_gather | solution.py:1030
  14.0 21.5 %collective-permute-start.2 = (f32[192,768]{1,0:T(8,128)S(1)}, f32[192,768]{1,0:T(8,128)S(1)}, u32[]{:S(2)}, u32[]{:S(2)}) collective-permute-start(f32[192,768]{1,0:T(8,128)S(1)} %maximum_convert_fusion), channel_id=1, source_target_pairs={{0,1},{1,0},{2,3},{3,2},{4,5},{5,4},{6,7},{7,6},{8,9},{9,8},{10,11... | collective-permute-start | bytes 1769480 | tf_op jit(solution)/shard_map/ppermute | solution.py:110
  35.6 17.2 %collective-permute-start.3 = (f32[2,192,384]{2,1,0:T(8,128)S(1)}, f32[2,192,384]{2,1,0:T(8,128)S(1)}, u32[]{:S(2)}, u32[]{:S(2)}) collective-permute-start(f32[2,192,384]{2,1,0:T(8,128)S(1)} %collective-permute-done.1), channel_id=1, source_target_pairs={{1,0},{2,3},{5,4},{6,7},{9,8},{10,11},{13,12},{14,15},{17,16},{18,... | collective-permute-start | bytes 1769480 | tf_op jit(solution)/shard_map/ppermute | solution.py:110
  38.5 33.8 %collective-permute-start.4 = (f32[2,192,768]{2,1,0:T(8,128)S(1)}, f32[2,192,768]{2,1,0:T(8,128)}, u32[]{:S(2)}, u32[]{:S(2)}) collective-permute-start(f32[2,192,768]{2,1,0:T(8,128)S(1)} %pad_maximum_fusion.1), channel_id=1, source_target_pairs={{1,2},{2,1},{5,6},{6,5},{9,10},{10,9},{13,14},{14,13},{17,18},{18,... | collective-permute-start | bytes 3538952 | tf_op jit(solution)/shard_map/ppermute | solution.py:110
  53.8 23.4 %collective-permute-start.5 = (f32[528,384]{1,0:T(8,128)S(1)}, f32[528,384]{1,0:T(8,128)S(1)}, u32[]{:S(2)}, u32[]{:S(2)}) collective-permute-start(f32[528,384]{1,0:T(8,128)S(1)} %pad_maximum_fusion.5), channel_id=1, source_target_pairs={{0,1},{1,0},{2,3},{3,2},{4,5},{5,4},{6,7},{7,6},{8,9},{9,8},{10,11... | collective-permute-start | bytes 2433032 | tf_op jit(solution)/shard_map/ppermute | solution.py:110
  72.2 28.4 %collective-permute-start.11 = (f32[2,192,768]{2,1,0:T(8,128)}, f32[2,192,768]{2,1,0:T(8,128)}, u32[]{:S(2)}, u32[]{:S(2)}) collective-permute-start(f32[2,192,768]{2,1,0:T(8,128)} %collective-permute-done.4), channel_id=1, source_target_pairs={{1,0},{2,3},{5,4},{6,7},{9,8},{10,11},{13,12},{14,15},{17,16},{18,... | collective-permute-start | bytes 3538952 | tf_op jit(solution)/shard_map/ppermute | solution.py:110
  77.2 16.6 %collective-permute-start.10 = (f32[2,3,96,384]{3,2,1,0:T(8,128)S(1)}, f32[2,3,96,384]{3,2,1,0:T(8,128)}, u32[]{:S(2)}, u32[]{:S(2)}) collective-permute-start(f32[2,3,96,384]{3,2,1,0:T(8,128)S(1)} %pad_maximum_fusion.4), channel_id=1, source_target_pairs={{0,8},{8,0},{16,24},{24,16},{1,9},{9,1},{17,25},{25,17},{2,10},{10... | collective-permute-start | bytes 2654216 | tf_op jit(solution)/shard_map/ppermute | solution.py:987
  103.8 370.8 %reduce-scatter.2.cloned.1.call-start = ((), (), s32[]{:S(2)}) async-start(), calls=%async_computation.1 | async-start | bytes 21233664 | tf_op jit(solution)/shard_map/reduce_scatter | solution.py:1109
  107.1 32.0 %collective-permute-start.13 = (f32[264,768]{1,0:T(8,128)S(1)}, f32[264,768]{1,0:T(8,128)S(1)}, u32[]{:S(2)}, u32[]{:S(2)}) collective-permute-start(f32[264,768]{1,0:T(8,128)S(1)} %pad_maximum_fusion.7), channel_id=1, source_target_pairs={{1,2},{2,1},{5,6},{6,5},{9,10},{10,9},{13,14},{14,13},{17,18},{18,... | collective-permute-start | bytes 2433032 | tf_op jit(solution)/shard_map/ppermute | solution.py:110
  108.0 31.1 %collective-permute-start.14 = (f32[264,768]{1,0:T(8,128)}, f32[264,768]{1,0:T(8,128)S(1)}, u32[]{:S(2)}, u32[]{:S(2)}) collective-permute-start(f32[264,768]{1,0:T(8,128)} %collective-permute-done.8.across_ref.refs_15_), channel_id=1, source_target_pairs={{1,0},{2,3},{5,4},{6,7},{9,8},{10,11},{13,12},{14,15},{17,16},{18,... | collective-permute-start | bytes 2433032 | tf_op jit(solution)/shard_map/ppermute | solution.py:110
  109.3 29.8 %collective-permute-start.12 = (f32[264,384]{1,0:T(8,128)S(1)}, f32[264,384]{1,0:T(8,128)S(1)}, u32[]{:S(2)}, u32[]{:S(2)}) collective-permute-start(f32[264,384]{1,0:T(8,128)S(1)} %copy-done.11), channel_id=1, source_target_pairs={{0,1},{1,0},{2,3},{3,2},{4,5},{5,4},{6,7},{7,6},{8,9},{9,8},{10,11... | collective-permute-start | bytes 1216520 | tf_op jit(solution)/shard_map/ppermute | solution.py:110
  139.1 18.3 %collective-permute-start.16 = (f32[264,384]{1,0:T(8,128)S(1)}, f32[264,384]{1,0:T(8,128)S(1)}, u32[]{:S(2)}, u32[]{:S(2)}) collective-permute-start(f32[264,384]{1,0:T(8,128)S(1)} %copy-done.5), channel_id=1, source_target_pairs={{0,1},{1,0},{2,3},{3,2},{4,5},{5,4},{6,7},{7,6},{8,9},{9,8},{10,11... | collective-permute-start | bytes 1216520 | tf_op jit(solution)/shard_map/ppermute | solution.py:110
  140.1 23.3 %collective-permute-start.17 = (f32[264,768]{1,0:T(8,128)S(1)}, f32[264,768]{1,0:T(8,128)}, u32[]{:S(2)}, u32[]{:S(2)}) collective-permute-start(f32[264,768]{1,0:T(8,128)S(1)} %pad_maximum_fusion.8), channel_id=1, source_target_pairs={{1,2},{2,1},{5,6},{6,5},{9,10},{10,9},{13,14},{14,13},{17,18},{18,... | collective-permute-start | bytes 2433032 | tf_op jit(solution)/shard_map/ppermute | solution.py:110
  141.6 25.8 %collective-permute-start.18 = (f32[264,768]{1,0:T(8,128)S(1)}, f32[264,768]{1,0:T(8,128)S(1)}, u32[]{:S(2)}, u32[]{:S(2)}) collective-permute-start(f32[264,768]{1,0:T(8,128)S(1)} %collective-permute-done.13.across_ref.refs_15_), channel_id=1, source_target_pairs={{1,0},{2,3},{5,4},{6,7},{9,8},{10,11},{13,12},{14,15},{17,16},{18,... | collective-permute-start | bytes 2433032 | tf_op jit(solution)/shard_map/ppermute | solution.py:110
  157.5 39.9 %collective-permute-start.21 = (f32[264,1536]{1,0:T(8,128)}, f32[264,1536]{1,0:T(8,128)}, u32[]{:S(2)}, u32[]{:S(2)}) collective-permute-start(f32[264,1536]{1,0:T(8,128)} %get-tuple-element.418), channel_id=1, source_target_pairs={{0,1},{3,2},{4,5},{7,6},{8,9},{11,10},{12,13},{15,14},{16,17},{19,... | collective-permute-start | bytes 4866056 | tf_op jit(solution)/shard_map/ppermute | solution.py:110
  168.4 28.9 %collective-permute-start.19 = (f32[264,768]{1,0:T(8,128)}, f32[264,768]{1,0:T(8,128)S(1)}, u32[]{:S(2)}, u32[]{:S(2)}) collective-permute-start(f32[264,768]{1,0:T(8,128)} %pad_maximum_fusion.9), channel_id=1, source_target_pairs={{1,2},{2,1},{5,6},{6,5},{9,10},{10,9},{13,14},{14,13},{17,18},{18,... | collective-permute-start | bytes 2433032 | tf_op jit(solution)/shard_map/ppermute | solution.py:110
  169.1 28.2 %collective-permute-start.20 = (f32[264,768]{1,0:T(8,128)}, f32[264,768]{1,0:T(8,128)S(1)}, u32[]{:S(2)}, u32[]{:S(2)}) collective-permute-start(f32[264,768]{1,0:T(8,128)} %collective-permute-done.17.across_ref.refs_15_), channel_id=1, source_target_pairs={{1,0},{2,3},{5,4},{6,7},{9,8},{10,11},{13,12},{14,15},{17,16},{18,... | collective-permute-start | bytes 2433032 | tf_op jit(solution)/shard_map/ppermute | solution.py:110
  197.4 39.4 %collective-permute-start.23 = (f32[264,1536]{1,0:T(8,128)}, f32[264,1536]{1,0:T(8,128)}, u32[]{:S(2)}, u32[]{:S(2)}) collective-permute-start(f32[264,1536]{1,0:T(8,128)} %get-tuple-element.444), channel_id=1, source_target_pairs={{0,1},{3,2},{4,5},{7,6},{8,9},{11,10},{12,13},{15,14},{16,17},{19,... | collective-permute-start | bytes 4866056 | tf_op jit(solution)/shard_map/ppermute | solution.py:110
  204.6 32.2 %collective-permute-start.24 = (f32[256,1536]{1,0:T(8,128)S(1)}, f32[256,1536]{1,0:T(8,128)S(1)}, u32[]{:S(2)}, u32[]{:S(2)}) collective-permute-start(f32[256,1536]{1,0:T(8,128)S(1)} %slice_add_fusion.3), channel_id=1, source_target_pairs={{1,2},{2,1},{5,6},{6,5},{9,10},{10,9},{13,14},{14,13},{17,18},{18,... | collective-permute-start | bytes 4718600 | tf_op jit(solution)/shard_map/ppermute | solution.py:110
  205.4 31.4 %collective-permute-start.22 = (f32[264,768]{1,0:T(8,128)S(1)}, f32[264,768]{1,0:T(8,128)S(1)}, u32[]{:S(2)}, u32[]{:S(2)}) collective-permute-start(f32[264,768]{1,0:T(8,128)S(1)} %collective-permute-done.19.across_ref.refs_15_), channel_id=1, source_target_pairs={{1,0},{2,3},{5,4},{6,7},{9,8},{10,11},{13,12},{14,15},{17,16},{18,... | collective-permute-start | bytes 2433032 | tf_op jit(solution)/shard_map/ppermute | solution.py:110
  239.8 40.2 %collective-permute-start.25 = (f32[256,1536]{1,0:T(8,128)S(1)}, f32[256,1536]{1,0:T(8,128)}, u32[]{:S(2)}, u32[]{:S(2)}) collective-permute-start(f32[256,1536]{1,0:T(8,128)S(1)} %slice_select_fusion.total_ref), channel_id=1, source_target_pairs={{0,1},{1,0},{2,3},{3,2},{4,5},{5,4},{6,7},{7,6},{8,9},{9,8},{10,11... | collective-permute-start | bytes 4718600 | tf_op jit(solution)/shard_map/ppermute | solution.py:110
  244.8 35.2 %collective-permute-start.26 = (f32[256,1536]{1,0:T(8,128)S(1)}, f32[256,1536]{1,0:T(8,128)}, u32[]{:S(2)}, u32[]{:S(2)}) collective-permute-start(f32[256,1536]{1,0:T(8,128)S(1)} %slice_add_fusion.2), channel_id=1, source_target_pairs={{1,2},{2,1},{5,6},{6,5},{9,10},{10,9},{13,14},{14,13},{17,18},{18,... | collective-permute-start | bytes 4718600 | tf_op jit(solution)/shard_map/ppermute | solution.py:110
  282.4 44.1 %collective-permute-start.27 = (f32[256,1536]{1,0:T(8,128)S(1)}, f32[256,1536]{1,0:T(8,128)}, u32[]{:S(2)}, u32[]{:S(2)}) collective-permute-start(f32[256,1536]{1,0:T(8,128)S(1)} %add_select_fusion.1.total_ref), channel_id=1, source_target_pairs={{0,1},{1,0},{2,3},{3,2},{4,5},{5,4},{6,7},{7,6},{8,9},{9,8},{10,11... | collective-permute-start | bytes 4718600 | tf_op jit(solution)/shard_map/ppermute | solution.py:110
  286.3 40.3 %collective-permute-start.28 = (f32[256,1536]{1,0:T(8,128)S(1)}, f32[256,1536]{1,0:T(8,128)}, u32[]{:S(2)}, u32[]{:S(2)}) collective-permute-start(f32[256,1536]{1,0:T(8,128)S(1)} %slice_add_fusion.1), channel_id=1, source_target_pairs={{1,2},{2,1},{5,6},{6,5},{9,10},{10,9},{13,14},{14,13},{17,18},{18,... | collective-permute-start | bytes 4718600 | tf_op jit(solution)/shard_map/ppermute | solution.py:110
  330.2 36.6 %collective-permute-start.30 = (f32[256,1536]{1,0:T(8,128)}, f32[256,1536]{1,0:T(8,128)}, u32[]{:S(2)}, u32[]{:S(2)}) collective-permute-start(f32[256,1536]{1,0:T(8,128)} %select_select_fusion.1.total_ref), channel_id=1, source_target_pairs={{0,1},{1,0},{2,3},{3,2},{4,5},{5,4},{6,7},{7,6},{8,9},{9,8},{10,11... | collective-permute-start | bytes 4718600 | tf_op jit(solution)/shard_map/ppermute | solution.py:110
  332.8 33.9 %collective-permute-start.29 = (f32[256,1536]{1,0:T(8,128)S(1)}, f32[256,1536]{1,0:T(8,128)}, u32[]{:S(2)}, u32[]{:S(2)}) collective-permute-start(f32[256,1536]{1,0:T(8,128)S(1)} %slice_add_fusion.4), channel_id=1, source_target_pairs={{1,2},{2,1},{5,6},{6,5},{9,10},{10,9},{13,14},{14,13},{17,18},{18,... | collective-permute-start | bytes 4718600 | tf_op jit(solution)/shard_map/ppermute | solution.py:110
  369.0 34.1 %collective-permute-start.31 = (f32[264,1536]{1,0:T(8,128)S(1)}, f32[264,1536]{1,0:T(8,128)S(1)}, u32[]{:S(2)}, u32[]{:S(2)}) collective-permute-start(f32[264,1536]{1,0:T(8,128)S(1)} %pad.9.total_ref), channel_id=1, source_target_pairs={{0,1},{1,0},{2,3},{3,2},{4,5},{5,4},{6,7},{7,6},{8,9},{9,8},{10,11... | collective-permute-start | bytes 4866056 | tf_op jit(solution)/shard_map/ppermute | solution.py:110
  373.8 38.8 %collective-permute-start.32 = (f32[256,1536]{1,0:T(8,128)}, f32[256,1536]{1,0:T(8,128)}, u32[]{:S(2)}, u32[]{:S(2)}) collective-permute-start(f32[256,1536]{1,0:T(8,128)} %select_add_fusion), channel_id=1, source_target_pairs={{1,2},{2,1},{5,6},{6,5},{9,10},{10,9},{13,14},{14,13},{17,18},{18,... | collective-permute-start | bytes 4718600 | tf_op jit(solution)/shard_map/ppermute | solution.py:110
  422.3 43.4 %collective-permute-start.39 = (f32[256,1536]{1,0:T(8,128)}, f32[256,1536]{1,0:T(8,128)}, u32[]{:S(2)}, u32[]{:S(2)}) collective-permute-start(f32[256,1536]{1,0:T(8,128)} %get-tuple-element.628), channel_id=1, source_target_pairs={{0,1},{1,0},{2,3},{3,2},{4,5},{5,4},{6,7},{7,6},{8,9},{9,8},{10,11... | collective-permute-start | bytes 4718600 | tf_op jit(solution)/shard_map/ppermute | solution.py:110
  423.5 42.2 %collective-permute-start.40 = (f32[256,1536]{1,0:T(8,128)}, f32[256,1536]{1,0:T(8,128)}, u32[]{:S(2)}, u32[]{:S(2)}) collective-permute-start(f32[256,1536]{1,0:T(8,128)} %get-tuple-element.627), channel_id=1, source_target_pairs={{1,2},{2,1},{5,6},{6,5},{9,10},{10,9},{13,14},{14,13},{17,18},{18,... | collective-permute-start | bytes 4718600 | tf_op jit(solution)/shard_map/ppermute | solution.py:110
  435.2 24.3 %collective-permute-start.34 = (f32[192,1152]{1,0:T(8,128)}, f32[192,1152]{1,0:T(8,128)S(1)}, u32[]{:S(2)}, u32[]{:S(2)}) collective-permute-start(f32[192,1152]{1,0:T(8,128)} %get-tuple-element.573), channel_id=1, source_target_pairs={{0,8},{8,0},{16,24},{24,16},{1,9},{9,1},{17,25},{25,17},{2,10},{10... | collective-permute-start | bytes 2654216 | tf_op jit(solution)/shard_map/ppermute | solution.py:987
  436.7 22.8 %collective-permute-start.35 = (f32[192,1152]{1,0:T(8,128)}, f32[192,1152]{1,0:T(8,128)}, u32[]{:S(2)}, u32[]{:S(2)}) collective-permute-start(f32[192,1152]{1,0:T(8,128)} %get-tuple-element.575), channel_id=1, source_target_pairs={{0,16},{8,24},{16,0},{24,8},{1,17},{9,25},{17,1},{25,9},{2,18},{10... | collective-permute-start | bytes 2654216 | tf_op jit(solution)/shard_map/ppermute | solution.py:987
  (77 other events, 804.1 us)
Sparse Core Ops, SparseCore 0:
  103.9 78.2 all-gather.2
  280.1 125.5 reduce-scatter.1
